TPU v7x, 128 devices: a whole 4x4x4 slice. The times are simulated.
128 devices in a mesh: case: 2 (over core), space: 64 (over y, x, z).
Axes of the slice: x: 4, y: 4, z: 4, core: 2. Of those that a mesh axis runs over, the one named last changes fastest.
Arguments:
- design: float32 [512, 40, 128], P('space'), may hold values from 0.05 to 1
- passive: int32 [512, 40, 128], P('space'), may hold values from 0 to 2, as said below
- fixed_mask: int32 [512, 40, 128], P('space'), may hold values 0 or 1
- load_index: int32 [4, 4096], P('case'), may hold values from 0 to 2621439
Outputs:
- state: float32 [4, 512, 40, 128], P('case', 'space')
- sensitivity: float32 [512, 40, 128], P('space')
Inputs may be any that keep to these rules, and one draw needn't show every extreme that they name: `passive`: 0 marks a design voxel, 1 a voxel held solid, 2 a voxel held void.
All inputs are finite; a program needn't handle non-finite values. No bound on the sum of `fixed_mask` on one device may be relied on, other than what follows from the above.
Results may differ from a plain program's by a relative error of at most 0.0001.
Values sent between devices are 32-bit elements; how exact they have to be, the bound alone decides.
No kernel may reach another device: no remote copies, remote signals or barrier semaphores. Data moves between devices by JAX's collectives and lax.ppermute only.
A program may use at most 128 MiB of HBM per device.

v0:
```python
from functools import partial

import jax
import jax.numpy as jnp
from jax import lax
from jax.sharding import PartitionSpec as P

LEVELS = 3
COARSE_SWEEPS = 8
ITERS = 3


E_MIN = 0.01
OMEGA = 0.8
HEAT_SOURCE = 0.05
EDGE_WEIGHT = 1.5 - 2.0**0.5


def extended(x, sides, width):
    for axis, dim in sides:
        devices, length = (lax.axis_size(axis), x.shape[dim])
        up = [(i, (i + 1) % devices) for i in range(devices - 1)]
        down = [(j, i) for i, j in up]
        last = lax.slice_in_dim(x, length - width, length, axis=dim)
        initial = lax.slice_in_dim(x, 0, width, axis=dim)
        before = lax.ppermute(last, axis, up)
        after = lax.ppermute(initial, axis, down)
        x = jnp.concatenate([before, x, after], axis=dim)
    return x


def cone_filter(padded):
    framed = jnp.pad(padded, [(0, 0)] * (padded.ndim - 2) + [(1, 1), (1, 1)])
    depth_z = padded.shape[-3] - 2
    rows_y = padded.shape[-2]
    cols_x = padded.shape[-1]
    summed = 1.5 * framed[..., 1 : 1 + depth_z, 1 : 1 + rows_y, 1 : 1 + cols_x]
    for offset_z in (-1, 0, 1):
        for offset_y in (-1, 0, 1):
            for offset_x in (-1, 0, 1):
                distance = offset_z * offset_z + offset_y * offset_y + offset_x * offset_x
                if distance == 1:
                    weight = 0.5
                elif distance == 2:
                    weight = EDGE_WEIGHT
                else:
                    continue
                summed = (
                    summed
                    + weight
                    * framed[
                        ...,
                        1 + offset_z : 1 + offset_z + depth_z,
                        1 + offset_y : 1 + offset_y + rows_y,
                        1 + offset_x : 1 + offset_x + cols_x,
                    ]
                )
    return summed


def edges(values, dimension, before, behind):
    widths = [(0, 0)] * values.ndim
    widths[dimension] = (before, behind)
    return jnp.pad(values, widths)


def conductances(modulus):
    along_x = jnp.sqrt(modulus[..., :, :, 1:] * modulus[..., :, :, :-1])
    along_y = jnp.sqrt(modulus[..., :, 1:, :] * modulus[..., :, :-1, :])
    along_z = jnp.sqrt(modulus[..., 1:, :, :] * modulus[..., :-1, :, :])
    return (along_x, along_y, along_z)


def face_total(couplings):
    along_x, along_y, along_z = couplings
    result = edges(along_x, -1, 1, 0) + edges(along_x, -1, 0, 1)
    result = result + edges(along_y, -2, 1, 0) + edges(along_y, -2, 0, 1)
    return result + edges(along_z, -3, 1, 0) + edges(along_z, -3, 0, 1)


def laplace(values, couplings):
    along_x, along_y, along_z = couplings
    flux_x = along_x * (values[..., 1:] - values[..., :-1])
    flux_y = along_y * (values[..., 1:, :] - values[..., :-1, :])
    flux_z = along_z * (values[..., 1:, :, :] - values[..., :-1, :, :])
    result = edges(flux_x, -1, 1, 0) - edges(flux_x, -1, 0, 1)
    result = result + edges(flux_y, -2, 1, 0) - edges(flux_y, -2, 0, 1)
    return result + edges(flux_z, -3, 1, 0) - edges(flux_z, -3, 0, 1)


def cell_energy(values, couplings):
    along_x, along_y, along_z = couplings
    power_x = along_x * (values[..., 1:] - values[..., :-1]) ** 2
    power_y = along_y * (values[..., 1:, :] - values[..., :-1, :]) ** 2
    power_z = along_z * (values[..., 1:, :, :] - values[..., :-1, :, :]) ** 2
    result = edges(power_x, -1, 1, 0) + edges(power_x, -1, 0, 1)
    result = result + edges(power_y, -2, 1, 0) + edges(power_y, -2, 0, 1)
    return result + edges(power_z, -3, 1, 0) + edges(power_z, -3, 0, 1)


def build_level(modulus, freedom, factor):
    couplings = conductances(modulus)
    diagonal = freedom * factor * face_total(couplings) + (1.0 - freedom)
    return (freedom, couplings, factor, diagonal)


def narrow(level, margin):
    freedom, couplings, factor, diagonal = level
    along_x, along_y, along_z = couplings
    return (
        freedom[margin:-margin],
        (along_x[margin:-margin], along_y[margin:-margin], along_z[margin:-margin]),
        factor,
        diagonal[margin:-margin],
    )


def operate(values, level):
    freedom, couplings, factor, diagonal = level
    return freedom * factor * laplace(freedom * values, couplings) + (1.0 - freedom) * values


def operate_rim(values_rim, level):
    return operate(values_rim, level)[:, 1:-1]


def relax(values_rim, forcing, level):
    return values_rim[:, 1:-1] + OMEGA * (forcing - operate_rim(values_rim, level)) / level[3][1:-1]


def children(values):
    leading = values.shape[:-3]
    depth_z, rows_y, cols_x = values.shape[-3:]
    return values.reshape(leading + (depth_z // 2, 2, rows_y // 2, 2, cols_x // 2, 2))


def restrict(values):
    return jnp.sum(children(values), axis=(-5, -3, -1))


def coarsen_mean(values):
    return 0.125 * jnp.sum(children(values), axis=(-5, -3, -1))


def coarsen_any(values):
    return jnp.max(children(values), axis=(-5, -3, -1))


def prolong(values):
    return jnp.repeat(jnp.repeat(jnp.repeat(values, 2, axis=-3), 2, axis=-2), 2, axis=-1)


def rim(values):
    return extended(values, (("space", 1),), 1)


def smooth_level(forcing, level, descend):
    single = narrow(level, 1)
    smoothed = OMEGA * forcing / level[3][2:-2]
    relaxed = relax(rim(smoothed), forcing, single)
    leftover = forcing - operate_rim(rim(relaxed), single)
    corrected = relaxed + prolong(descend(restrict(leftover)))
    polished = relax(rim(corrected), forcing, single)
    return relax(rim(polished), forcing, single)


def cycle(forcing, levels, solver, tier_index):
    if tier_index == len(levels):
        return solver(forcing)
    descend = partial(cycle, levels=levels, solver=solver, tier_index=tier_index + 1)
    return smooth_level(forcing, levels[tier_index], descend)


def inner_product(first_arg, second_arg):
    return lax.psum(jnp.sum(first_arg * second_arg, axis=(1, 2, 3)), "space")


def on_device(design, passive, fixed_mask, load_index):
    members = lax.axis_size("space")
    position = lax.axis_index("space")
    planes = design.shape[0]
    one_plane = jnp.ones((1,) + design.shape[1:], jnp.float32)
    lower_rim = one_plane * (position > 0).astype(jnp.float32)
    upper_rim = one_plane * (position < members - 1).astype(jnp.float32)
    inside = jnp.concatenate([lower_rim, jnp.ones(design.shape, jnp.float32), upper_rim], axis=0)
    weights = cone_filter(inside)
    design_padded = extended(design, (("space", 0),), 1)
    filtered = cone_filter(design_padded) / weights
    density = jnp.where(passive == 1, 1.0, jnp.where(passive == 2, 0.0, filtered))
    modulus = E_MIN + (1.0 - E_MIN) * density**3
    freedom = (1 - fixed_mask).astype(jnp.float32)
    levels = []
    current_mod = modulus
    current_free = freedom
    for tier_index in range(LEVELS):
        padded = extended(jnp.stack([current_mod, current_free]), (("space", 1),), 2)
        levels.append(build_level(padded[0], padded[1], 2.0**tier_index))
        current_mod = coarsen_mean(current_mod)
        current_free = coarsen_any(current_free)
    joined = extended(jnp.stack([current_mod, current_free]), (("space", 1),), 1)
    coarse = build_level(joined[0], joined[1], 2.0**LEVELS)

    def solver(forcing):
        values = OMEGA * forcing / coarse[3][1:-1]
        for repeat in range(COARSE_SWEEPS - 1):
            values = relax(extended(values, (("space", 1),), 1), forcing, coarse)
        return values

    case_count = load_index.shape[0]
    voxels = planes * design.shape[1] * design.shape[2]
    local_index = load_index - position * voxels
    present = (local_index >= 0) & (local_index < voxels)
    case_rows = jnp.broadcast_to(jnp.arange(case_count, dtype=jnp.int32)[:, None], load_index.shape)
    sources = (
        jnp.zeros((case_count, voxels), jnp.float32)
        .at[case_rows, jnp.where(present, local_index, 0)]
        .add(present.astype(jnp.float32))
    )
    sources = (HEAT_SOURCE + sources.reshape((case_count,) + design.shape)) * freedom
    fine_single = narrow(levels[0], 1)
    solution = jnp.zeros_like(sources)
    residual = sources
    precond = cycle(residual, levels, solver, 0)
    product = inner_product(residual, precond)
    direction = precond
    for iteration in range(ITERS):
        direction_rim = extended(direction, (("space", 1),), 1)
        applied = operate_rim(direction_rim, fine_single)
        curvature = lax.psum(jnp.sum(direction * applied, axis=(1, 2, 3)), "space")
        step_size = (product / curvature)[:, None, None, None]
        solution = solution + step_size * direction
        residual = residual - step_size * applied
        if iteration + 1 < ITERS:
            precond = cycle(residual, levels, solver, 0)
            product_next = inner_product(residual, precond)
            direction = precond + (product_next / product)[:, None, None, None] * direction
            product = product_next
    masked_rim = extended(solution * freedom, (("space", 1),), 1)
    local_energy = jnp.sum(cell_energy(masked_rim, fine_single[1])[:, 1:-1], axis=0)
    energy = lax.psum(local_energy, "case")
    gradient = -1.5 * (1.0 - E_MIN) * density**2 * energy / modulus
    gradient = jnp.where(passive == 0, gradient, 0.0)
    scaled_rim = extended(gradient / weights, (("space", 0),), 1)
    sensitivity = jnp.where(passive == 0, cone_filter(scaled_rim), 0.0)
    return (solution, sensitivity)


def solution(mesh):
    placed = (
        P("space", None, None),
        P("space", None, None),
        P("space", None, None),
        P("case", None),
    )
    return jax.shard_map(
        on_device,
        mesh=mesh,
        in_specs=placed,
        out_specs=(P("case", "space", None, None), P("space", None, None)),
        check_vma=False,
    )
```

profile of v0, /device:TPU:1, one launch (start us, length us, event | category | flops | bytes accessed | tf_op | source)
XLA Modules:
  0.0 1906.8 jit_solution(2610501965379605256)
XLA Ops:
  21.2 11.9 reshape.268
  39.4 56.2 %scatter_custom_fusion = f32[81920]{0:T(1024)S(1)} fusion(s32[8192]{0:T(1024)S(1)} %bitcast.215, f32[8192]{0:T(1024)S(1)} %bitcast.214, f32[]{:T(128)} %constant.21.clone.1), kind=kCustom, calls=%fused_computation.517 | custom fusion | flops 8192 | bytes 327684
  98.8 11.8 reshape.267
  170.6 23.1 %reshape.266 = f32[2,4,2,20,2,64,2]{6,5,4,3,2,1,0:T(8,128)} reshape(f32[2,8,40,128]{3,2,1,0:T(8,128)} %fusion.72) | data formatting | bytes 655360 | tf_op jit(solution)/shard_map/reshape | solution.py:134
  193.7 8.2 reduce_sum.205
  282.9 6.3 collective-permute-start.32
  291.5 6.3 collective-permute-start.34
  364.7 6.9 collective-permute-start.46
  372.9 8.2 collective-permute-done.47
  381.8 8.3 collective-permute-start.48
  391.4 7.2 collective-permute-done.49
  400.0 154.8 %all-reduce.395 = (f32[2]{0:T(128)S(1)}, f32[2]{0:T(128)S(1)}) all-reduce(f32[2]{0:T(128)S(1)} %get-tuple-element.5, f32[2]{0:T(128)S(1)} %get-tuple-element.4), channel_id=1, replica_groups=mesh['case'=2,'space'=64] {'space'}, use_global_device_ids=true, to_apply=%region_16.17 | all-reduce | flops 4 | bytes 32 | tf_op jit(solution)/shard_map/psum | solution.py:175
  570.0 22.3 %reshape.277 = f32[2,4,2,20,2,64,2]{6,5,4,3,2,1,0:T(8,128)} reshape(f32[2,8,40,128]{3,2,1,0:T(8,128)S(1)} %fusion.120) | data formatting | bytes 655360 | tf_op jit(solution)/shard_map/reshape | solution.py:134
  592.3 8.1 reduce_sum.218
  664.2 7.8 collective-permute-start.68
  674.3 8.1 collective-permute-start.70
  684.7 6.3 collective-permute-start.72
  693.4 6.3 collective-permute-start.74
  770.0 6.8 collective-permute-start.86
  778.1 8.2 collective-permute-done.87
  787.2 159.6 %psum.51 = f32[2]{0:T(128)S(1)} all-reduce(f32[2]{0:T(128)S(1)} %get-tuple-element.18), channel_id=1, replica_groups=mesh['case'=2,'space'=64] {'space'}, use_global_device_ids=true, to_apply=%region_24.25 | all-reduce | flops 2 | bytes 16 | tf_op jit(solution)/shard_map/psum | solution.py:175
  954.6 144.2 %psum.52 = f32[2]{0:T(128)S(1)} all-reduce(f32[2]{0:T(128)S(1)} %get-tuple-element.16), channel_id=1, replica_groups=mesh['case'=2,'space'=64] {'space'}, use_global_device_ids=true, to_apply=%region_26.27 | all-reduce | flops 2 | bytes 16 | tf_op jit(solution)/shard_map/psum | solution.py:229
  1116.0 22.4 %reshape.285 = f32[2,4,2,20,2,64,2]{6,5,4,3,2,1,0:T(8,128)} reshape(f32[2,8,40,128]{3,2,1,0:T(8,128)S(1)} %fusion.168) | data formatting | bytes 655360 | tf_op jit(solution)/shard_map/reshape | solution.py:134
  1138.4 8.1 reduce_sum.226
  1214.6 6.5 collective-permute-start.110
  1223.3 6.3 collective-permute-start.112
  1231.9 6.3 collective-permute-start.114
  1306.5 6.6 collective-permute-start.126
  1314.4 8.4 collective-permute-done.127
  1323.7 159.1 %psum.53 = f32[2]{0:T(128)S(1)} all-reduce(f32[2]{0:T(128)S(1)} %get-tuple-element.12), channel_id=1, replica_groups=mesh['case'=2,'space'=64] {'space'}, use_global_device_ids=true, to_apply=%region_32.33 | all-reduce | flops 2 | bytes 16 | tf_op jit(solution)/shard_map/psum | solution.py:175
  1489.7 144.0 %psum.54 = f32[2]{0:T(128)S(1)} all-reduce(f32[2]{0:T(128)S(1)} %fusion.200), channel_id=1, replica_groups=mesh['case'=2,'space'=64] {'space'}, use_global_device_ids=true, to_apply=%region_34.35 | all-reduce | flops 2 | bytes 16 | tf_op jit(solution)/shard_map/psum | solution.py:229
  1644.3 245.3 %all-reduce.398.cloned.1.call-done = f32[8,40,128]{2,1,0:T(8,128)} async-done(((f32[8,40,128]{2,1,0:T(8,128)}), f32[8,40,128]{2,1,0:T(8,128)}) %all-reduce.398.cloned.1.call-update) | async-done | bytes 163856 | tf_op jit(solution)/shard_map/psum | solution.py:240
  (826 shorter events, 587.7 us)
Async XLA Ops:
  7.2 1882.4 %all-reduce.398.cloned.1.call-start = ((), (), s32[]{:S(2)}) async-start(), calls=%async_computation | async-start | bytes 327680 | tf_op jit(solution)/shard_map/psum | solution.py:240
  8.0 87.6 %collective-permute-start = (f32[1,40,128]{2,1,0:T(8,128)S(1)}, f32[1,40,128]{2,1,0:T(8,128)S(1)}, u32[]{:S(2)}, u32[]{:S(2)}) collective-permute-start(f32[1,40,128]{2,1,0:T(8,128)S(1)} %get-tuple-element.102), channel_id=1, source_target_pairs={{0,1},{1,2},{2,3},{3,4},{4,5},{5,6},{6,7},{7,8},{8,9},{9,10},{10,1... | collective-permute-start | bytes 61448 | tf_op jit(solution)/shard_map/ppermute | solution.py:26
  12.3 83.3 %collective-permute-start.1 = (f32[1,40,128]{2,1,0:T(8,128)S(1)}, f32[1,40,128]{2,1,0:T(8,128)S(1)}, u32[]{:S(2)}, u32[]{:S(2)}) collective-permute-start(f32[1,40,128]{2,1,0:T(8,128)S(1)} %get-tuple-element.103), channel_id=1, source_target_pairs={{1,0},{2,1},{3,2},{4,3},{5,4},{6,5},{7,6},{8,7},{9,8},{10,9},{11,1... | collective-permute-start | bytes 61448 | tf_op jit(solution)/shard_map/ppermute | solution.py:27
  117.2 15.0 collective-permute-start.21
  118.5 15.0 collective-permute-start.20
  123.4 16.8 collective-permute-start.15
  124.7 17.0 collective-permute-start.14
  128.8 20.0 %collective-permute-start.2 = (f32[2,2,40,128]{3,2,1,0:T(8,128)S(1)}, f32[2,2,40,128]{3,2,1,0:T(8,128)S(1)}, u32[]{:S(2)}, u32[]{:S(2)}) collective-permute-start(f32[2,2,40,128]{3,2,1,0:T(8,128)S(1)} %get-tuple-element.92), channel_id=1, source_target_pairs={{0,1},{1,2},{2,3},{3,4},{4,5},{5,6},{6,7},{7,8},{8,9},{9,10},{10,1... | collective-permute-start | bytes 245768 | tf_op jit(solution)/shard_map/ppermute | solution.py:26
  132.2 16.6 collective-permute-start.3
  133.5 9.2 collective-permute-start.8
  264.8 7.4 collective-permute-start.29
  273.2 7.4 collective-permute-start.31
  281.6 7.7 collective-permute-start.33
  290.2 7.7 collective-permute-start.35
  364.7 8.2 collective-permute-start.46
  371.6 9.5 collective-permute-start.47
  381.8 9.6 collective-permute-start.48
  390.1 8.5 collective-permute-start.49
  662.9 9.1 collective-permute-start.69
  664.2 8.6 collective-permute-start.68
  673.0 9.4 collective-permute-start.71
  674.3 8.9 collective-permute-start.70
  683.4 7.7 collective-permute-start.73
  692.1 7.7 collective-permute-start.75
  713.8 7.4 collective-permute-start.78
  770.0 8.1 collective-permute-start.86
  776.8 9.6 collective-permute-start.87
  1213.3 7.8 collective-permute-start.111
  1222.0 7.7 collective-permute-start.113
  1230.6 7.7 collective-permute-start.115
  1306.5 7.9 collective-permute-start.126
  1313.1 9.8 collective-permute-start.127
  (125 other events, 1618.5 us)
Sparse Core Ops, SparseCore 0:
  1644.4 245.0 all-reduce.397
where the time goes:
time: 1920 us; the launch traced here: 1910 us
  blocking collectives  762 us (40%)
  waiting for transfers between devices  442 us (23%)
  starting transfers between devices  407 us (21%)
  other arithmetic  142 us (7%)
  local copies, waits for them, and re-layouts  135 us (7%)
    psum x3, blocking collectives, inner_product(): return lax.psum(jnp.sum(first_arg * second_arg, axis=(1, 2, 3)), 'space')  473 us
    ppermute x67, starting transfers between devices, extended(): before = lax.ppermute(last, axis, up)  320 us
    psum x2, blocking collectives, on_device(): curvature = lax.psum(jnp.sum(direction * applied, axis=(1, 2, 3)), 'space')  288 us
    psum x1, waiting for transfers between devices, on_device(): energy = lax.psum(local_energy, 'case')  245 us
    ppermute x67, waiting for transfers between devices, extended(): after = lax.ppermute(initial, axis, down)  182 us
    reshape x9, local copies, waits for them, and re-layouts, children(): values.reshape(leading + (depth_z // 2, 2, rows_y // 2, 2, cols_x // 2, 2))  106 us
    ppermute x67, starting transfers between devices, extended(): after = lax.ppermute(initial, axis, down)  87.4 us
    unnamed x5, other arithmetic  58.6 us
  transfers between devices with their start and end apart: 135, of which 63 were waited for; matrix products, arithmetic and copies ran while one was open for 5% of the time, Pallas kernels for 0%

commit v1 on v0

v1 whole, which is shorter than its diff:
```python
import functools

import jax
import jax.numpy as jnp
from jax import lax
from jax.experimental import pallas as pl
from jax.experimental.pallas import tpu as pltpu
from jax.sharding import PartitionSpec as P

ITERS = 3
E_MIN = 0.01
OMEGA = 0.8
HEAT_SOURCE = 0.05
EDGE_WEIGHT = 1.5 - 2.0**0.5

F32 = jnp.float32
NY, NX = 40, 128
BLOCK = 8
HALO = 7
WINDOW = BLOCK + 2 * HALO
Q1, R1 = 10, 24
REACH = 11
ND = 2 * REACH + 1
R2 = 16
R3 = 8
TALK = 24
CPARAMS = pltpu.CompilerParams(vmem_limit_bytes=40 * 1024 * 1024)


def iota(shape, dim):
    return lax.broadcasted_iota(jnp.int32, shape, dim)


def roll(v, by, dim):
    return pltpu.roll(v, by % v.shape[dim], dim)


def dot(a, b):
    return lax.dot_general(
        a, b, (((1,), (0,)), ((), ())), precision=lax.Precision.HIGHEST, preferred_element_type=F32
    )


def planes(lo, hi, body, group=2):
    count = (hi - lo) // group

    def step(i, carry):
        for k in range(group):
            body(lo + i * group + k)
        return carry

    lax.fori_loop(0, count, step, 0)
    for j in range(lo + count * group, hi):
        body(j)


def fine_to_half(case):
    i, j = iota((128, 128), 0), iota((128, 128), 1)
    return (j == 64 * case + (i >> 1)).astype(F32)


def half_to_fine(case):
    i, j = iota((128, 128), 0), iota((128, 128), 1)
    return (i == 64 * case + (j >> 1)).astype(F32)


def half_to_quarter(low):
    i, j = iota((128, 128), 0), iota((128, 128), 1)
    return (j == 64 * low + 32 * (i >> 6) + ((i & 63) >> 1)).astype(F32)


def quarter_to_half(low):
    i, j = iota((128, 128), 0), iota((128, 128), 1)
    return (i == 64 * low + 32 * (j >> 6) + ((j & 63) >> 1)).astype(F32)


def quarter_to_eighth():
    i, j = iota((128, 128), 0), iota((128, 128), 1)
    return (j == 16 * ((i >> 5) & 1) + ((i & 31) >> 1)).astype(F32)


def eighth_to_quarter():
    i, j = iota((128, 128), 0), iota((128, 128), 1)
    return (i == 16 * ((j >> 5) & 1) + ((j & 31) >> 1)).astype(F32)


def z_prev(v):
    return jnp.concatenate([jnp.zeros_like(v[:1]), v[:-1]], axis=0)


def z_next(v):
    return jnp.concatenate([v[1:], jnp.zeros_like(v[:1])], axis=0)


def z_prev2(v):
    turned = roll(v, 64, 2)
    return jnp.where(iota(v.shape, 2) >= 64, turned, z_prev(turned))


def z_next2(v):
    turned = roll(v, 64, 2)
    return jnp.where(iota(v.shape, 2) < 64, turned, z_next(turned))


def couple(m, f, factor, width, zp, zn):
    lead = (iota(m.shape, 2) & (width - 1)) > 0
    first = iota(m.shape, 1) > 0
    sides = (
        (lambda v: roll(v, 1, 2), lambda v: roll(v, -1, 2), lead),
        (lambda v: roll(v, 1, 1), lambda v: roll(v, -1, 1), first),
        (zp, zn, None),
    )
    total = jnp.zeros_like(m)
    held = jnp.zeros_like(m)
    coupling = []
    for prev, after, mask in sides:
        k = jnp.sqrt(m * prev(m))
        if mask is not None:
            k = jnp.where(mask, k, 0.0)
        ka = after(k)
        total = total + k + ka
        held = held + k * (1.0 - prev(f)) + ka * (1.0 - after(f))
        coupling.append(factor * k * f * prev(f))
    rest = f * factor * held + (1.0 - f)
    weight = OMEGA / (f * factor * total + (1.0 - f))
    return coupling[0], coupling[1], coupling[2], rest, weight


def apply(v, c, zp, zn):
    kx, ky, kz, rest = c[:4]
    fx = kx * (v - roll(v, 1, 2))
    fy = ky * (v - roll(v, 1, 1))
    fz = kz * (v - zp(v))
    return rest * v + (fx - roll(fx, -1, 2)) + (fy - roll(fy, -1, 1)) + (fz - zn(fz))


def cut(c, lo, hi):
    return tuple(x[lo:hi] for x in c)


def apply_plane(v_ref, case, j, c_ref):
    v = v_ref[case, j]
    fx = c_ref[0, j] * (v - roll(v, 1, 1))
    fy = c_ref[1, j] * (v - roll(v, 1, 0))
    out = c_ref[3, j] * v + (fx - roll(fx, -1, 1)) + (fy - roll(fy, -1, 0))
    return out + c_ref[2, j] * (v - v_ref[case, j - 1]) + c_ref[2, j + 1] * (v - v_ref[case, j + 1])


def pairs_of_rows(v, scratch):
    n, rows, _ = v.shape
    scratch[: n * rows, :] = v.reshape(n * rows, 128)
    half = n * rows // 2
    even = scratch[pl.ds(0, half, stride=2), :]
    odd = scratch[pl.ds(1, half, stride=2), :]
    return (even + odd).reshape(n, rows // 2, 128)


def rows_twice(v, scratch):
    n, rows, _ = v.shape
    flat = v.reshape(n * rows, 128)
    scratch[pl.ds(0, n * rows, stride=2), :] = flat
    scratch[pl.ds(1, n * rows, stride=2), :] = flat
    return scratch[: 2 * n * rows, :].reshape(n, 2 * rows, 128)


def flat_dot(v, matrix):
    n, rows, _ = v.shape
    return dot(v.reshape(n * rows, 128), matrix).reshape(n, rows, 128)


def fine_to_level1(t_ref, r_ref, work, count, split):
    flat0 = t_ref[0, :count].reshape(count * NY, 128)
    flat1 = t_ref[1, :count].reshape(count * NY, 128)
    work[: count * NY, :] = dot(flat0, fine_to_half(0)) + dot(flat1, fine_to_half(1))
    r_ref[...] = jnp.zeros_like(r_ref)
    for p in range(count):
        even = work[pl.ds(p * NY, NY // 2, stride=2), :]
        odd = work[pl.ds(p * NY + 1, NY // 2, stride=2), :]
        r_ref[split + p, 0 : NY // 2, :] = even + odd


def down(r_ref, c0, c1, s1, s2, t_ref, work, s2_out, s21_out, r1_out):
    def first(j):
        for case in range(2):
            s1[case, j] = c0[4, j] * r_ref[case, j]

    planes(1, WINDOW - 1, first)

    def second(j):
        for case in range(2):
            s2[case, j] = s1[case, j] + c0[4, j] * (r_ref[case, j] - apply_plane(s1, case, j, c0))

    planes(2, WINDOW - 2, second)

    def third(q):
        for case in range(2):
            a, b = 2 * q + 3, 2 * q + 4
            t_ref[case, q] = (r_ref[case, a] - apply_plane(s2, case, a, c0)) + (
                r_ref[case, b] - apply_plane(s2, case, b, c0)
            )

    planes(0, 8, third, 1)
    for case in range(2):
        s2_out[case] = s2[case, 5:17]
    fine_to_level1(t_ref, r1_out, work, 8, 1)

    c = tuple(c1[k] for k in range(5))
    forcing = r1_out[1:9]
    smoothed = c[4][1:9] * forcing
    leftover = forcing - apply(smoothed, cut(c, 1, 9), z_prev, z_next)
    relaxed = (smoothed + c[4][1:9] * leftover)[1:7]
    s21_out[...] = relaxed[1:5]
    rest = (forcing[1:7] - apply(relaxed, cut(c, 2, 8), z_prev, z_next))[1:5]
    low, high = rest[0] + rest[1], rest[2] + rest[3]
    mixed = dot(low, half_to_quarter(0)) + dot(high, half_to_quarter(1))
    summed = pairs_of_rows(mixed[None], work)[0]
    return jnp.concatenate([summed, jnp.zeros((4, 128), F32)], axis=0)


def spread(out_ref, tile):
    out_ref[...] = jnp.broadcast_to(tile[None], out_ref.shape)


def count_kernel(me, index, out, acc):
    base = (me[0] * BLOCK - HALO) * NY
    rows = WINDOW * NY
    chunk = 512
    total = index.shape[1]
    for case in range(2):
        acc[...] = jnp.zeros_like(acc)

        def step(i, carry):
            ids = index[pl.ds(case, 1), pl.ds(pl.multiple_of(i * chunk, chunk), chunk)]
            row = (ids >> 7) - base
            col = ids & 127
            hit_row = jnp.where(iota((rows, chunk), 0) == row, 1.0, 0.0).astype(jnp.bfloat16)
            hit_col = jnp.where(iota((128, chunk), 0) == col, 1.0, 0.0).astype(jnp.bfloat16)
            acc[...] += lax.dot_general(
                hit_row, hit_col, (((1,), (1,)), ((), ())), preferred_element_type=F32
            )
            return carry

        lax.fori_loop(0, total // chunk, step, 0)
        out[case] = acc[...].reshape(WINDOW, NY, 128)


def neighbours_x(p):
    lane = iota(p.shape, 1)
    return jnp.where(lane > 0, roll(p, 1, 1), 0.0) + jnp.where(lane < NX - 1, roll(p, -1, 1), 0.0)


def neighbours_y(p):
    row = iota(p.shape, 0)
    return jnp.where(row > 0, roll(p, 1, 0), 0.0) + jnp.where(row < NY - 1, roll(p, -1, 0), 0.0)


def filter_parts(p):
    sides_y = neighbours_y(p)
    cross = neighbours_x(p) + sides_y
    return cross, 1.5 * p + 0.5 * cross + EDGE_WEIGHT * neighbours_x(sides_y)


def weight_of(me, members, z):
    at = me * BLOCK + z
    lane, row = iota((NY, NX), 1), iota((NY, NX), 0)
    nx = (lane > 0).astype(F32) + (lane < NX - 1).astype(F32)
    ny = (row > 0).astype(F32) + (row < NY - 1).astype(F32)
    nz = jnp.where(at > 0, 1.0, 0.0) + jnp.where(at < members * BLOCK - 1, 1.0, 0.0)
    return 1.5 + 0.5 * (nx + ny + nz) + EDGE_WEIGHT * (nx * ny + nx * nz + ny * nz)


def setup_kernel(
    members, me_ref, own, before, after, counts,
    c0, c1, force, s2_out, s21_out, r1_out, talk, mod, free, scale,
    raw, cross, base, s1, s2, t_ref, work, small,
):
    me = me_ref[0]

    def fill(k):
        raw[k] = before[0, k]
        raw[8 + k] = own[0, k]
        raw[16 + k] = after[0, k]

    planes(0, 8, fill, 1)

    def parts(k):
        a, b = filter_parts(raw[k])
        cross[k] = a
        base[k] = b

    planes(0, 24, parts)

    def material(j, passive, fixed):
        z = j - HALO
        at = me * BLOCK + z
        inside = jnp.where((at >= 0) & (at < members * BLOCK), 1.0, 0.0)
        filtered = base[j + 1] + 0.5 * (raw[j] + raw[j + 2]) + EDGE_WEIGHT * (cross[j] + cross[j + 2])
        weight = weight_of(me, members, z)
        density = jnp.where(passive == 1.0, 1.0, jnp.where(passive == 2.0, 0.0, filtered / weight))
        modulus = E_MIN + (1.0 - E_MIN) * density * density * density
        mod[j] = inside * modulus
        freedom = inside * (1.0 - fixed)
        free[j] = freedom
        for case in range(2):
            force[case, j] = freedom * (HEAT_SOURCE + counts[case, j])
        gradient = (-1.5 * (1.0 - E_MIN)) * density * density / (modulus * weight)
        return jnp.where(passive == 0.0, inside * gradient, 0.0)

    def below(j):
        material(j, before[1, j + 1], before[2, j + 1])

    def above(k):
        material(15 + k, after[1, k], after[2, k])

    planes(0, 6, below)
    scale[0] = material(6, before[1, 7], before[2, 7])

    def middle(k):
        scale[1 + k] = material(HALO + k, own[1, k], own[2, k])

    planes(0, 8, middle)
    scale[9] = material(15, after[1, 0], after[2, 0])
    planes(1, 7, above)

    lane, row = iota((NY, NX), 1), iota((NY, NX), 0)
    zero = jnp.zeros((NY, NX), F32)
    c0[2, 0] = zero

    def coefficients(j):
        m, f = mod[j], free[j]
        total, held = zero, zero
        for dim, mask, slot in ((1, lane > 0, 0), (0, row > 0, 1)):
            k = jnp.where(mask, jnp.sqrt(m * roll(m, 1, dim)), 0.0)
            ka = roll(k, -1, dim)
            fp = roll(f, 1, dim)
            total = total + k + ka
            held = held + k * (1.0 - fp) + ka * (1.0 - roll(f, -1, dim))
            c0[slot, j] = k * f * fp
        k, ka = jnp.sqrt(m * mod[j - 1]), jnp.sqrt(m * mod[j + 1])
        total = total + k + ka
        held = held + k * (1.0 - free[j - 1]) + ka * (1.0 - free[j + 1])
        c0[2, j] = k * f * free[j - 1]
        c0[3, j] = f * held + (1.0 - f)
        c0[4, j] = OMEGA / (f * total + (1.0 - f))

    planes(1, WINDOW - 1, coefficients)
    last = WINDOW - 1
    c0[2, last] = jnp.sqrt(mod[last] * mod[last - 1]) * free[last] * free[last - 1]
    for slot in (0, 1, 3, 4):
        c0[slot, 0] = zero
        c0[slot, last] = zero

    def add_up(q):
        t_ref[0, q] = mod[2 * q + 1] + mod[2 * q + 2]
        t_ref[1, q] = free[2 * q + 1] + free[2 * q + 2]

    planes(0, Q1, add_up)
    fine_to_level1(t_ref, small, work, Q1, 0)
    both = small[...]
    second = iota(both.shape, 2) >= 64
    both = jnp.where(second, (both > 0.0).astype(F32), 0.125 * both)
    turned = roll(both, 64, 2)
    m1 = jnp.where(second, turned, both)
    f1 = jnp.where(second, both, turned)
    for k, value in enumerate(couple(m1, f1, 2.0, 64, z_prev, z_next)):
        c1[k] = value

    low, high = both[3] + both[4], both[5] + both[6]
    mixed = dot(low, half_to_quarter(0)) + dot(high, half_to_quarter(1))
    coarse = pairs_of_rows(mixed[None], work)[0]
    is_free = (iota(coarse.shape, 1) & 32) > 0
    coarse = jnp.where(is_free, (coarse > 0.0).astype(F32), 0.125 * coarse)

    tile = down(force, c0, c1, s1, s2, t_ref, work, s2_out, s21_out, r1_out)
    small[0, 0:16, :] = tile
    small[0, 10:22, :] = coarse
    spread(talk, small[0])


def coarse_window(me, members, gathered, rows):
    lo, hi = rows
    tiles = []
    for d in range(ND):
        at = me + d - REACH
        inside = jnp.where((at >= 0) & (at < members), 1.0, 0.0)
        tiles.append(inside * gathered[jnp.clip(at, 0, members - 1), lo:hi, :])
    return jnp.stack(tiles, axis=0)


def coarse_setup(me, members, gathered, c2, c3, work, wide):
    wide[...] = jnp.zeros_like(wide)
    wide[:, 0:10, :] = coarse_window(me, members, gathered, (10, 20))
    both = wide[...]
    is_free = (iota(both.shape, 2) & 32) > 0
    m = jnp.where(is_free, roll(both, 32, 2), both)
    f = jnp.where(is_free, both, roll(both, -32, 2))
    for k, value in enumerate(couple(m, f, 4.0, 32, z_prev2, z_next2)):
        c2[k] = value
    eighth = quarter_to_eighth()
    m3 = 0.125 * pairs_of_rows(flat_dot(m, eighth), work)
    f3 = (pairs_of_rows(flat_dot(f, eighth), work) > 0.0).astype(F32)
    for k, value in enumerate(couple(m3, f3, 8.0, 16, z_prev, z_next)):
        c3[k] = value


def coarse_solve(r2, c2, c3, work):
    c = tuple(c2[k] for k in range(5))
    smoothed = c[4] * r2
    relaxed = smoothed + c[4] * (r2 - apply(smoothed, c, z_prev2, z_next2))
    leftover = (r2 - apply(relaxed, c, z_prev2, z_next2))[2 : ND - 2]
    forcing = pairs_of_rows(flat_dot(leftover, quarter_to_eighth()), work)
    lo, hi = 2, ND - 2
    v = c3[4, lo:hi] * forcing
    for _ in range(7):
        ck = tuple(c3[k, lo:hi] for k in range(5))
        v = v + ck[4] * (forcing - apply(v, ck, z_prev, z_next))
        v, forcing = v[1:-1], forcing[1:-1]
        lo, hi = lo + 1, hi - 1
    up = rows_twice(flat_dot(v, eighth_to_quarter()), work)
    lo, hi = REACH - 2, REACH + 3
    v = relaxed[lo:hi] + up
    ck = cut(c, lo, hi)
    for _ in range(2):
        v = v + ck[4] * (r2[lo:hi] - apply(v, ck, z_prev2, z_next2))
    return v[1:4]


def up_kernel(
    members, first, me_ref, gathered, r_ref, s2_ref, s21, s21_before, s21_after, r1_ref, c0, c1, *rest
):
    if first:
        out, c2, c3, va, vb, work, wide = rest
    else:
        c2, c3, out, dots, va, vb, work, wide = rest
    me = me_ref[0]
    if first:
        coarse_setup(me, members, gathered, c2, c3, work, wide)
    else:
        total = gathered[0, 8:16, :]
        for d in range(1, members):
            total = total + gathered[d, 8:16, :]
        dots[...] = total
    r2 = coarse_window(me, members, gathered, (0, 16))
    r2 = jnp.where(iota(r2.shape, 1) < 10, r2, 0.0)
    e2 = coarse_solve(r2, c2, c3, work)

    parts = []
    for low in range(2):
        spread_out = flat_dot(e2, quarter_to_half(low))
        parts.append(rows_twice(spread_out, work)[:, :R1])
    lifted = [parts[(z + 2) & 1][(z + 2) >> 1] for z in range(-2, 4)]
    correction = jnp.stack([lifted[(q - 3) // 2 + 2] for q in range(Q1)], axis=0)
    relaxed = jnp.concatenate([s21_before[1:4], s21[...], s21_after[0:3]], axis=0)
    c = tuple(c1[k] for k in range(5))
    v = relaxed + correction
    v = (v + c[4] * (r1_ref[...] - apply(v, c, z_prev, z_next)))[1:9]
    v = (v + c[4][1:9] * (r1_ref[1:9] - apply(v, cut(c, 1, 9), z_prev, z_next)))[1:7]

    for case in range(2):
        work[0 : 12 * R1, :] = rows_twice(flat_dot(v, half_to_fine(case)), work).reshape(12 * R1, 128)
        for p in range(6):
            fine = work[p * 2 * R1 : p * 2 * R1 + NY, :]
            va[case, 5 + 2 * p] = s2_ref[case, 2 * p] + fine
            va[case, 6 + 2 * p] = s2_ref[case, 2 * p + 1] + fine

    def once(j):
        for case in range(2):
            vb[case, j] = va[case, j] + c0[4, j] * (r_ref[case, j] - apply_plane(va, case, j, c0))

    planes(6, 16, once)

    def twice(j):
        for case in range(2):
            out[case, j - HALO] = vb[case, j] + c0[4, j] * (r_ref[case, j] - apply_plane(vb, case, j, c0))

    planes(7, 15, twice)


def lay_out(win, own, before, after, width):
    for case in range(2):
        for k in range(width):
            win[case, HALO - 1 - k] = before[case, before.shape[1] - 1 - k]
            win[case, HALO + BLOCK + k] = after[case, k]

    def inner(k):
        for case in range(2):
            win[case, HALO + k] = own[case, k]

    planes(0, BLOCK, inner)


def dot_rows(values):
    lane = iota((1, 128), 1)
    rows = []
    for a, b in values:
        rows.append(jnp.where(lane < 64, jnp.sum(a, keepdims=True), jnp.sum(b, keepdims=True)))
    return rows


def accumulate(count, term):
    def step(k, carry):
        return tuple(
            tuple(s + t for s, t in zip(carry[case], term(case, k))) for case in range(2)
        )

    zero = jnp.zeros((NY, NX), F32)
    start = tuple(tuple(zero for _ in range(count)) for _ in range(2))
    sums = lax.fori_loop(0, BLOCK, step, start)
    return dot_rows([(sums[0][i], sums[1][i]) for i in range(count)])


def finish_talk(talk, tile, rows, small):
    small[0, 0:16, :] = tile
    for i, row in enumerate(rows):
        small[0, 10 + i : 11 + i, :] = row
    spread(talk, small[0, 0:16])


def first_kernel(
    own, before, after, force, c0, c1,
    u_win, w_win, s2_out, s21_out, r1_out, talk,
    s1, s2, t_ref, work, small,
):
    lay_out(u_win, own, before, after, HALO)

    def image(j):
        for case in range(2):
            w_win[case, j] = apply_plane(u_win, case, j, c0)

    planes(1, WINDOW - 1, image)

    def term(case, k):
        u = own[case, k]
        return (force[case, HALO + k] * u, w_win[case, HALO + k] * u)

    rows = accumulate(2, term)
    tile = down(w_win, c0, c1, s1, s2, t_ref, work, s2_out, s21_out, r1_out)
    finish_talk(talk, tile, rows, small)


def of_case(row, case):
    return row[:, 64 * case : 64 * case + 1]


def second_kernel(
    own, before, after, dots0, force, u0, w0, c0, c1,
    m_win, u1, w1, n0, s2_out, s21_out, r1_out, talk,
    s1, s2, t_ref, work, small,
):
    lay_out(m_win, own, before, after, HALO)
    alpha = [of_case(dots0[2:3, :] / dots0[3:4, :], case) for case in range(2)]

    def update(j):
        for case in range(2):
            u1[case, j] = u0[case, j] - alpha[case] * m_win[case, j]

    planes(0, WINDOW, update)

    def image(j):
        for case in range(2):
            n = apply_plane(m_win, case, j, c0)
            s1[case, j] = n
            w1[case, j] = w0[case, j] - alpha[case] * n

    planes(1, WINDOW - 1, image)
    for case in range(2):
        n0[case] = s1[case, HALO : HALO + BLOCK]

    def term(case, k):
        j = HALO + k
        u, w = u1[case, j], w1[case, j]
        r = force[case, j] - alpha[case] * w0[case, j]
        return (r * u, w * u, u * w0[case, j] + u0[case, j] * w)

    rows = accumulate(3, term)
    tile = down(w1, c0, c1, s1, s2, t_ref, work, s2_out, s21_out, r1_out)
    finish_talk(talk, tile, rows, small)


def third_kernel(
    own, before, after, dots0, dots1, force, u0, w0, m0, n0, u1, w1, c0,
    u2, p1, x2, talk, m_win,
):
    lay_out(m_win, own, before, after, 2)
    gamma0, delta0 = dots0[2:3, :], dots0[3:4, :]
    gamma1 = dots1[2:3, :]
    beta = gamma1 / gamma0
    curve = dots1[3:4, :] + beta * dots1[4:5, :] + beta * beta * delta0
    a0 = [of_case(gamma0 / delta0, case) for case in range(2)]
    a1 = [of_case(gamma1 / curve, case) for case in range(2)]
    b1 = [of_case(beta, case) for case in range(2)]

    def update(i):
        j = i + 5
        for case in range(2):
            p = u1[case, j] + b1[case] * u0[case, j]
            p1[case, i] = p
            x2[case, i] = a0[case] * u0[case, j] + a1[case] * p
            u2[case, i] = u1[case, j] - a1[case] * (m_win[case, j] + b1[case] * m0[case, j])

    planes(0, 12, update)

    def term(case, k):
        j = HALO + k
        n1 = apply_plane(m_win, case, j, c0)
        s = w1[case, j] + b1[case] * w0[case, j]
        w = w1[case, j] - a1[case] * (n1 + b1[case] * n0[case, k])
        r = force[case, j] - a0[case] * w0[case, j] - a1[case] * s
        u, p = u2[case, k + 2], p1[case, k + 2]
        return (r * u, w * u, u * s + p * w)

    rows = accumulate(3, term)
    talk[...] = jnp.zeros_like(talk)
    for i, row in enumerate(rows):
        talk[:, i, :] = jnp.broadcast_to(row, (talk.shape[0], 128))


def last_kernel(gathered, dots0, dots1, u2, p1, x2, mod, free, state, energy, w_win):
    total = gathered[0]
    for d in range(1, gathered.shape[0]):
        total = total + gathered[d]
    gamma0, delta0 = dots0[2:3, :], dots0[3:4, :]
    gamma1 = dots1[2:3, :]
    beta1 = gamma1 / gamma0
    curve1 = dots1[3:4, :] + beta1 * dots1[4:5, :] + beta1 * beta1 * delta0
    gamma2 = total[0:1, :]
    beta2 = gamma2 / gamma1
    curve2 = total[1:2, :] + beta2 * total[2:3, :] + beta2 * beta2 * curve1
    a2 = [of_case(gamma2 / curve2, case) for case in range(2)]
    b2 = [of_case(beta2, case) for case in range(2)]

    def update(i):
        for case in range(2):
            x = x2[case, i] + a2[case] * (u2[case, i] + b2[case] * p1[case, i])
            w_win[case, i] = x

    planes(0, 12, update)
    for case in range(2):
        state[case] = w_win[case, 2:10]

    def hold(i):
        for case in range(2):
            w_win[case, i] = w_win[case, i] * free[i + 5]

    planes(0, 12, hold)
    lane, row = iota((NY, NX), 1), iota((NY, NX), 0)

    def power(i):
        m = mod[i + 6]
        out = jnp.zeros((NY, NX), F32)
        kx = jnp.where(lane > 0, jnp.sqrt(m * roll(m, 1, 1)), 0.0)
        ky = jnp.where(row > 0, jnp.sqrt(m * roll(m, 1, 0)), 0.0)
        kz, kn = jnp.sqrt(m * mod[i + 5]), jnp.sqrt(m * mod[i + 7])
        for case in range(2):
            v = w_win[case, i + 1]
            dx, dy = v - roll(v, 1, 1), v - roll(v, 1, 0)
            dz, dn = v - w_win[case, i], v - w_win[case, i + 2]
            px, py = kx * dx * dx, ky * dy * dy
            out = out + px + roll(px, -1, 1) + py + roll(py, -1, 0) + kz * dz * dz + kn * dn * dn
        energy[i] = out

    planes(0, 10, power)


def sensitivity_kernel(mine, other, scale, passive, out, g, cross, base):
    def gradient(i):
        value = scale[i] * (mine[i] + other[i])
        g[i] = value
        a, b = filter_parts(value)
        cross[i] = a
        base[i] = b

    planes(0, 10, gradient)

    def final(k):
        i = k + 1
        value = base[i] + 0.5 * (g[i - 1] + g[i + 1]) + EDGE_WEIGHT * (cross[i - 1] + cross[i + 1])
        out[k] = jnp.where(passive[k] == 0, value, 0.0)

    planes(0, 8, final)


def shape(*dims):
    return jax.ShapeDtypeStruct(dims, F32)


def call(body, outs, scratch, args, smem=0, name=None):
    vmem = pl.BlockSpec(memory_space=pltpu.VMEM)
    specs = [pl.BlockSpec(memory_space=pltpu.SMEM)] * smem + [vmem] * (len(args) - smem)
    return pl.pallas_call(
        body,
        out_shape=outs,
        in_specs=specs,
        out_specs=[vmem] * len(outs),
        scratch_shapes=[pltpu.VMEM(s, F32) for s in scratch],
        compiler_params=CPARAMS,
        name=name,
    )(*args)


def on_device(design, passive, fixed_mask, load_index):
    members = lax.axis_size("space")
    position = lax.axis_index("space")
    me = position.astype(jnp.int32).reshape(1)
    ahead = [(i, i + 1) for i in range(members - 1)]
    back = [(i + 1, i) for i in range(members - 1)]

    def both_ways(to_next, to_previous):
        return lax.ppermute(to_next, "space", ahead), lax.ppermute(to_previous, "space", back)

    def gather(tiles):
        return lax.all_to_all(tiles, "space", 0, 0)

    plane = (NY, NX)
    window = (2, WINDOW) + plane
    block = (2, BLOCK) + plane
    wide = (2, 12) + plane
    work = (800, 128)
    down_outs = [shape(*wide), shape(4, R1, 128), shape(Q1, R1, 128)]
    down_scratch = [window, window, (2, Q1) + plane, work, (Q1, R1, 128)]

    own = jnp.stack([design, passive.astype(F32), fixed_mask.astype(F32)])
    before, after = both_ways(own, own)
    counts = call(
        count_kernel, [shape(*window)], [(WINDOW * NY, 128)], (me, load_index), 1, "counts"
    )[0]
    c0, c1, force, s2, s21, r1, talk, mod, free, scale = call(
        functools.partial(setup_kernel, members),
        [shape(5, WINDOW, *plane), shape(5, Q1, R1, 128), shape(*window)]
        + down_outs
        + [shape(members, TALK, 128), shape(WINDOW, *plane), shape(WINDOW, *plane), shape(10, *plane)],
        [(24,) + plane] * 3 + down_scratch,
        (me, own, before, after, counts),
        1,
        "setup",
    )

    def up(first, r, talk, s2, s21, r1, coarse):
        s21_before, s21_after = both_ways(s21, s21)
        gathered = gather(talk)
        args = (me, gathered, r, s2, s21, s21_before, s21_after, r1, c0, c1) + tuple(coarse)
        outs = [shape(*block)]
        if first:
            outs += [shape(5, ND, R2, 128), shape(5, ND, R3, 128)]
        else:
            outs += [shape(8, 128)]
        scratch = [window, window, work, (ND, R2, 128)]
        return call(functools.partial(up_kernel, members, first), outs, scratch, args, 1, "up")

    u, c2, c3 = up(True, force, talk, s2, s21, r1, ())
    u_before, u_after = both_ways(u, u)
    u0, w0, s2, s21, r1, talk = call(
        first_kernel,
        [shape(*window), shape(*window)] + down_outs + [shape(members, R2, 128)],
        down_scratch,
        (u, u_before, u_after, force, c0, c1),
        name="first",
    )
    m, dots0 = up(False, w0, talk, s2, s21, r1, (c2, c3))
    m_before, m_after = both_ways(m, m)
    m0, u1, w1, n0, s2, s21, r1, talk = call(
        second_kernel,
        [shape(*window), shape(*window), shape(*window), shape(*block)] + down_outs + [shape(members, R2, 128)],
        down_scratch,
        (m, m_before, m_after, dots0, force, u0, w0, c0, c1),
        name="second",
    )
    m, dots1 = up(False, w1, talk, s2, s21, r1, (c2, c3))
    m_before, m_after = both_ways(m, m)
    u2, p1, x2, talk = call(
        third_kernel,
        [shape(*wide)] * 3 + [shape(members, 8, 128)],
        [window],
        (m, m_before, m_after, dots0, dots1, force, u0, w0, m0, n0, u1, w1, c0),
        name="third",
    )
    state, energy = call(
        last_kernel,
        [shape(*block), shape(10, *plane)],
        [wide],
        (gather(talk), dots0, dots1, u2, p1, x2, mod, free),
        name="last",
    )
    other = lax.ppermute(energy, "case", [(0, 1), (1, 0)])
    sensitivity = call(
        sensitivity_kernel,
        [shape(BLOCK, *plane)],
        [(10,) + plane] * 3,
        (energy, other, scale, passive),
        name="sensitivity",
    )[0]
    return state, sensitivity


def solution(mesh):
    placed = (
        P("space", None, None),
        P("space", None, None),
        P("space", None, None),
        P("case", None),
    )
    return jax.shard_map(
        on_device,
        mesh=mesh,
        in_specs=placed,
        out_specs=(P("case", "space", None, None), P("space", None, None)),
        check_vma=False,
    )
```

time: 1920 us -> 245 us (0.13)
  blocking collectives: 762 us -> 26.4 us
  waiting for transfers between devices: 442 us -> 31.2 us
  starting transfers between devices: 407 us -> 91.7 us
  other arithmetic: 142 us -> 1.97 us
  local copies, waits for them, and re-layouts: 135 us -> 38.4 us
  Pallas kernels: 0 us -> 52.9 us
    psum x5 -> x0, blocking collectives: 762 us -> none  [the longest x3 473 us: inner_product(): return lax.psum(jnp.sum(first_arg * second_arg, axis=(1, 2, 3)), 'space')]
    ppermute x134 -> x15, starting transfers between devices: 407 us -> 48.9 us  [the longest x7 29.2 us: both_ways(): lax.ppermute(to_next, 'space', ahead)]
    psum x1 -> x0, waiting for transfers between devices: 245 us -> none  [on_device(): energy = lax.psum(local_energy, 'case')]
    ppermute x134 -> x15, waiting for transfers between devices: 197 us -> 19.6 us  [the longest x7 10.5 us: both_ways(): lax.ppermute(to_previous, 'space', back)]
    reshape x21 -> x0, local copies, waits for them, and re-layouts: 118 us -> none  [the longest x9 106 us: children(): values.reshape(leading + (depth_z // 2, 2, rows_y // 2, 2, cols_x // 2, 2))]
    unnamed x5 -> x0, other arithmetic: 58.6 us -> none
    pallas_call x0 -> x10, Pallas kernels: none -> 52.9 us  [call(): pl.pallas_call(body, out_shape=outs, in_specs=specs, out_specs=[vmem] * l...]
    all_to_all x0 -> x3, starting transfers between devices: none -> 42.7 us  [gather(): return lax.all_to_all(tiles, 'space', 0, 0)]
  transfers between devices with their start and end apart: 135 -> 18, of which waited for: 63 -> 16; matrix products, arithmetic and copies ran while one was open for 5% -> 0% of each run, Pallas kernels for 0% -> 3%
where the time goes in v1:
time: 245 us; the launch traced here: 244 us
  starting transfers between devices  91.7 us (37%)
  Pallas kernels  52.9 us (22%)
  local copies, waits for them, and re-layouts  38.4 us (16%)
  waiting for transfers between devices  31.2 us (13%)
  blocking collectives  26.4 us (11%)
    pallas_call x10, Pallas kernels, call(): pl.pallas_call(body, out_shape=outs, in_specs=specs, out_specs=[vmem] * l...  52.9 us
    all_to_all x3, starting transfers between devices, gather(): return lax.all_to_all(tiles, 'space', 0, 0)  42.7 us
    unnamed x118, local copies, waits for them, and re-layouts  38.4 us
    ppermute x7, starting transfers between devices, both_ways(): lax.ppermute(to_next, 'space', ahead)  29.2 us
    all_to_all x1, blocking collectives, gather(): return lax.all_to_all(tiles, 'space', 0, 0)  26.4 us
    all_to_all x3, waiting for transfers between devices, gather(): return lax.all_to_all(tiles, 'space', 0, 0)  11.6 us
    ppermute x1, starting transfers between devices, on_device(): other = lax.ppermute(energy, 'case', [(0, 1), (1, 0)])  10.7 us
    ppermute x7, waiting for transfers between devices, both_ways(): lax.ppermute(to_previous, 'space', back)  10.5 us
  transfers between devices with their start and end apart: 18, of which 16 were waited for; matrix products, arithmetic and copies ran while one was open for 0% of the time, Pallas kernels for 3%

profile of v1, /device:TPU:1, one launch (start us, length us, event | category | flops | bytes accessed | tf_op | source)
XLA Modules:
  0.0 243.6 jit_solution(10924614514545569158)
XLA Ops:
  3.9 5.0 %collective-permute-start = (f32[3,8,40,128]{3,2,1,0:T(8,128)S(1)}, f32[3,8,40,128]{3,2,1,0:T(8,128)S(1)}, u32[]{:S(2)}, u32[]{:S(2)}) collective-permute-start(f32[3,8,40,128]{3,2,1,0:T(8,128)S(1)} %pad_maximum_fusion.own), channel_id=1, source_target_pairs={{0,1},{1,2},{2,3},{3,4},{4,5},{5,6},{6,7},{7,8},{8,9},{9,10},{10,1... | collective-permute-start | bytes 1474568 | tf_op jit(solution)/shard_map/ppermute | solution.py:709
  9.7 6.6 %counts.1 = f32[2,22,40,128]{3,2,1,0:T(8,128)S(1)} custom-call(s32[1]{0:T(128)} %bitcast.me.me_ref, s32[2,4096]{1,0:T(2,128)S(1)} %copy-done.58), custom_call_target="tpu_custom_call" | custom-call | tf_op jit(solution)/shard_map/counts/pallas_call | solution.py:690
  16.3 1.6 collective-permute-done.1.after
  21.6 9.5 %setup.1 = (f32[5,22,40,128]{3,2,1,0:T(8,128)S(1)}, f32[5,10,24,128]{3,2,1,0:T(8,128)S(1)}, f32[2,22,40,128]{3,2,1,0:T(8,128)S(1)}, f32[2,12,40,128]{3,2,1,0:T(8...) custom-call(s32[1]{0:T(128)} %bitcast.me.me_ref, ...), custom_call_target="tpu_custom_call" | custom-call | tf_op jit(solution)/shard_map/setup/pallas_call | solution.py:690
  35.9 15.9 %all-to-all-start = ((f32[64,24,128]{2,1,0:T(8,128)}), f32[64,24,128]{2,1,0:T(8,128)}, u32[]{:S(2)}, u32[]{:S(2)}) async-start(f32[64,24,128]{2,1,0:T(8,128)} %copy-done.24), calls=%async_computation | async-start | bytes 1572864 | tf_op jit(solution)/shard_map/all_to_all | solution.py:712
  53.1 4.0 %collective-permute-start.2 = (f32[4,24,128]{2,1,0:T(8,128)S(1)}, f32[4,24,128]{2,1,0:T(8,128)S(1)}, u32[]{:S(2)}, u32[]{:S(2)}) collective-permute-start(f32[4,24,128]{2,1,0:T(8,128)S(1)} %get-tuple-element.42.s21), channel_id=1, source_target_pairs={{0,1},{1,2},{2,3},{3,4},{4,5},{5,6},{6,7},{7,8},{8,9},{9,10},{10,1... | collective-permute-start | bytes 147464 | tf_op jit(solution)/shard_map/ppermute | solution.py:709
  58.3 1.8 collective-permute-done.2.s21_before
  60.1 5.3 %all-to-all-done.gathered = f32[64,24,128]{2,1,0:T(8,128)} async-done(((f32[64,24,128]{2,1,0:T(8,128)}), f32[64,24,128]{2,1,0:T(8,128)}, u32[]{:S(2)}, u32[]{:S(2)}) %all-to-all-start) | async-done | bytes 786464 | tf_op jit(solution)/shard_map/all_to_all | solution.py:712
  67.6 6.7 %up.3 = (f32[2,8,40,128]{3,2,1,0:T(8,128)S(1)}, f32[5,23,16,128]{3,2,1,0:T(8,128)S(1)}, f32[5,23,8,128]{3,2,1,0:T(8,128)S(1)}) custom-call(s32[1]{0:T(128)} %bitcast.me.me_ref, f32[64,24,128]{2,1,0:T(8,128)} %all-to-all-done.gathered, f32[2,22,40,128]{3,2,1,0:T(8,128)S(1)} %copy-done.1, f32[2,12,40,128]{3,2,1,0:T(8,128)S(1)} %copy-done.37, ...), custom_call_target="tpu_custom_call" | custom-call | tf_op jit(solution)/shard_map/up/pallas_call | solution.py:690
  76.5 4.0 %collective-permute-start.4 = (f32[2,8,40,128]{3,2,1,0:T(8,128)S(1)}, f32[2,8,40,128]{3,2,1,0:T(8,128)S(1)}, u32[]{:S(2)}, u32[]{:S(2)}) collective-permute-start(f32[2,8,40,128]{3,2,1,0:T(8,128)S(1)} %get-tuple-element.46.own), channel_id=1, source_target_pairs={{0,1},{1,2},{2,3},{3,4},{4,5},{5,6},{6,7},{7,8},{8,9},{9,10},{10,1... | collective-permute-start | bytes 983048 | tf_op jit(solution)/shard_map/ppermute | solution.py:709
  80.6 2.5 %collective-permute-done.5.after = f32[2,8,40,128]{3,2,1,0:T(8,128)S(1)} collective-permute-done((f32[2,8,40,128]{3,2,1,0:T(8,128)S(1)}, f32[2,8,40,128]{3,2,1,0:T(8,128)S(1)}, u32[]{:S(2)}, u32[]{:S(2)}) %collective-permute-start.5) | collective-permute-done | bytes 327712 | tf_op jit(solution)/shard_map/ppermute | solution.py:709
  83.1 1.5 collective-permute-done.4.before
  84.5 6.3 %first.1 = (f32[2,22,40,128]{3,2,1,0:T(8,128)S(1)}, f32[2,22,40,128]{3,2,1,0:T(8,128)S(1)}, f32[2,12,40,128]{3,2,1,0:T(8,128)S(1)}, f32[4,24,128]{2,1,0:T(8,128)...) custom-call(f32[2,8,40,128]{3,2,1,0:T(8,128)S(1)} %get-tuple-element.46.own, ...), custom_call_target="tpu_custom_call" | custom-call | tf_op jit(solution)/shard_map/first/pallas_call | solution.py:690
  95.0 11.4 %all-to-all-start.1 = ((f32[64,16,128]{2,1,0:T(8,128)}), f32[64,16,128]{2,1,0:T(8,128)S(1)}, u32[]{:S(2)}, u32[]{:S(2)}) async-start(f32[64,16,128]{2,1,0:T(8,128)} %copy-done.27), calls=%async_computation.1 | async-start | bytes 1048576 | tf_op jit(solution)/shard_map/all_to_all | solution.py:712
  107.7 4.2 %collective-permute-start.6 = (f32[4,24,128]{2,1,0:T(8,128)}, f32[4,24,128]{2,1,0:T(8,128)S(1)}, u32[]{:S(2)}, u32[]{:S(2)}) collective-permute-start(f32[4,24,128]{2,1,0:T(8,128)} %copy-done.48), channel_id=1, source_target_pairs={{0,1},{1,2},{2,3},{3,4},{4,5},{5,6},{6,7},{7,8},{8,9},{9,10},{10,1... | collective-permute-start | bytes 147464 | tf_op jit(solution)/shard_map/ppermute | solution.py:709
  114.1 3.0 %all-to-all-done.1.gathered = f32[64,16,128]{2,1,0:T(8,128)S(1)} async-done(((f32[64,16,128]{2,1,0:T(8,128)}), f32[64,16,128]{2,1,0:T(8,128)S(1)}, u32[]{:S(2)}, u32[]{:S(2)}) %all-to-all-start.1) | async-done | bytes 524320 | tf_op jit(solution)/shard_map/all_to_all | solution.py:712
  123.9 4.8 %up.4 = (f32[2,8,40,128]{3,2,1,0:T(8,128)S(1)}, f32[8,128]{1,0:T(8,128)S(1)}) custom-call(s32[1]{0:T(128)} %bitcast.me.me_ref, f32[64,16,128]{2,1,0:T(8,128)S(1)} %all-to-all-done.1.gathered, f32[2,22,40,128]{3,2,1,0:T(8,128)S(1)} %copy-done.5, f32[2,12,40,128]{3,2,1,0:T(8,128)S(1)} %copy-done.31, f32[4,24,128]{2,1,0:T(8,128)S(1)} %copy-done.49, ...), custom_call_target="tpu_custom_call" | custom-call | tf_op jit(solution)/shard_map/up/pallas_call | solution.py:690
  130.1 4.0 %collective-permute-start.8 = (f32[2,8,40,128]{3,2,1,0:T(8,128)S(1)}, f32[2,8,40,128]{3,2,1,0:T(8,128)S(1)}, u32[]{:S(2)}, u32[]{:S(2)}) collective-permute-start(f32[2,8,40,128]{3,2,1,0:T(8,128)S(1)} %get-tuple-element.54.own), channel_id=1, source_target_pairs={{0,1},{1,2},{2,3},{3,4},{4,5},{5,6},{6,7},{7,8},{8,9},{9,10},{10,1... | collective-permute-start | bytes 983048 | tf_op jit(solution)/shard_map/ppermute | solution.py:709
  134.1 2.5 %collective-permute-done.9.after = f32[2,8,40,128]{3,2,1,0:T(8,128)S(1)} collective-permute-done((f32[2,8,40,128]{3,2,1,0:T(8,128)S(1)}, f32[2,8,40,128]{3,2,1,0:T(8,128)S(1)}, u32[]{:S(2)}, u32[]{:S(2)}) %collective-permute-start.9) | collective-permute-done | bytes 327712 | tf_op jit(solution)/shard_map/ppermute | solution.py:709
  136.6 1.5 collective-permute-done.8.before
  138.1 8.3 %second.1 = (f32[2,22,40,128]{3,2,1,0:T(8,128)S(1)}, f32[2,22,40,128]{3,2,1,0:T(8,128)S(1)}, f32[2,22,40,128]{3,2,1,0:T(8,128)S(1)}, f32[2,8,40,128]{3,2,1,0:T(8...) custom-call(f32[2,8,40,128]{3,2,1,0:T(8,128)S(1)} %get-tuple-element, ...), custom_call_target="tpu_custom_call" | custom-call | tf_op jit(solution)/shard_map/second/pallas_call | solution.py:690
  152.2 15.4 %all-to-all-start.2 = ((f32[64,16,128]{2,1,0:T(8,128)}), f32[64,16,128]{2,1,0:T(8,128)S(1)}, u32[]{:S(2)}, u32[]{:S(2)}) async-start(f32[64,16,128]{2,1,0:T(8,128)} %copy-done.26), calls=%async_computation.2 | async-start | bytes 1048576 | tf_op jit(solution)/shard_map/all_to_all | solution.py:712
  169.0 4.0 %collective-permute-start.10 = (f32[4,24,128]{2,1,0:T(8,128)}, f32[4,24,128]{2,1,0:T(8,128)S(1)}, u32[]{:S(2)}, u32[]{:S(2)}) collective-permute-start(f32[4,24,128]{2,1,0:T(8,128)} %copy-done.46), channel_id=1, source_target_pairs={{0,1},{1,2},{2,3},{3,4},{4,5},{5,6},{6,7},{7,8},{8,9},{9,10},{10,1... | collective-permute-start | bytes 147464 | tf_op jit(solution)/shard_map/ppermute | solution.py:709
  175.1 3.3 %all-to-all-done.2.gathered = f32[64,16,128]{2,1,0:T(8,128)S(1)} async-done(((f32[64,16,128]{2,1,0:T(8,128)}), f32[64,16,128]{2,1,0:T(8,128)S(1)}, u32[]{:S(2)}, u32[]{:S(2)}) %all-to-all-start.2) | async-done | bytes 524320 | tf_op jit(solution)/shard_map/all_to_all | solution.py:712
  185.2 4.9 %up.5 = (f32[2,8,40,128]{3,2,1,0:T(8,128)S(1)}, f32[8,128]{1,0:T(8,128)S(1)}) custom-call(s32[1]{0:T(128)} %bitcast.me.me_ref, f32[64,16,128]{2,1,0:T(8,128)S(1)} %all-to-all-done.2.gathered, f32[2,22,40,128]{3,2,1,0:T(8,128)S(1)} %copy-done.15, f32[2,12,40,128]{3,2,1,0:T(8,128)S(1)} %copy-done.29, f32[4,24,128]{2,1,0:T(8,128)S(1)} %copy-done.47, ...), custom_call_target="tpu_custom_call" | custom-call | tf_op jit(solution)/shard_map/up/pallas_call | solution.py:690
  191.4 4.0 %collective-permute-start.12 = (f32[2,8,40,128]{3,2,1,0:T(8,128)S(1)}, f32[2,8,40,128]{3,2,1,0:T(8,128)S(1)}, u32[]{:S(2)}, u32[]{:S(2)}) collective-permute-start(f32[2,8,40,128]{3,2,1,0:T(8,128)S(1)} %get-tuple-element.62.own), channel_id=1, source_target_pairs={{0,1},{1,2},{2,3},{3,4},{4,5},{5,6},{6,7},{7,8},{8,9},{9,10},{10,1... | collective-permute-start | bytes 983048 | tf_op jit(solution)/shard_map/ppermute | solution.py:709
  195.4 2.5 %collective-permute-done.13.after = f32[2,8,40,128]{3,2,1,0:T(8,128)S(1)} collective-permute-done((f32[2,8,40,128]{3,2,1,0:T(8,128)S(1)}, f32[2,8,40,128]{3,2,1,0:T(8,128)S(1)}, u32[]{:S(2)}, u32[]{:S(2)}) %collective-permute-start.13) | collective-permute-done | bytes 327712 | tf_op jit(solution)/shard_map/ppermute | solution.py:709
  197.9 1.5 collective-permute-done.12.before
  199.5 2.3 third.1
  201.8 26.4 %all_to_all.20.gathered = f32[64,8,128]{2,1,0:T(8,128)S(1)} all-to-all(f32[64,8,128]{2,1,0:T(8,128)S(1)} %get-tuple-element.67), channel_id=1, replica_groups=mesh['case'=2,'space'=64] {'space'}, dimensions={0} | all-to-all | bytes 524288 | tf_op jit(solution)/shard_map/all_to_all | solution.py:712
  228.2 2.3 last.1
  230.5 10.7 %collective-permute-start.14 = (f32[10,40,128]{2,1,0:T(8,128)S(1)}, f32[10,40,128]{2,1,0:T(8,128)S(1)}, u32[]{:S(2)}, u32[]{:S(2)}) collective-permute-start(f32[10,40,128]{2,1,0:T(8,128)S(1)} %get-tuple-element.74.mine), channel_id=1, source_target_pairs={{0,64},{64,0},{1,65},{65,1},{2,66},{66,2},{3,67},{67,3},{4,68},{68... | collective-permute-start | bytes 614408 | tf_op jit(solution)/shard_map/ppermute | solution.py:784
  (135 shorter events, 55.0 us)
Async XLA Ops:
  2.6 15.3 %collective-permute-start.1 = (f32[3,8,40,128]{3,2,1,0:T(8,128)S(1)}, f32[3,8,40,128]{3,2,1,0:T(8,128)S(1)}, u32[]{:S(2)}, u32[]{:S(2)}) collective-permute-start(f32[3,8,40,128]{3,2,1,0:T(8,128)S(1)} %pad_maximum_fusion.own), channel_id=1, source_target_pairs={{1,0},{2,1},{3,2},{4,3},{5,4},{6,5},{7,6},{8,7},{9,8},{10,9},{11,1... | collective-permute-start | bytes 1474568 | tf_op jit(solution)/shard_map/ppermute | solution.py:709
  3.9 14.9 %collective-permute-start = (f32[3,8,40,128]{3,2,1,0:T(8,128)S(1)}, f32[3,8,40,128]{3,2,1,0:T(8,128)S(1)}, u32[]{:S(2)}, u32[]{:S(2)}) collective-permute-start(f32[3,8,40,128]{3,2,1,0:T(8,128)S(1)} %pad_maximum_fusion.own), channel_id=1, source_target_pairs={{0,1},{1,2},{2,3},{3,4},{4,5},{5,6},{6,7},{7,8},{8,9},{9,10},{10,1... | collective-permute-start | bytes 1474568 | tf_op jit(solution)/shard_map/ppermute | solution.py:709
  35.9 29.5 %all-to-all-start = ((f32[64,24,128]{2,1,0:T(8,128)}), f32[64,24,128]{2,1,0:T(8,128)}, u32[]{:S(2)}, u32[]{:S(2)}) async-start(f32[64,24,128]{2,1,0:T(8,128)} %copy-done.24), calls=%async_computation | async-start | bytes 1572864 | tf_op jit(solution)/shard_map/all_to_all | solution.py:712
  51.8 6.6 %collective-permute-start.3 = (f32[4,24,128]{2,1,0:T(8,128)S(1)}, f32[4,24,128]{2,1,0:T(8,128)S(1)}, u32[]{:S(2)}, u32[]{:S(2)}) collective-permute-start(f32[4,24,128]{2,1,0:T(8,128)S(1)} %get-tuple-element.42.s21), channel_id=1, source_target_pairs={{1,0},{2,1},{3,2},{4,3},{5,4},{6,5},{7,6},{8,7},{9,8},{10,9},{11,1... | collective-permute-start | bytes 147464 | tf_op jit(solution)/shard_map/ppermute | solution.py:709
  53.1 7.0 %collective-permute-start.2 = (f32[4,24,128]{2,1,0:T(8,128)S(1)}, f32[4,24,128]{2,1,0:T(8,128)S(1)}, u32[]{:S(2)}, u32[]{:S(2)}) collective-permute-start(f32[4,24,128]{2,1,0:T(8,128)S(1)} %get-tuple-element.42.s21), channel_id=1, source_target_pairs={{0,1},{1,2},{2,3},{3,4},{4,5},{5,6},{6,7},{7,8},{8,9},{9,10},{10,1... | collective-permute-start | bytes 147464 | tf_op jit(solution)/shard_map/ppermute | solution.py:709
  75.3 15.6 %copy-start.17 = (f32[5,23,8,128]{3,2,1,0:T(8,128)}, f32[5,23,8,128]{3,2,1,0:T(8,128)S(1)}, u32[]{:S(2)}) copy-start(f32[5,23,8,128]{3,2,1,0:T(8,128)S(1)} %get-tuple-element.53.rest_1_) | copy-start | bytes 1413124
  75.3 7.8 %collective-permute-start.5 = (f32[2,8,40,128]{3,2,1,0:T(8,128)S(1)}, f32[2,8,40,128]{3,2,1,0:T(8,128)S(1)}, u32[]{:S(2)}, u32[]{:S(2)}) collective-permute-start(f32[2,8,40,128]{3,2,1,0:T(8,128)S(1)} %get-tuple-element.46.own), channel_id=1, source_target_pairs={{1,0},{2,1},{3,2},{4,3},{5,4},{6,5},{7,6},{8,7},{9,8},{10,9},{11,1... | collective-permute-start | bytes 983048 | tf_op jit(solution)/shard_map/ppermute | solution.py:709
  76.5 8.0 %collective-permute-start.4 = (f32[2,8,40,128]{3,2,1,0:T(8,128)S(1)}, f32[2,8,40,128]{3,2,1,0:T(8,128)S(1)}, u32[]{:S(2)}, u32[]{:S(2)}) collective-permute-start(f32[2,8,40,128]{3,2,1,0:T(8,128)S(1)} %get-tuple-element.46.own), channel_id=1, source_target_pairs={{0,1},{1,2},{2,3},{3,4},{4,5},{5,6},{6,7},{7,8},{8,9},{9,10},{10,1... | collective-permute-start | bytes 983048 | tf_op jit(solution)/shard_map/ppermute | solution.py:709
  95.0 22.2 %all-to-all-start.1 = ((f32[64,16,128]{2,1,0:T(8,128)}), f32[64,16,128]{2,1,0:T(8,128)S(1)}, u32[]{:S(2)}, u32[]{:S(2)}) async-start(f32[64,16,128]{2,1,0:T(8,128)} %copy-done.27), calls=%async_computation.1 | async-start | bytes 1048576 | tf_op jit(solution)/shard_map/all_to_all | solution.py:712
  106.4 5.5 %collective-permute-start.7 = (f32[4,24,128]{2,1,0:T(8,128)}, f32[4,24,128]{2,1,0:T(8,128)S(1)}, u32[]{:S(2)}, u32[]{:S(2)}) collective-permute-start(f32[4,24,128]{2,1,0:T(8,128)} %copy-done.48), channel_id=1, source_target_pairs={{1,0},{2,1},{3,2},{4,3},{5,4},{6,5},{7,6},{8,7},{9,8},{10,9},{11,1... | collective-permute-start | bytes 147464 | tf_op jit(solution)/shard_map/ppermute | solution.py:709
  107.7 5.8 %collective-permute-start.6 = (f32[4,24,128]{2,1,0:T(8,128)}, f32[4,24,128]{2,1,0:T(8,128)S(1)}, u32[]{:S(2)}, u32[]{:S(2)}) collective-permute-start(f32[4,24,128]{2,1,0:T(8,128)} %copy-done.48), channel_id=1, source_target_pairs={{0,1},{1,2},{2,3},{3,4},{4,5},{5,6},{6,7},{7,8},{8,9},{9,10},{10,1... | collective-permute-start | bytes 147464 | tf_op jit(solution)/shard_map/ppermute | solution.py:709
  123.9 14.2 %copy-start.6 = (f32[2,22,40,128]{3,2,1,0:T(8,128)S(1)}, f32[2,22,40,128]{3,2,1,0:T(8,128)}, u32[]{:S(2)}) copy-start(f32[2,22,40,128]{3,2,1,0:T(8,128)} %copy-done.4) | copy-start | bytes 2703364
  123.9 14.2 %copy-start.12 = (f32[2,22,40,128]{3,2,1,0:T(8,128)S(1)}, f32[2,22,40,128]{3,2,1,0:T(8,128)}, u32[]{:S(2)}) copy-start(f32[2,22,40,128]{3,2,1,0:T(8,128)} %copy-done.11) | copy-start | bytes 2703364
  128.8 7.8 %collective-permute-start.9 = (f32[2,8,40,128]{3,2,1,0:T(8,128)S(1)}, f32[2,8,40,128]{3,2,1,0:T(8,128)S(1)}, u32[]{:S(2)}, u32[]{:S(2)}) collective-permute-start(f32[2,8,40,128]{3,2,1,0:T(8,128)S(1)} %get-tuple-element.54.own), channel_id=1, source_target_pairs={{1,0},{2,1},{3,2},{4,3},{5,4},{6,5},{7,6},{8,7},{9,8},{10,9},{11,1... | collective-permute-start | bytes 983048 | tf_op jit(solution)/shard_map/ppermute | solution.py:709
  130.1 8.0 %collective-permute-start.8 = (f32[2,8,40,128]{3,2,1,0:T(8,128)S(1)}, f32[2,8,40,128]{3,2,1,0:T(8,128)S(1)}, u32[]{:S(2)}, u32[]{:S(2)}) collective-permute-start(f32[2,8,40,128]{3,2,1,0:T(8,128)S(1)} %get-tuple-element.54.own), channel_id=1, source_target_pairs={{0,1},{1,2},{2,3},{3,4},{4,5},{5,6},{6,7},{7,8},{8,9},{9,10},{10,1... | collective-permute-start | bytes 983048 | tf_op jit(solution)/shard_map/ppermute | solution.py:709
  152.2 26.2 %all-to-all-start.2 = ((f32[64,16,128]{2,1,0:T(8,128)}), f32[64,16,128]{2,1,0:T(8,128)S(1)}, u32[]{:S(2)}, u32[]{:S(2)}) async-start(f32[64,16,128]{2,1,0:T(8,128)} %copy-done.26), calls=%async_computation.2 | async-start | bytes 1048576 | tf_op jit(solution)/shard_map/all_to_all | solution.py:712
  167.7 5.5 %collective-permute-start.11 = (f32[4,24,128]{2,1,0:T(8,128)}, f32[4,24,128]{2,1,0:T(8,128)S(1)}, u32[]{:S(2)}, u32[]{:S(2)}) collective-permute-start(f32[4,24,128]{2,1,0:T(8,128)} %copy-done.46), channel_id=1, source_target_pairs={{1,0},{2,1},{3,2},{4,3},{5,4},{6,5},{7,6},{8,7},{9,8},{10,9},{11,1... | collective-permute-start | bytes 147464 | tf_op jit(solution)/shard_map/ppermute | solution.py:709
  169.0 5.5 %collective-permute-start.10 = (f32[4,24,128]{2,1,0:T(8,128)}, f32[4,24,128]{2,1,0:T(8,128)S(1)}, u32[]{:S(2)}, u32[]{:S(2)}) collective-permute-start(f32[4,24,128]{2,1,0:T(8,128)} %copy-done.46), channel_id=1, source_target_pairs={{0,1},{1,2},{2,3},{3,4},{4,5},{5,6},{6,7},{7,8},{8,9},{9,10},{10,1... | collective-permute-start | bytes 147464 | tf_op jit(solution)/shard_map/ppermute | solution.py:709
  185.2 14.2 %copy-start.3 = (f32[2,22,40,128]{3,2,1,0:T(8,128)S(1)}, f32[2,22,40,128]{3,2,1,0:T(8,128)}, u32[]{:S(2)}) copy-start(f32[2,22,40,128]{3,2,1,0:T(8,128)} %copy-done) | copy-start | bytes 2703364
  185.2 14.2 %copy-start.7 = (f32[2,22,40,128]{3,2,1,0:T(8,128)S(1)}, f32[2,22,40,128]{3,2,1,0:T(8,128)}, u32[]{:S(2)}) copy-start(f32[2,22,40,128]{3,2,1,0:T(8,128)} %copy-done.4) | copy-start | bytes 2703364
  185.2 14.2 %copy-start.13 = (f32[2,22,40,128]{3,2,1,0:T(8,128)S(1)}, f32[2,22,40,128]{3,2,1,0:T(8,128)}, u32[]{:S(2)}) copy-start(f32[2,22,40,128]{3,2,1,0:T(8,128)} %copy-done.11) | copy-start | bytes 2703364
  185.2 14.2 %copy-start.16 = (f32[2,22,40,128]{3,2,1,0:T(8,128)S(1)}, f32[2,22,40,128]{3,2,1,0:T(8,128)}, u32[]{:S(2)}) copy-start(f32[2,22,40,128]{3,2,1,0:T(8,128)} %copy-done.14) | copy-start | bytes 2703364
  185.2 14.2 %copy-start.21 = (f32[2,22,40,128]{3,2,1,0:T(8,128)S(1)}, f32[2,22,40,128]{3,2,1,0:T(8,128)}, u32[]{:S(2)}) copy-start(f32[2,22,40,128]{3,2,1,0:T(8,128)} %copy-done.20) | copy-start | bytes 2703364
  185.2 14.2 %copy-start.23 = (f32[2,22,40,128]{3,2,1,0:T(8,128)S(1)}, f32[2,22,40,128]{3,2,1,0:T(8,128)}, u32[]{:S(2)}) copy-start(f32[2,22,40,128]{3,2,1,0:T(8,128)} %copy-done.22) | copy-start | bytes 2703364
  185.2 14.2 %copy-start.43 = (f32[2,8,40,128]{3,2,1,0:T(8,128)S(1)}, f32[2,8,40,128]{3,2,1,0:T(8,128)}, u32[]{:S(2)}) copy-start(f32[2,8,40,128]{3,2,1,0:T(8,128)} %copy-done.42) | copy-start | bytes 983044
  190.1 7.8 %collective-permute-start.13 = (f32[2,8,40,128]{3,2,1,0:T(8,128)S(1)}, f32[2,8,40,128]{3,2,1,0:T(8,128)S(1)}, u32[]{:S(2)}, u32[]{:S(2)}) collective-permute-start(f32[2,8,40,128]{3,2,1,0:T(8,128)S(1)} %get-tuple-element.62.own), channel_id=1, source_target_pairs={{1,0},{2,1},{3,2},{4,3},{5,4},{6,5},{7,6},{8,7},{9,8},{10,9},{11,1... | collective-permute-start | bytes 983048 | tf_op jit(solution)/shard_map/ppermute | solution.py:709
  191.4 8.0 %collective-permute-start.12 = (f32[2,8,40,128]{3,2,1,0:T(8,128)S(1)}, f32[2,8,40,128]{3,2,1,0:T(8,128)S(1)}, u32[]{:S(2)}, u32[]{:S(2)}) collective-permute-start(f32[2,8,40,128]{3,2,1,0:T(8,128)S(1)} %get-tuple-element.62.own), channel_id=1, source_target_pairs={{0,1},{1,2},{2,3},{3,4},{4,5},{5,6},{6,7},{7,8},{8,9},{9,10},{10,1... | collective-permute-start | bytes 983048 | tf_op jit(solution)/shard_map/ppermute | solution.py:709
  199.4 28.7 %copy-start.39 = (f32[22,40,128]{2,1,0:T(8,128)S(1)}, f32[22,40,128]{2,1,0:T(8,128)}, u32[]{:S(2)}) copy-start(f32[22,40,128]{2,1,0:T(8,128)} %copy-done.38) | copy-start | bytes 1351684
  199.5 28.7 %copy-start.41 = (f32[22,40,128]{2,1,0:T(8,128)S(1)}, f32[22,40,128]{2,1,0:T(8,128)}, u32[]{:S(2)}) copy-start(f32[22,40,128]{2,1,0:T(8,128)} %copy-done.40) | copy-start | bytes 1351684
  201.8 40.5 %copy-start.25 = (s32[8,40,128]{2,1,0:T(8,128)S(1)}, s32[8,40,128]{2,1,0:T(8,128)}, u32[]{:S(2)}) copy-start(s32[8,40,128]{2,1,0:T(8,128)} %passive.1) | copy-start | bytes 491524
  201.8 40.5 %copy-start.45 = (f32[10,40,128]{2,1,0:T(8,128)S(1)}, f32[10,40,128]{2,1,0:T(8,128)}, u32[]{:S(2)}) copy-start(f32[10,40,128]{2,1,0:T(8,128)} %copy-done.44) | copy-start | bytes 614404
  230.5 11.8 %collective-permute-start.14 = (f32[10,40,128]{2,1,0:T(8,128)S(1)}, f32[10,40,128]{2,1,0:T(8,128)S(1)}, u32[]{:S(2)}, u32[]{:S(2)}) collective-permute-start(f32[10,40,128]{2,1,0:T(8,128)S(1)} %get-tuple-element.74.mine), channel_id=1, source_target_pairs={{0,64},{64,0},{1,65},{65,1},{2,66},{66,2},{3,67},{67,3},{4,68},{68... | collective-permute-start | bytes 614408 | tf_op jit(solution)/shard_map/ppermute | solution.py:784
  (45 other events, 52.5 us)

commit v2 on v1

v2 whole, which is shorter than its diff:
```python
import functools

import jax
import jax.numpy as jnp
from jax import lax
from jax.experimental import pallas as pl
from jax.experimental.pallas import tpu as pltpu
from jax.sharding import PartitionSpec as P

ITERS = 3
E_MIN = 0.01
OMEGA = 0.8
HEAT_SOURCE = 0.05
EDGE_WEIGHT = 1.5 - 2.0**0.5

F32 = jnp.float32
NY, NX = 40, 128
BLOCK = 8
HALO = 13
NEXT = HALO - BLOCK
WINDOW = BLOCK + 2 * HALO
Q1, R1 = 16, 24
QB = 6
REACH = 11
ND = 2 * REACH + 1
R2 = 16
R3 = 8
TALK = 24
CPARAMS = pltpu.CompilerParams(vmem_limit_bytes=32 * 1024 * 1024)


def iota(shape, dim):
    return lax.broadcasted_iota(jnp.int32, shape, dim)


def roll(v, by, dim):
    return pltpu.roll(v, by % v.shape[dim], dim)


def dot(a, b):
    return lax.dot_general(
        a, b, (((1,), (0,)), ((), ())), precision=lax.Precision.HIGHEST, preferred_element_type=F32
    )


def planes(lo, hi, body, group=8):
    def do(js):
        writes = [w for j in js for w in body(j)]
        for ref, index, value in writes:
            ref[index] = value

    count = (hi - lo) // group
    if count == 1:
        do([lo + k for k in range(group)])
    elif count > 1:

        def step(i, carry):
            do([lo + i * group + k for k in range(group)])
            return carry

        lax.fori_loop(0, count, step, 0)
    if lo + count * group < hi:
        do(list(range(lo + count * group, hi)))


def fine_to_half(case):
    i, j = iota((128, 128), 0), iota((128, 128), 1)
    return (j == 64 * case + (i >> 1)).astype(F32)


def half_to_fine(case):
    i, j = iota((128, 128), 0), iota((128, 128), 1)
    return (i == 64 * case + (j >> 1)).astype(F32)


def half_to_quarter(low):
    i, j = iota((128, 128), 0), iota((128, 128), 1)
    return (j == 64 * low + 32 * (i >> 6) + ((i & 63) >> 1)).astype(F32)


def quarter_to_half(low):
    i, j = iota((128, 128), 0), iota((128, 128), 1)
    return (i == 64 * low + 32 * (j >> 6) + ((j & 63) >> 1)).astype(F32)


def quarter_to_eighth():
    i, j = iota((128, 128), 0), iota((128, 128), 1)
    return (j == 16 * ((i >> 5) & 1) + ((i & 31) >> 1)).astype(F32)


def eighth_to_quarter():
    i, j = iota((128, 128), 0), iota((128, 128), 1)
    return (i == 16 * ((j >> 5) & 1) + ((j & 31) >> 1)).astype(F32)


def z_prev(v):
    return jnp.concatenate([jnp.zeros_like(v[:1]), v[:-1]], axis=0)


def z_next(v):
    return jnp.concatenate([v[1:], jnp.zeros_like(v[:1])], axis=0)


def z_prev2(v):
    turned = roll(v, 64, 2)
    return jnp.where(iota(v.shape, 2) >= 64, turned, z_prev(turned))


def z_next2(v):
    turned = roll(v, 64, 2)
    return jnp.where(iota(v.shape, 2) < 64, turned, z_next(turned))


def couple(m, f, factor, width, zp, zn):
    lead = (iota(m.shape, 2) & (width - 1)) > 0
    first = iota(m.shape, 1) > 0
    sides = (
        (lambda v: roll(v, 1, 2), lambda v: roll(v, -1, 2), lead),
        (lambda v: roll(v, 1, 1), lambda v: roll(v, -1, 1), first),
        (zp, zn, None),
    )
    total = jnp.zeros_like(m)
    held = jnp.zeros_like(m)
    coupling = []
    for prev, after, mask in sides:
        k = jnp.sqrt(m * prev(m))
        if mask is not None:
            k = jnp.where(mask, k, 0.0)
        ka = after(k)
        total = total + k + ka
        held = held + k * (1.0 - prev(f)) + ka * (1.0 - after(f))
        inner = factor * k * f * prev(f)
        coupling += [inner, after(inner)]
    rest = f * factor * held + (1.0 - f)
    weight = OMEGA / (f * factor * total + (1.0 - f))
    return tuple(coupling) + (rest, weight)


COUNT = 8
REST, WEIGHT = 6, 7


def apply(v, c, zp, zn):
    out = c[REST] * v + c[0] * (v - roll(v, 1, 2)) + c[1] * (v - roll(v, -1, 2))
    out = out + c[2] * (v - roll(v, 1, 1)) + c[3] * (v - roll(v, -1, 1))
    return out + c[4] * (v - zp(v)) + c[5] * (v - zn(v))


def cut(c, lo, hi):
    return tuple(x[lo:hi] for x in c)


COUNT0 = 7
Z0, REST0, WEIGHT0 = 4, 5, 6


def apply_plane(v_ref, case, i, c_ref, j):
    v = v_ref[case, i]
    out = c_ref[REST0, j] * v + c_ref[0, j] * (v - roll(v, 1, 1)) + c_ref[1, j] * (v - roll(v, -1, 1))
    out = out + c_ref[2, j] * (v - roll(v, 1, 0)) + c_ref[3, j] * (v - roll(v, -1, 0))
    return out + c_ref[Z0, j] * (v - v_ref[case, i - 1]) + c_ref[Z0, j + 1] * (v - v_ref[case, i + 1])


def copy_in(source, target, sem):
    copy = pltpu.make_async_copy(source, target, sem)
    copy.start()
    return copy


def pairs_of_rows(v, scratch):
    n, rows, _ = v.shape
    scratch[: n * rows, :] = v.reshape(n * rows, 128)
    half = n * rows // 2
    even = scratch[pl.ds(0, half, stride=2), :]
    odd = scratch[pl.ds(1, half, stride=2), :]
    return (even + odd).reshape(n, rows // 2, 128)


def put_rows_twice(v, scratch):
    n, rows, _ = v.shape
    flat = v.reshape(n * rows, 128)
    scratch[pl.ds(0, n * rows, stride=2), :] = flat
    scratch[pl.ds(1, n * rows, stride=2), :] = flat


def rows_twice(v, scratch):
    n, rows, _ = v.shape
    put_rows_twice(v, scratch)
    return scratch[: 2 * n * rows, :].reshape(n, 2 * rows, 128)


def flat_dot(v, matrix):
    n, rows, _ = v.shape
    return dot(v.reshape(n * rows, 128), matrix).reshape(n, rows, 128)


def fine_to_level1(t_ref, r_ref, work, count, split):
    flat0 = t_ref[0, :count].reshape(count * NY, 128)
    flat1 = t_ref[1, :count].reshape(count * NY, 128)
    work[: count * NY, :] = dot(flat0, fine_to_half(0)) + dot(flat1, fine_to_half(1))
    r_ref[...] = jnp.zeros_like(r_ref)
    for p in range(count):
        even = work[pl.ds(p * NY, NY // 2, stride=2), :]
        odd = work[pl.ds(p * NY + 1, NY // 2, stride=2), :]
        r_ref[split + p, 0 : NY // 2, :] = even + odd


def down(r_ref, c0, c1, s1, s2, t_ref, work, s2_hbm, sem, reach, rows, s21_out, r1_out, talk):
    trim = 4 - reach
    t = trim // 2

    def first(j):
        return [(s1, (case, j), c0[WEIGHT0, j] * r_ref[case, j]) for case in range(2)]

    planes(1 + trim, WINDOW - 1 - trim, first)

    def second(j):
        return [
            (s2, (case, j), s1[case, j] + c0[WEIGHT0, j] * (r_ref[case, j] - apply_plane(s1, case, j, c0, j)))
            for case in range(2)
        ]

    planes(2 + trim, WINDOW - 2 - trim, second)
    copy = copy_in(s2.at[:, HALO - reach : HALO + BLOCK + reach], s2_hbm, sem)
    count = Q1 - 2 - 2 * t

    def third(p):
        a = 2 * (p + 1 + t) + 1
        return [
            (
                t_ref,
                (case, p),
                (r_ref[case, a] - apply_plane(s2, case, a, c0, a))
                + (r_ref[case, a + 1] - apply_plane(s2, case, a + 1, c0, a + 1)),
            )
            for case in range(2)
        ]

    planes(0, count, third, 4)
    fine_to_level1(t_ref, r1_out, work, count, 1 + t)

    c = tuple(c1[k] for k in range(COUNT))
    lo, hi = 1 + t, Q1 - 1 - t
    forcing = r1_out[lo:hi]
    smoothed = c[WEIGHT][lo:hi] * forcing
    leftover = forcing - apply(smoothed, cut(c, lo, hi), z_prev, z_next)
    relaxed = (smoothed + c[WEIGHT][lo:hi] * leftover)[1:-1]
    s21_out[...] = relaxed
    lo, hi = QB - 1, QB + 5
    inner = relaxed[lo - 2 - t : hi - 2 - t]
    rest = (r1_out[lo:hi] - apply(inner, cut(c, lo, hi), z_prev, z_next))[1:5]
    low, high = rest[0] + rest[1], rest[2] + rest[3]
    mixed = dot(low, half_to_quarter(0)) + dot(high, half_to_quarter(1))
    summed = pairs_of_rows(mixed[None], work)[0]
    work[0:12, :] = summed
    at = 10
    for row in rows:
        work[at : at + row.shape[0], :] = row
        at += row.shape[0]
    tile = work[0 : talk.shape[1], :]
    talk[...] = jnp.broadcast_to(tile[None], talk.shape)
    return copy


def count_kernel(me, index, out, acc):
    base = (me[0] * BLOCK - HALO) * NY
    rows = WINDOW * NY
    chunk = 512
    total = index.shape[1]
    for case in range(2):
        acc[...] = jnp.zeros_like(acc)

        def step(i, carry):
            ids = index[pl.ds(case, 1), pl.ds(pl.multiple_of(i * chunk, chunk), chunk)]
            row = (ids >> 7) - base
            col = ids & 127
            hit_row = jnp.where(iota((rows, chunk), 0) == row, 1.0, 0.0).astype(jnp.bfloat16)
            hit_col = jnp.where(iota((128, chunk), 0) == col, 1.0, 0.0).astype(jnp.bfloat16)
            acc[...] += lax.dot_general(
                hit_row, hit_col, (((1,), (1,)), ((), ())), preferred_element_type=F32
            )
            return carry

        lax.fori_loop(0, total // chunk, step, 0)
        out[case] = acc[...].reshape(WINDOW, NY, 128)


def neighbours_x(p):
    lane = iota(p.shape, 1)
    return jnp.where(lane > 0, roll(p, 1, 1), 0.0) + jnp.where(lane < NX - 1, roll(p, -1, 1), 0.0)


def neighbours_y(p):
    row = iota(p.shape, 0)
    return jnp.where(row > 0, roll(p, 1, 0), 0.0) + jnp.where(row < NY - 1, roll(p, -1, 0), 0.0)


def filter_parts(p):
    sides_y = neighbours_y(p)
    cross = neighbours_x(p) + sides_y
    return cross, 1.5 * p + 0.5 * cross + EDGE_WEIGHT * neighbours_x(sides_y)


def weight_of(me, members, z):
    at = me * BLOCK + z
    lane, row = iota((NY, NX), 1), iota((NY, NX), 0)
    nx = (lane > 0).astype(F32) + (lane < NX - 1).astype(F32)
    ny = (row > 0).astype(F32) + (row < NY - 1).astype(F32)
    nz = jnp.where(at > 0, 1.0, 0.0) + jnp.where(at < members * BLOCK - 1, 1.0, 0.0)
    return 1.5 + 0.5 * (nx + ny + nz) + EDGE_WEIGHT * (nx * ny + nx * nz + ny * nz)


NEAR, AWAY = 3 * BLOCK, 3 * NEXT + 1


def collect_kernel(case_ref, design, passive, fixed, own, near, head, tail, all_head, all_tail):
    at = 0
    for k, source in enumerate((design, passive, fixed)):
        value = source[...].astype(F32)
        own[k * BLOCK : (k + 1) * BLOCK] = value
        count = NEXT + 1 if k == 0 else NEXT
        all_head[at : at + count] = value[0:count]
        all_tail[at : at + count] = value[BLOCK - count : BLOCK]
        at += count
    case = case_ref[0]
    near[...] = own[pl.ds(case * (NEAR // 2), NEAR // 2)]
    head[...] = all_head[pl.ds(case * (AWAY // 2), AWAY // 2)]
    tail[...] = all_tail[pl.ds(case * (AWAY // 2), AWAY // 2)]


def setup_kernel(
    members, me_ref, case_ref, own, before, after, before2, after2, o_before, o_after, o_before2, o_after2, counts,
    c0_hbm, c1_hbm, force_hbm, s2_hbm, s21, r1_out, talk, mod_hbm, free_hbm, scale_hbm,
    near_b, near_a, away_b, away_a,
    raw, cross, base, c0, c1, force, mod, free, scale, s1, s2, t_ref, work, small, sems,
):
    me, case = me_ref[0], case_ref[0]
    halves = (
        (near_b, before, o_before),
        (near_a, after, o_after),
        (away_b, before2, o_before2),
        (away_a, after2, o_after2),
    )
    for target, mine, other in halves:
        half = mine.shape[0]
        target[pl.ds(case * half, half)] = mine[...]
        target[pl.ds((1 - case) * half, half)] = other[...]
    start = 0
    for source, count in ((away_b, NEXT + 1), (near_b, BLOCK), (own, BLOCK), (near_a, BLOCK), (away_a, NEXT + 1)):
        raw[start : start + count] = source[0:count]
        start += count

    def parts(k):
        a, b = filter_parts(raw[k])
        return [(cross, (k,), a), (base, (k,), b)]

    planes(0, WINDOW + 2, parts, 6)

    def material(j, passive, fixed, near):
        z = j - HALO
        at = me * BLOCK + z
        inside = jnp.where((at >= 0) & (at < members * BLOCK), 1.0, 0.0)
        filtered = base[j + 1] + 0.5 * (raw[j] + raw[j + 2]) + EDGE_WEIGHT * (cross[j] + cross[j + 2])
        weight = weight_of(me, members, z)
        density = jnp.where(passive == 1.0, 1.0, jnp.where(passive == 2.0, 0.0, filtered / weight))
        modulus = E_MIN + (1.0 - E_MIN) * density * density * density
        freedom = inside * (1.0 - fixed)
        writes = [(mod, (j,), inside * modulus), (free, (j,), freedom)]
        writes += [(force, (case, j), freedom * (HEAT_SOURCE + counts[case, j])) for case in range(2)]
        if near:
            gradient = (-1.5 * (1.0 - E_MIN)) * density * density / (modulus * weight)
            gradient = jnp.where(passive == 0.0, inside * gradient, 0.0)
            writes.append((scale, (j - HALO + 1,), gradient))
        return writes

    def stretch(source, first, second, j0, lo, hi, near=False):
        planes(lo, hi, lambda j: material(j, source[first + j - j0], source[second + j - j0], near), 5)

    stretch(away_b, NEXT + 1, 2 * NEXT + 1, 0, 0, NEXT)
    stretch(near_b, BLOCK, 2 * BLOCK, NEXT, NEXT, HALO - 1)
    stretch(near_b, BLOCK, 2 * BLOCK, NEXT, HALO - 1, HALO, True)
    stretch(own, BLOCK, 2 * BLOCK, HALO, HALO, HALO + BLOCK, True)
    stretch(near_a, BLOCK, 2 * BLOCK, HALO + BLOCK, HALO + BLOCK, HALO + BLOCK + 1, True)
    stretch(near_a, BLOCK, 2 * BLOCK, HALO + BLOCK, HALO + BLOCK + 1, HALO + 2 * BLOCK)
    stretch(away_a, NEXT + 1, 2 * NEXT + 1, HALO + 2 * BLOCK, HALO + 2 * BLOCK, WINDOW)
    near = slice(HALO - 2, HALO + BLOCK + 2)
    copies = [
        copy_in(force, force_hbm, sems.at[0]),
        copy_in(mod.at[near], mod_hbm, sems.at[1]),
        copy_in(free.at[near], free_hbm, sems.at[2]),
        copy_in(scale, scale_hbm, sems.at[3]),
    ]

    lane, row = iota((NY, NX), 1), iota((NY, NX), 0)
    zero = jnp.zeros((NY, NX), F32)

    def coefficients(j):
        m, f = mod[j], free[j]
        total, held = zero, zero
        writes = []
        for dim, mask, slot in ((1, lane > 0, 0), (0, row > 0, 2)):
            k = jnp.where(mask, jnp.sqrt(m * roll(m, 1, dim)), 0.0)
            ka = roll(k, -1, dim)
            fp = roll(f, 1, dim)
            total = total + k + ka
            held = held + k * (1.0 - fp) + ka * (1.0 - roll(f, -1, dim))
            inner = k * f * fp
            writes += [(c0, (slot, j), inner), (c0, (slot + 1, j), roll(inner, -1, dim))]
        k, ka = jnp.sqrt(m * mod[j - 1]), jnp.sqrt(m * mod[j + 1])
        total = total + k + ka
        held = held + k * (1.0 - free[j - 1]) + ka * (1.0 - free[j + 1])
        writes.append((c0, (Z0, j), k * f * free[j - 1]))
        writes.append((c0, (REST0, j), f * held + (1.0 - f)))
        writes.append((c0, (WEIGHT0, j), OMEGA / (f * total + (1.0 - f))))
        return writes

    planes(1, WINDOW - 1, coefficients, 4)
    last = WINDOW - 1
    for slot in range(COUNT0):
        c0[slot, 0] = zero
        c0[slot, last] = zero
    c0[Z0, last] = jnp.sqrt(mod[last] * mod[last - 1]) * free[last] * free[last - 1]
    copies.append(copy_in(c0, c0_hbm, sems.at[4]))

    def join(q):
        return [(t_ref, (k, q), x[2 * q + 1] + x[2 * q + 2]) for k, x in enumerate((mod, free))]

    planes(0, Q1, join)
    fine_to_level1(t_ref, small, work, Q1, 0)
    both = small[...]
    second = iota(both.shape, 2) >= 64
    both = jnp.where(second, (both > 0.0).astype(F32), 0.125 * both)
    turned = roll(both, 64, 2)
    m1 = jnp.where(second, turned, both)
    f1 = jnp.where(second, both, turned)
    for k, value in enumerate(couple(m1, f1, 2.0, 64, z_prev, z_next)):
        c1[k] = value
    copies.append(copy_in(c1, c1_hbm, sems.at[5]))

    low, high = both[QB] + both[QB + 1], both[QB + 2] + both[QB + 3]
    mixed = dot(low, half_to_quarter(0)) + dot(high, half_to_quarter(1))
    coarse = pairs_of_rows(mixed[None], work)[0]
    is_free = (iota(coarse.shape, 1) & 32) > 0
    coarse = jnp.where(is_free, (coarse > 0.0).astype(F32), 0.125 * coarse)

    rows = (coarse, jnp.zeros((2, 128), F32))
    copies.append(down(force, c0, c1, s1, s2, t_ref, work, s2_hbm, sems.at[6], 2, rows, s21, r1_out, talk))
    for copy in copies:
        copy.wait()


def coarse_window(me, gathered, lo, hi):
    members = gathered.shape[0]
    tiles = []
    for d in range(ND):
        at = me + d - REACH
        inside = jnp.where((at >= 0) & (at < members), 1.0, 0.0)
        tiles.append(inside * gathered[jnp.clip(at, 0, members - 1), lo:hi, :])
    return jnp.stack(tiles, axis=0)


def coarse_setup(me, gathered, c2, c3, work, wide):
    wide[...] = jnp.zeros_like(wide)
    wide[:, 0:10, :] = coarse_window(me, gathered, 10, 20)
    both = wide[...]
    is_free = (iota(both.shape, 2) & 32) > 0
    m = jnp.where(is_free, roll(both, 32, 2), both)
    f = jnp.where(is_free, both, roll(both, -32, 2))
    for k, value in enumerate(couple(m, f, 4.0, 32, z_prev2, z_next2)):
        c2[k] = value
    eighth = quarter_to_eighth()
    m3 = 0.125 * pairs_of_rows(flat_dot(m, eighth), work)
    f3 = (pairs_of_rows(flat_dot(f, eighth), work) > 0.0).astype(F32)
    for k, value in enumerate(couple(m3, f3, 8.0, 16, z_prev, z_next)):
        c3[k] = value


def coarse_solve(r2, c2, c3, work):
    c = tuple(c2[k] for k in range(COUNT))
    smoothed = c[WEIGHT] * r2
    relaxed = smoothed + c[WEIGHT] * (r2 - apply(smoothed, c, z_prev2, z_next2))
    leftover = (r2 - apply(relaxed, c, z_prev2, z_next2))[2 : ND - 2]
    forcing = pairs_of_rows(flat_dot(leftover, quarter_to_eighth()), work)
    lo, hi = 2, ND - 2
    v = c3[WEIGHT, lo:hi] * forcing
    for _ in range(7):
        ck = tuple(c3[k, lo:hi] for k in range(COUNT))
        v = v + ck[WEIGHT] * (forcing - apply(v, ck, z_prev, z_next))
        v, forcing = v[1:-1], forcing[1:-1]
        lo, hi = lo + 1, hi - 1
    up = rows_twice(flat_dot(v, eighth_to_quarter()), work)
    lo, hi = REACH - 2, REACH + 3
    v = relaxed[lo:hi] + up
    ck = cut(c, lo, hi)
    for _ in range(2):
        v = v + ck[WEIGHT] * (r2[lo:hi] - apply(v, ck, z_prev2, z_next2))
    return v[1:4]


def level1_up(e2, relaxed, forcing, c, work):
    parts = []
    for low in range(2):
        lanes = flat_dot(e2, quarter_to_half(low))
        parts.append(rows_twice(lanes, work)[:, :R1])
    lifted = [parts[z & 1][z >> 1] for z in range(6)]
    n = relaxed.shape[0]
    lead = (12 - n) // 2
    v = relaxed + jnp.stack([lifted[(q + lead) // 2] for q in range(n)], axis=0)
    for _ in range(2):
        v = (v + c[WEIGHT] * (forcing - apply(v, c, z_prev, z_next)))[1:-1]
        forcing, c = forcing[1:-1], cut(c, 1, -1)
    return v


def level0_up(v1, s2, r, vb, c0, out, work):
    count = v1.shape[0]
    for case in range(2):
        lanes = flat_dot(v1, half_to_fine(case))
        put_rows_twice(lanes, work)
        for p in range(count):
            fine = work[p * 2 * R1 : p * 2 * R1 + NY, :]
            s2[case, 2 * p] = s2[case, 2 * p] + fine
            s2[case, 2 * p + 1] = s2[case, 2 * p + 1] + fine
    total = s2.shape[1]

    def sweep(v, case, i):
        return v[case, i] + c0[WEIGHT0, i] * (r[case, i - 1] - apply_plane(v, case, i, c0, i))

    def once(i):
        return [(vb, (case, i), sweep(s2, case, i)) for case in range(2)]

    planes(1, total - 1, once, 7 if total == 16 else 5)

    def twice(i):
        return [(out, (case, i - 2), sweep(vb, case, i)) for case in range(2)]

    planes(2, total - 2, twice, 6 if total == 16 else 8)


def add_up(parts):
    while len(parts) > 1:
        parts = [sum(parts[i : i + 2][1:], parts[i]) for i in range(0, len(parts), 2)]
    return parts[0]


def sum_of_rows(gathered, lo, hi):
    return add_up([gathered[d, lo:hi, :] for d in range(gathered.shape[0])])


def residual_window(me, gathered):
    r2 = coarse_window(me, gathered, 0, 16)
    return jnp.where(iota(r2.shape, 1) < 10, r2, 0.0)


def around(reach):
    return slice(HALO - reach, HALO + BLOCK + reach)


def up_kernel(first, me_ref, gathered, r_hbm, s2_hbm, s21, r1_ref, c0_hbm, c1_hbm, *rest):
    if first:
        out, head, tail, c2, c3, s2, r, c0, c1, vb, work, wide, sems = rest
    else:
        c2, c3, out, head, tail, dots, s2, r, c0, c1, vb, work, wide, sems = rest
    sources = (
        (s2_hbm, s2),
        (r_hbm.at[:, around(1)], r),
        (c0_hbm.at[:, around(2)], c0),
        (c1_hbm.at[:, 3:13], c1),
    )
    copies = [copy_in(a, b, sems.at[i]) for i, (a, b) in enumerate(sources)]
    me = me_ref[0]
    if first:
        coarse_setup(me, gathered, c2, c3, work, wide)
    else:
        dots[...] = sum_of_rows(gathered, 8, 16)
    e2 = coarse_solve(residual_window(me, gathered), c2, c3, work)
    for copy in copies:
        copy.wait()
    v1 = level1_up(e2, s21[...], r1_ref[3:13], tuple(c1[k] for k in range(COUNT)), work)

    level0_up(v1, s2, r, vb, c0, out, work)
    for case in range(2):
        head[case] = out[case, 0:NEXT]
        tail[case] = out[case, BLOCK - NEXT : BLOCK]


def lay_out(win, own, before, after, before2, after2):
    start = 0
    for source in (before2, before, own, after, after2):
        count = source.shape[1]
        for case in range(2):
            win[case, start : start + count] = source[case]
        start += count


def dot_rows(values):
    lane = iota((1, 128), 1)
    rows = []
    for a, b in values:
        rows.append(jnp.where(lane < 64, jnp.sum(a, keepdims=True), jnp.sum(b, keepdims=True)))
    return rows


def accumulate(count, term):
    sums = []
    for case in range(2):
        terms = [term(case, k) for k in range(BLOCK)]
        sums.append([add_up([t[i] for t in terms]) for i in range(count)])
    return dot_rows([(sums[0][i], sums[1][i]) for i in range(count)])


def first_kernel(
    own, before, after, before2, after2, force_hbm, c0, c1,
    u_hbm, w_hbm, s2_hbm, s21, r1_out, talk,
    u_win, w_win, force, s1, s2, t_ref, work, sems,
):
    copy_f = copy_in(force_hbm.at[:, around(0)], force, sems.at[0])
    lay_out(u_win, own, before, after, before2, after2)
    copies = [copy_in(u_win.at[:, around(2)], u_hbm, sems.at[1])]

    def image(j):
        return [(w_win, (case, j), apply_plane(u_win, case, j, c0, j)) for case in range(2)]

    planes(1, WINDOW - 1, image)
    copies.append(copy_in(w_win, w_hbm, sems.at[2]))
    copy_f.wait()

    def term(case, k):
        u = own[case, k]
        return (force[case, k] * u, w_win[case, HALO + k] * u)

    rows = accumulate(2, term) + [jnp.zeros((4, 128), F32)]
    copies.append(down(w_win, c0, c1, s1, s2, t_ref, work, s2_hbm, sems.at[3], 2, rows, s21, r1_out, talk))
    for copy in copies:
        copy.wait()


def of_case(row, case):
    return row[:, 64 * case : 64 * case + 1]


def second_kernel(
    own, before, after, before2, after2, dots0, force_hbm, u0_hbm, w0_hbm, c0, c1,
    m_hbm, u1_hbm, w1_hbm, n0_hbm, s2_hbm, s21, r1_out, talk,
    m_win, u0, w0, n0, u1, w1, force, s1, s2, t_ref, work, sems,
):
    copy_w = copy_in(w0_hbm, w0, sems.at[0])
    copy_u = copy_in(u0_hbm, u0, sems.at[1])
    copy_f = copy_in(force_hbm.at[:, around(0)], force, sems.at[2])
    lay_out(m_win, own, before, after, before2, after2)
    copies = [copy_in(m_win.at[:, around(2)], m_hbm, sems.at[3])]
    alpha = [of_case(dots0[2:3, :] / dots0[3:4, :], case) for case in range(2)]
    copy_w.wait()

    def image(j, block=False):
        writes = []
        for case in range(2):
            n = apply_plane(m_win, case, j, c0, j)
            writes.append((w1, (case, j), w0[case, j] - alpha[case] * n))
            if block:
                writes.append((n0, (case, j - HALO), n))
        return writes

    planes(1, HALO, image, 6)
    planes(HALO, HALO + BLOCK, functools.partial(image, block=True))
    planes(HALO + BLOCK, WINDOW - 1, image, 6)
    copies.append(copy_in(n0, n0_hbm, sems.at[4]))
    copies.append(copy_in(w1, w1_hbm, sems.at[5]))
    copy_u.wait()

    def update(i):
        return [(u1, (case, i), u0[case, i] - alpha[case] * m_win[case, i + HALO - 2]) for case in range(2)]

    planes(0, BLOCK + 4, update)
    copies.append(copy_in(u1, u1_hbm, sems.at[6]))
    copy_f.wait()

    def term(case, k):
        j = HALO + k
        u, w, ww = u1[case, k + 2], w1[case, j], w0[case, j]
        r = force[case, k] - alpha[case] * ww
        return (r * u, w * u, u * ww + u0[case, k + 2] * w)

    rows = accumulate(3, term) + [jnp.zeros((3, 128), F32)]
    copies.append(down(w1, c0, c1, s1, s2, t_ref, work, s2_hbm, sems.at[7], 4, rows, s21, r1_out, talk))
    for copy in copies:
        copy.wait()


def third_kernel(
    me_ref, gathered, dots0, s21, r1_ref, c0_hbm, c1_hbm, c2, c3,
    w1_hbm, s2_hbm, force_hbm, u0_hbm, w0_hbm, m0_hbm, n0_hbm, u1_hbm,
    u2, p1, x2, talk, dots1,
    s2, w1, vb, m_win, force, u0, w0, m0, n0, u1, c0, c1, work, sems,
):
    sources = (
        (c1_hbm.at[:, 2:14], c1),
        (s2_hbm, s2),
        (c0_hbm.at[:, around(4)], c0),
        (w1_hbm.at[:, around(3)], w1),
        (force_hbm.at[:, around(0)], force),
        (u0_hbm, u0),
        (w0_hbm.at[:, around(0)], w0),
        (m0_hbm, m0),
        (n0_hbm, n0),
        (u1_hbm, u1),
    )
    copies = [copy_in(a, b, sems.at[i]) for i, (a, b) in enumerate(sources)]
    dots1[...] = sum_of_rows(gathered, 8, 16)
    e2 = coarse_solve(residual_window(me_ref[0], gathered), c2, c3, work)
    copies[0].wait()
    v1 = level1_up(e2, s21[...], r1_ref[2:14], tuple(c1[k] for k in range(COUNT)), work)

    for copy in copies[1:]:
        copy.wait()
    level0_up(v1, s2, w1, vb, c0, m_win, work)

    gamma0, delta0 = dots0[2:3, :], dots0[3:4, :]
    gamma1 = dots1[2:3, :]
    beta = gamma1 / gamma0
    curve = dots1[3:4, :] + beta * dots1[4:5, :] + beta * beta * delta0
    a0 = [of_case(gamma0 / delta0, case) for case in range(2)]
    a1 = [of_case(gamma1 / curve, case) for case in range(2)]
    b1 = [of_case(beta, case) for case in range(2)]

    def update(i):
        writes = []
        for case in range(2):
            p = u1[case, i] + b1[case] * u0[case, i]
            writes.append((p1, (case, i), p))
            writes.append((x2, (case, i), a0[case] * u0[case, i] + a1[case] * p))
            u = u1[case, i] - a1[case] * (m_win[case, i] + b1[case] * m0[case, i])
            writes.append((u2, (case, i), u))
        return writes

    planes(0, 12, update)

    def term(case, k):
        n1 = apply_plane(m_win, case, k + 2, c0, k + 4)
        ww, wv = w0[case, k], w1[case, k + 3]
        s = wv + b1[case] * ww
        w = wv - a1[case] * (n1 + b1[case] * n0[case, k])
        r = force[case, k] - a0[case] * ww - a1[case] * s
        u, p = u2[case, k + 2], p1[case, k + 2]
        return (r * u, w * u, u * s + p * w)

    rows = accumulate(3, term) + [jnp.zeros((5, 128), F32)]
    tile = jnp.concatenate(rows, axis=0)
    talk[...] = jnp.broadcast_to(tile[None], talk.shape)


def last_kernel(gathered, dots0, dots1, u2, p1, x2, mod, free, state, energy, w_win):
    total = add_up([gathered[d] for d in range(gathered.shape[0])])
    gamma0, delta0 = dots0[2:3, :], dots0[3:4, :]
    gamma1 = dots1[2:3, :]
    beta1 = gamma1 / gamma0
    curve1 = dots1[3:4, :] + beta1 * dots1[4:5, :] + beta1 * beta1 * delta0
    gamma2 = total[0:1, :]
    beta2 = gamma2 / gamma1
    curve2 = total[1:2, :] + beta2 * total[2:3, :] + beta2 * beta2 * curve1
    a2 = [of_case(gamma2 / curve2, case) for case in range(2)]
    b2 = [of_case(beta2, case) for case in range(2)]

    def update(i):
        return [
            (w_win, (case, i), x2[case, i] + a2[case] * (u2[case, i] + b2[case] * p1[case, i])) for case in range(2)
        ]

    planes(0, 12, update, 4)
    state[...] = w_win[:, 2:10]

    def hold(i):
        return [(w_win, (case, i), w_win[case, i] * free[i]) for case in range(2)]

    planes(0, 12, hold, 4)
    lane, row = iota((NY, NX), 1), iota((NY, NX), 0)

    def power(i):
        m = mod[i + 1]
        out = jnp.zeros((NY, NX), F32)
        kx = jnp.where(lane > 0, jnp.sqrt(m * roll(m, 1, 1)), 0.0)
        ky = jnp.where(row > 0, jnp.sqrt(m * roll(m, 1, 0)), 0.0)
        kz, kn = jnp.sqrt(m * mod[i]), jnp.sqrt(m * mod[i + 2])
        for case in range(2):
            v = w_win[case, i + 1]
            dx, dy = v - roll(v, 1, 1), v - roll(v, 1, 0)
            dz, dn = v - w_win[case, i], v - w_win[case, i + 2]
            px, py = kx * dx * dx, ky * dy * dy
            out = out + px + roll(px, -1, 1) + py + roll(py, -1, 0) + kz * dz * dz + kn * dn * dn
        return [(energy, (i,), out)]

    planes(0, 10, power, 5)


def sensitivity_kernel(mine, other, scale, passive, out, g, cross, base):
    def gradient(i):
        value = scale[i] * (mine[i] + other[i])
        a, b = filter_parts(value)
        return [(g, (i,), value), (cross, (i,), a), (base, (i,), b)]

    planes(0, 10, gradient, 5)

    def final(k):
        i = k + 1
        value = base[i] + 0.5 * (g[i - 1] + g[i + 1]) + EDGE_WEIGHT * (cross[i - 1] + cross[i + 1])
        return [(out, (k,), jnp.where(passive[k] == 0, value, 0.0))]

    planes(0, 8, final)


def shape(*dims):
    return jax.ShapeDtypeStruct(dims, F32)


def hbm(*dims):
    return pltpu.HBM(dims, F32), pltpu.HBM


def vmem(*dims):
    return shape(*dims), pltpu.VMEM


def call(body, outs, scratch, args, name, sems=0, cost=None):
    pairs = [a if isinstance(a, tuple) else (a, pltpu.VMEM) for a in args]
    scratches = [pltpu.VMEM(s, F32) for s in scratch]
    if sems:
        scratches.append(pltpu.SemaphoreType.DMA((sems,)))
    given = [pltpu.with_memory_space_constraint(a, m) if m is pltpu.HBM else a for a, m in pairs]
    return pl.pallas_call(
        body,
        out_shape=[o for o, _ in outs],
        in_specs=[pl.BlockSpec(memory_space=m) for _, m in pairs],
        out_specs=[pl.BlockSpec(memory_space=m) for _, m in outs],
        scratch_shapes=scratches,
        compiler_params=CPARAMS,
        cost_estimate=cost,
        name=name,
    )(*given)


def on_device(design, passive, fixed_mask, load_index):
    members = lax.axis_size("space")
    position = lax.axis_index("space")
    me = position.astype(jnp.int32).reshape(1)
    ahead = [(i, i + 1) for i in range(members - 1)]
    back = [(i + 1, i) for i in range(members - 1)]

    def two_either_side(own, head, tail):
        skip = [(i, i + 2) for i in range(members - 2)]
        skip_back = [(i + 2, i) for i in range(members - 2)]
        return (
            lax.ppermute(own, "space", ahead),
            lax.ppermute(own, "space", back),
            lax.ppermute(tail, "space", skip),
            lax.ppermute(head, "space", skip_back),
        )

    def gather(tiles):
        return lax.all_to_all(tiles, "space", 0, 0)

    plane = (NY, NX)
    window = (2, WINDOW) + plane
    block = (2, BLOCK) + plane
    wide = (2, BLOCK + 4) + plane
    wider = (2, BLOCK + 8) + plane
    work = (800, 128)
    t_shape = (2, Q1) + plane
    position_ref = (me, pltpu.SMEM)

    def down_outs(reach, count):
        near = 2 + reach // 2
        return [
            hbm(2, BLOCK + 2 * reach, *plane),
            vmem(4 + 2 * near, R1, 128),
            vmem(Q1, R1, 128),
            vmem(members, count, 128),
        ]

    def far(x):
        return (x, pltpu.HBM)

    case_ref = (lax.axis_index("case").astype(jnp.int32).reshape(1), pltpu.SMEM)
    own, near, head, tail = call(
        collect_kernel,
        [vmem(NEAR, *plane), vmem(NEAR // 2, *plane), vmem(AWAY // 2, *plane), vmem(AWAY // 2, *plane)],
        [(AWAY,) + plane] * 2,
        (case_ref, design, passive, fixed_mask),
        "collect",
    )
    listened = two_either_side(near, head, tail)
    listened += tuple(lax.ppermute(x, "case", [(0, 1), (1, 0)]) for x in listened)
    counts = call(
        count_kernel,
        [vmem(*window)],
        [(WINDOW * NY, 128)],
        (position_ref, load_index),
        "counts",
        cost=pl.CostEstimate(flops=3 * 10**10, bytes_accessed=10**7, transcendentals=0),
    )[0]
    c0, c1, force, s2, s21, r1, talk, mod, free, scale = call(
        functools.partial(setup_kernel, members),
        [hbm(COUNT0, WINDOW, *plane), hbm(COUNT, Q1, R1, 128), hbm(*window)]
        + down_outs(2, TALK)
        + [hbm(12, *plane), hbm(12, *plane), hbm(10, *plane)],
        [(NEAR,) + plane] * 2
        + [(AWAY,) + plane] * 2
        + [(WINDOW + 2,) + plane] * 3
        + [(COUNT0, WINDOW) + plane, (COUNT, Q1, R1, 128)]
        + [window, (WINDOW,) + plane, (WINDOW,) + plane, (10,) + plane, window, window, t_shape, work]
        + [(Q1, R1, 128)],
        (position_ref, case_ref, own) + listened + (counts,),
        "setup",
        7,
    )

    def up(first, r, s2, s21, r1, talk, more):
        args = (position_ref, gather(talk), far(r), far(s2), s21, r1, far(c0), far(c1)) + tuple(more)
        outs = [vmem(*block), vmem(2, NEXT, *plane), vmem(2, NEXT, *plane)]
        if first:
            outs += [vmem(COUNT, ND, R2, 128), vmem(COUNT, ND, R3, 128)]
        else:
            outs += [vmem(8, 128)]
        scratch = [wide, (2, 10) + plane, (COUNT0, 12) + plane, (COUNT, 10, R1, 128), wide, work, (ND, R2, 128)]
        return call(functools.partial(up_kernel, first), outs, scratch, args, "up", 4)

    u, head, tail, c2, c3 = up(True, force, s2, s21, r1, talk, ())
    u0, w0, s2, s21, r1, talk = call(
        first_kernel,
        [hbm(*wide), hbm(*window)] + down_outs(2, R2),
        [window, window, block, window, window, t_shape, work],
        (u,) + two_either_side(u, head, tail) + (far(force), c0, c1),
        "first",
        4,
    )
    m, head, tail, dots0 = up(False, w0, s2, s21, r1, talk, (c2, c3))
    m0, u1, w1, n0, s2, s21, r1, talk = call(
        second_kernel,
        [hbm(*wide), hbm(*wide), hbm(*window), hbm(*block)] + down_outs(4, R2),
        [window, wide, window, block, wide, window, block, window, window, t_shape, work],
        (m,) + two_either_side(m, head, tail) + (dots0, far(force), far(u0), far(w0), c0, c1),
        "second",
        8,
    )
    u2, p1, x2, talk, dots1 = call(
        third_kernel,
        [vmem(*wide)] * 3 + [vmem(members, 8, 128), vmem(8, 128)],
        [wider, (2, 14) + plane, wider, wide, block, wide, block, wide, block, wide]
        + [(COUNT0, 16) + plane, (COUNT, 12, R1, 128), work],
        (position_ref, gather(talk), dots0, s21, r1, far(c0), far(c1), c2, c3)
        + tuple(far(x) for x in (w1, s2, force, u0, w0, m0, n0, u1)),
        "third",
        10,
    )
    state, energy = call(
        last_kernel,
        [vmem(*block), vmem(10, *plane)],
        [wide],
        (gather(talk), dots0, dots1, u2, p1, x2, mod, free),
        "last",
    )
    other = lax.ppermute(energy, "case", [(0, 1), (1, 0)])
    sensitivity = call(
        sensitivity_kernel,
        [vmem(BLOCK, *plane)],
        [(10,) + plane] * 3,
        (energy, other, scale, passive),
        "sensitivity",
    )[0]
    return state, sensitivity


def solution(mesh):
    placed = (
        P("space", None, None),
        P("space", None, None),
        P("space", None, None),
        P("case", None),
    )
    return jax.shard_map(
        on_device,
        mesh=mesh,
        in_specs=placed,
        out_specs=(P("case", "space", None, None), P("space", None, None)),
        check_vma=False,
    )
```

time: 245 us -> 212 us (0.87)
  blocking collectives: 26.4 us -> 94.3 us
  starting transfers between devices: 91.7 us -> 41.5 us
  local copies, waits for them, and re-layouts: 38.4 us -> 3.54 us
  waiting for transfers between devices: 31.2 us -> 19.2 us
    all_to_all x1 -> x4, blocking collectives: 26.4 us -> 94.3 us  [gather(): return lax.all_to_all(tiles, 'space', 0, 0)]
    all_to_all x3 -> x0, starting transfers between devices: 42.7 us -> none  [gather(): return lax.all_to_all(tiles, 'space', 0, 0)]
    unnamed x118 -> x28, local copies, waits for them, and re-layouts: 38.4 us -> 3.54 us
    all_to_all x3 -> x0, waiting for transfers between devices: 11.6 us -> none  [gather(): return lax.all_to_all(tiles, 'space', 0, 0)]
    ppermute x1, starting transfers between devices: 10.7 us -> 4.32 us  [on_device(): other = lax.ppermute(energy, 'case', [(0, 1), (1, 0)])]
    ppermute x14 -> x16, starting transfers between devices: 38.2 us -> 37.2 us  [the longest x3 13 us: two_either_side(): lax.ppermute(own, 'space', ahead)]
    ppermute x14 -> x16, waiting for transfers between devices: 18.5 us -> 18.1 us  [the longest x3 12.3 us: two_either_side(): lax.ppermute(tail, 'space', skip)]
  transfers between devices with their start and end apart: 18 -> 17, of which waited for: 16 -> 6; matrix products, arithmetic and copies ran while one was open for 0% -> 0% of each run, Pallas kernels for 3% -> 4%
where the time goes in v2:
time: 212 us
  blocking collectives  94.3 us (44%)
  Pallas kernels  52 us (25%)
  starting transfers between devices  41.5 us (20%)
  waiting for transfers between devices  19.2 us (9%)
  local copies, waits for them, and re-layouts  3.54 us (2%)
    all_to_all x4, blocking collectives, gather(): return lax.all_to_all(tiles, 'space', 0, 0)  94.3 us
    pallas_call x10, Pallas kernels, call(): pl.pallas_call(body, out_shape=[o for o, _ in outs], in_specs=[pl.BlockSp...  52 us
    ppermute x3, starting transfers between devices, two_either_side(): lax.ppermute(own, 'space', ahead)  13 us
    ppermute x3, waiting for transfers between devices, two_either_side(): lax.ppermute(tail, 'space', skip)  12.3 us
    ppermute x3, starting transfers between devices, two_either_side(): lax.ppermute(tail, 'space', skip)  10.9 us
    ppermute x3, waiting for transfers between devices, two_either_side(): lax.ppermute(head, 'space', skip_back)  5.82 us
    ppermute x4, starting transfers between devices, on_device(): lax.ppermute(x, 'case', [(0, 1), (1, 0)])  5.32 us
    ppermute x1, starting transfers between devices, on_device(): other = lax.ppermute(energy, 'case', [(0, 1), (1, 0)])  4.32 us
  transfers between devices with their start and end apart: 17, of which 6 were waited for; matrix products, arithmetic and copies ran while one was open for 0% of the time, Pallas kernels for 4%

profile of v2, /device:TPU:1, one launch (start us, length us, event | category | flops | bytes accessed | tf_op | source)
XLA Modules:
  0.0 211.5 jit_solution(710658945749465183)
XLA Ops:
  3.5 1.3 collective-permute-start.1
  4.8 5.0 %collective-permute-start = (f32[12,40,128]{2,1,0:T(8,128)S(1)}, f32[12,40,128]{2,1,0:T(8,128)S(1)}, u32[]{:S(2)}, u32[]{:S(2)}) collective-permute-start(f32[12,40,128]{2,1,0:T(8,128)S(1)} %get-tuple-element.47), channel_id=1, source_target_pairs={{0,1},{1,2},{2,3},{3,4},{4,5},{5,6},{6,7},{7,8},{8,9},{9,10},{10,1... | collective-permute-start | bytes 737288 | tf_op jit(solution)/shard_map/ppermute | solution.py:852
  9.8 5.3 %collective-permute-start.2 = (f32[8,40,128]{2,1,0:T(8,128)S(1)}, f32[8,40,128]{2,1,0:T(8,128)S(1)}, u32[]{:S(2)}, u32[]{:S(2)}) collective-permute-start(f32[8,40,128]{2,1,0:T(8,128)S(1)} %get-tuple-element.48), channel_id=1, source_target_pairs={{0,2},{1,3},{2,4},{3,5},{4,6},{5,7},{6,8},{7,9},{8,10},{9,11},{10,... | collective-permute-start | bytes 491528 | tf_op jit(solution)/shard_map/ppermute | solution.py:854
  15.1 1.3 collective-permute-start.3
  17.4 2.1 %collective-permute-start.6 = (f32[8,40,128]{2,1,0:T(8,128)S(1)}, f32[8,40,128]{2,1,0:T(8,128)S(1)}, u32[]{:S(2)}, u32[]{:S(2)}) collective-permute-start(f32[8,40,128]{2,1,0:T(8,128)S(1)} %collective-permute-done.2.before2), channel_id=1, source_target_pairs={{0,64},{64,0},{1,65},{65,1},{2,66},{66,2},{3,67},{67,3},{4,68},{68... | collective-permute-start | bytes 491528 | tf_op jit(solution)/shard_map/ppermute | solution.py:891
  19.6 3.1 %collective-permute-done.3.after2 = f32[8,40,128]{2,1,0:T(8,128)S(1)} collective-permute-done((f32[8,40,128]{2,1,0:T(8,128)S(1)}, f32[8,40,128]{2,1,0:T(8,128)S(1)}, u32[]{:S(2)}, u32[]{:S(2)}) %collective-permute-start.3) | collective-permute-done | bytes 163872 | tf_op jit(solution)/shard_map/ppermute | solution.py:855
  22.7 2.7 %collective-permute-start.7 = (f32[8,40,128]{2,1,0:T(8,128)S(1)}, f32[8,40,128]{2,1,0:T(8,128)S(1)}, u32[]{:S(2)}, u32[]{:S(2)}) collective-permute-start(f32[8,40,128]{2,1,0:T(8,128)S(1)} %collective-permute-done.3.after2), channel_id=1, source_target_pairs={{0,64},{64,0},{1,65},{65,1},{2,66},{66,2},{3,67},{67,3},{4,68},{68... | collective-permute-start | bytes 491528 | tf_op jit(solution)/shard_map/ppermute | solution.py:891
  26.7 8.8 %counts.1 = f32[2,34,40,128]{3,2,1,0:T(8,128)S(1)} custom-call(s32[1]{0:T(128)} %bitcast.me.me_ref, s32[2,4096]{1,0:T(2,128)S(1)} %copy-done.9), custom_call_target="tpu_custom_call" | custom-call | flops 30000001024 | bytes 10000000 | tf_op jit(solution)/shard_map/counts/pallas_call | solution.py:829
  35.5 9.6 %setup.1 = (f32[7,34,40,128]{3,2,1,0:T(8,128)}, f32[8,16,24,128]{3,2,1,0:T(8,128)}, f32[2,34,40,128]{3,2,1,0:T(8,128)}, f32[2,12,40,128]{3,2,1,0:T(8,128)}, f32[...) custom-call(s32[1]{0:T(128)} %bitcast.me.me_ref, ...), custom_call_target="tpu_custom_call" | custom-call | tf_op jit(solution)/shard_map/setup/pallas_call | solution.py:829
  45.1 29.6 %all_to_all.20.gathered = f32[64,24,128]{2,1,0:T(8,128)S(1)} all-to-all(f32[64,24,128]{2,1,0:T(8,128)S(1)} %get-tuple-element.50), channel_id=1, replica_groups=mesh['case'=2,'space'=64] {'space'}, dimensions={0} | all-to-all | bytes 1572864 | tf_op jit(solution)/shard_map/all_to_all | solution.py:859
  74.7 5.9 %up.2 = (f32[2,8,40,128]{3,2,1,0:T(8,128)S(1)}, f32[2,5,40,128]{3,2,1,0:T(8,128)S(1)}, f32[2,5,40,128]{3,2,1,0:T(8,128)S(1)}, f32[8,23,16,128]{3,2,1,0:T(8,128)S(1)}, f32[8,23,8,128]{3,2,1,0:T(8,128)S(1)}) custom-call(s32[1]{0:T(128)} %bitcast.me.me_ref, f32[64,24,128]{2,1,0:T(8,128)S(1)} %all_to_all.20.gathered, ...), custom_call_target="tpu_custom_call" | custom-call | tf_op jit(solution)/shard_map/up/pallas_call | solution.py:829
  80.6 1.3 collective-permute-start.9
  81.9 4.0 %collective-permute-start.8 = (f32[2,8,40,128]{3,2,1,0:T(8,128)S(1)}, f32[2,8,40,128]{3,2,1,0:T(8,128)S(1)}, u32[]{:S(2)}, u32[]{:S(2)}) collective-permute-start(f32[2,8,40,128]{3,2,1,0:T(8,128)S(1)} %get-tuple-element.57.own), channel_id=1, source_target_pairs={{0,1},{1,2},{2,3},{3,4},{4,5},{5,6},{6,7},{7,8},{8,9},{9,10},{10,1... | collective-permute-start | bytes 983048 | tf_op jit(solution)/shard_map/ppermute | solution.py:852
  85.9 2.9 %collective-permute-start.10 = (f32[2,5,40,128]{3,2,1,0:T(8,128)S(1)}, f32[2,5,40,128]{3,2,1,0:T(8,128)S(1)}, u32[]{:S(2)}, u32[]{:S(2)}) collective-permute-start(f32[2,5,40,128]{3,2,1,0:T(8,128)S(1)} %get-tuple-element.58), channel_id=1, source_target_pairs={{0,2},{1,3},{2,4},{3,5},{4,6},{5,7},{6,8},{7,9},{8,10},{9,11},{10,... | collective-permute-start | bytes 614408 | tf_op jit(solution)/shard_map/ppermute | solution.py:854
  88.8 1.5 collective-permute-start.11
  90.3 7.1 %collective-permute-done.10.before2 = f32[2,5,40,128]{3,2,1,0:T(8,128)S(1)} collective-permute-done((f32[2,5,40,128]{3,2,1,0:T(8,128)S(1)}, f32[2,5,40,128]{3,2,1,0:T(8,128)S(1)}, u32[]{:S(2)}, u32[]{:S(2)}) %collective-permute-start.10) | collective-permute-done | bytes 204832 | tf_op jit(solution)/shard_map/ppermute | solution.py:854
  97.4 5.0 %first.1 = (f32[2,12,40,128]{3,2,1,0:T(8,128)}, f32[2,34,40,128]{3,2,1,0:T(8,128)}, f32[2,12,40,128]{3,2,1,0:T(8,128)}, f32[10,24,128]{2,1,0:T(8,128)S(1)}, f32[...) custom-call(f32[2,8,40,128]{3,2,1,0:T(8,128)S(1)} %get-tuple-element.57.own, ...), custom_call_target="tpu_custom_call" | custom-call | tf_op jit(solution)/shard_map/first/pallas_call | solution.py:829
  102.5 25.3 %all_to_all.21.gathered = f32[64,16,128]{2,1,0:T(8,128)S(1)} all-to-all(f32[64,16,128]{2,1,0:T(8,128)S(1)} %get-tuple-element.60), channel_id=1, replica_groups=mesh['case'=2,'space'=64] {'space'}, dimensions={0} | all-to-all | bytes 1048576 | tf_op jit(solution)/shard_map/all_to_all | solution.py:859
  127.7 5.6 %up.3 = (f32[2,8,40,128]{3,2,1,0:T(8,128)S(1)}, f32[2,5,40,128]{3,2,1,0:T(8,128)S(1)}, f32[2,5,40,128]{3,2,1,0:T(8,128)S(1)}, f32[8,128]{1,0:T(8,128)S(1)}) custom-call(s32[1]{0:T(128)} %bitcast.me.me_ref, f32[64,16,128]{2,1,0:T(8,128)S(1)} %all_to_all.21.gathered, f32[2,34,40,128]{3,2,1,0:T(8,128)} %get-tuple-element.61.r_hbm.w0_hbm, ...), custom_call_target="tpu_custom_call" | custom-call | tf_op jit(solution)/shard_map/up/pallas_call | solution.py:829
  133.3 1.3 collective-permute-start.13
  134.6 4.0 %collective-permute-start.12 = (f32[2,8,40,128]{3,2,1,0:T(8,128)S(1)}, f32[2,8,40,128]{3,2,1,0:T(8,128)S(1)}, u32[]{:S(2)}, u32[]{:S(2)}) collective-permute-start(f32[2,8,40,128]{3,2,1,0:T(8,128)S(1)} %get-tuple-element.67.own), channel_id=1, source_target_pairs={{0,1},{1,2},{2,3},{3,4},{4,5},{5,6},{6,7},{7,8},{8,9},{9,10},{10,1... | collective-permute-start | bytes 983048 | tf_op jit(solution)/shard_map/ppermute | solution.py:852
  138.6 2.7 %collective-permute-start.14 = (f32[2,5,40,128]{3,2,1,0:T(8,128)S(1)}, f32[2,5,40,128]{3,2,1,0:T(8,128)S(1)}, u32[]{:S(2)}, u32[]{:S(2)}) collective-permute-start(f32[2,5,40,128]{3,2,1,0:T(8,128)S(1)} %get-tuple-element.68), channel_id=1, source_target_pairs={{0,2},{1,3},{2,4},{3,5},{4,6},{5,7},{6,8},{7,9},{8,10},{9,11},{10,... | collective-permute-start | bytes 614408 | tf_op jit(solution)/shard_map/ppermute | solution.py:854
  141.3 1.3 collective-permute-start.15
  142.6 4.2 %collective-permute-done.14.before2 = f32[2,5,40,128]{3,2,1,0:T(8,128)S(1)} collective-permute-done((f32[2,5,40,128]{3,2,1,0:T(8,128)S(1)}, f32[2,5,40,128]{3,2,1,0:T(8,128)S(1)}, u32[]{:S(2)}, u32[]{:S(2)}) %collective-permute-start.14) | collective-permute-done | bytes 204832 | tf_op jit(solution)/shard_map/ppermute | solution.py:854
  146.9 2.7 %collective-permute-done.15.after2 = f32[2,5,40,128]{3,2,1,0:T(8,128)S(1)} collective-permute-done((f32[2,5,40,128]{3,2,1,0:T(8,128)S(1)}, f32[2,5,40,128]{3,2,1,0:T(8,128)S(1)}, u32[]{:S(2)}, u32[]{:S(2)}) %collective-permute-start.15) | collective-permute-done | bytes 204832 | tf_op jit(solution)/shard_map/ppermute | solution.py:855
  149.6 7.3 %second.1 = (f32[2,12,40,128]{3,2,1,0:T(8,128)}, f32[2,12,40,128]{3,2,1,0:T(8,128)}, f32[2,34,40,128]{3,2,1,0:T(8,128)}, f32[2,8,40,128]{3,2,1,0:T(8,128)}, f32[...) custom-call(f32[2,8,40,128]{3,2,1,0:T(8,128)S(1)} %get-tuple-element, ...), custom_call_target="tpu_custom_call" | custom-call | tf_op jit(solution)/shard_map/second/pallas_call | solution.py:829
  156.9 25.6 %all_to_all.22.gathered = f32[64,16,128]{2,1,0:T(8,128)S(1)} all-to-all(f32[64,16,128]{2,1,0:T(8,128)S(1)} %get-tuple-element.72), channel_id=1, replica_groups=mesh['case'=2,'space'=64] {'space'}, dimensions={0} | all-to-all | bytes 1048576 | tf_op jit(solution)/shard_map/all_to_all | solution.py:859
  182.5 7.1 %third.1 = (f32[2,12,40,128]{3,2,1,0:T(8,128)S(1)}, f32[2,12,40,128]{3,2,1,0:T(8,128)S(1)}, f32[2,12,40,128]{3,2,1,0:T(8,128)S(1)}, f32[64,8,128]{2,1,0:T(8,128)S(1)}, f32[8,128]{1,0:T(8,128)S(1)}) custom-call(s32[1]{0:T(128)} %bitcast.me.me_ref, f32[64,16,128]{2,1,0:T(8,128)S(1)} %all_to_all.22.gathered, f32[8,128]{1,0:T(8,128)S(1)} %get-tuple-element.70.dots0, ...), custom_call_target="tpu_custom_call" | custom-call | tf_op jit(solution)/shard_map/third/pallas_call | solution.py:829
  189.7 13.9 %all_to_all.23.gathered = f32[64,8,128]{2,1,0:T(8,128)S(1)} all-to-all(f32[64,8,128]{2,1,0:T(8,128)S(1)} %get-tuple-element.80), channel_id=1, replica_groups=mesh['case'=2,'space'=64] {'space'}, dimensions={0} | all-to-all | bytes 524288 | tf_op jit(solution)/shard_map/all_to_all | solution.py:859
  203.6 1.5 last.1
  205.1 4.3 %collective-permute-start.16 = (f32[10,40,128]{2,1,0:T(8,128)S(1)}, f32[10,40,128]{2,1,0:T(8,128)S(1)}, u32[]{:S(2)}, u32[]{:S(2)}) collective-permute-start(f32[10,40,128]{2,1,0:T(8,128)S(1)} %get-tuple-element.88.mine), channel_id=1, source_target_pairs={{0,64},{64,0},{1,65},{65,1},{2,66},{66,2},{3,67},{67,3},{4,68},{68... | collective-permute-start | bytes 614408 | tf_op jit(solution)/shard_map/ppermute | solution.py:961
  209.4 1.1 collective-permute-done.16.other
  (46 shorter events, 6.2 us)
Async XLA Ops:
  0.6 0.9 copy-start.2
  1.6 0.9 copy-start.7
  2.5 0.9 copy-start.8
  3.5 21.9 %collective-permute-start.1 = (f32[12,40,128]{2,1,0:T(8,128)S(1)}, f32[12,40,128]{2,1,0:T(8,128)S(1)}, u32[]{:S(2)}, u32[]{:S(2)}) collective-permute-start(f32[12,40,128]{2,1,0:T(8,128)S(1)} %get-tuple-element.47), channel_id=1, source_target_pairs={{1,0},{2,1},{3,2},{4,3},{5,4},{6,5},{7,6},{8,7},{9,8},{10,9},{11,1... | collective-permute-start | bytes 737288 | tf_op jit(solution)/shard_map/ppermute | solution.py:853
  4.8 20.6 %collective-permute-start = (f32[12,40,128]{2,1,0:T(8,128)S(1)}, f32[12,40,128]{2,1,0:T(8,128)S(1)}, u32[]{:S(2)}, u32[]{:S(2)}) collective-permute-start(f32[12,40,128]{2,1,0:T(8,128)S(1)} %get-tuple-element.47), channel_id=1, source_target_pairs={{0,1},{1,2},{2,3},{3,4},{4,5},{5,6},{6,7},{7,8},{8,9},{9,10},{10,1... | collective-permute-start | bytes 737288 | tf_op jit(solution)/shard_map/ppermute | solution.py:852
  9.8 7.6 %collective-permute-start.2 = (f32[8,40,128]{2,1,0:T(8,128)S(1)}, f32[8,40,128]{2,1,0:T(8,128)S(1)}, u32[]{:S(2)}, u32[]{:S(2)}) collective-permute-start(f32[8,40,128]{2,1,0:T(8,128)S(1)} %get-tuple-element.48), channel_id=1, source_target_pairs={{0,2},{1,3},{2,4},{3,5},{4,6},{5,7},{6,8},{7,9},{8,10},{9,11},{10,... | collective-permute-start | bytes 491528 | tf_op jit(solution)/shard_map/ppermute | solution.py:854
  15.1 7.6 %collective-permute-start.3 = (f32[8,40,128]{2,1,0:T(8,128)S(1)}, f32[8,40,128]{2,1,0:T(8,128)S(1)}, u32[]{:S(2)}, u32[]{:S(2)}) collective-permute-start(f32[8,40,128]{2,1,0:T(8,128)S(1)} %get-tuple-element.49), channel_id=1, source_target_pairs={{2,0},{3,1},{4,2},{5,3},{6,4},{7,5},{8,6},{9,7},{10,8},{11,9},{12,... | collective-permute-start | bytes 491528 | tf_op jit(solution)/shard_map/ppermute | solution.py:855
  17.4 18.0 %collective-permute-start.6 = (f32[8,40,128]{2,1,0:T(8,128)S(1)}, f32[8,40,128]{2,1,0:T(8,128)S(1)}, u32[]{:S(2)}, u32[]{:S(2)}) collective-permute-start(f32[8,40,128]{2,1,0:T(8,128)S(1)} %collective-permute-done.2.before2), channel_id=1, source_target_pairs={{0,64},{64,0},{1,65},{65,1},{2,66},{66,2},{3,67},{67,3},{4,68},{68... | collective-permute-start | bytes 491528 | tf_op jit(solution)/shard_map/ppermute | solution.py:891
  22.7 12.7 %collective-permute-start.7 = (f32[8,40,128]{2,1,0:T(8,128)S(1)}, f32[8,40,128]{2,1,0:T(8,128)S(1)}, u32[]{:S(2)}, u32[]{:S(2)}) collective-permute-start(f32[8,40,128]{2,1,0:T(8,128)S(1)} %collective-permute-done.3.after2), channel_id=1, source_target_pairs={{0,64},{64,0},{1,65},{65,1},{2,66},{66,2},{3,67},{67,3},{4,68},{68... | collective-permute-start | bytes 491528 | tf_op jit(solution)/shard_map/ppermute | solution.py:891
  25.4 10.1 %collective-permute-start.5 = (f32[12,40,128]{2,1,0:T(8,128)S(1)}, f32[12,40,128]{2,1,0:T(8,128)S(1)}, u32[]{:S(2)}, u32[]{:S(2)}) collective-permute-start(f32[12,40,128]{2,1,0:T(8,128)S(1)} %collective-permute-done.1.after), channel_id=1, source_target_pairs={{0,64},{64,0},{1,65},{65,1},{2,66},{66,2},{3,67},{67,3},{4,68},{68... | collective-permute-start | bytes 737288 | tf_op jit(solution)/shard_map/ppermute | solution.py:891
  25.4 10.1 %collective-permute-start.4 = (f32[12,40,128]{2,1,0:T(8,128)S(1)}, f32[12,40,128]{2,1,0:T(8,128)S(1)}, u32[]{:S(2)}, u32[]{:S(2)}) collective-permute-start(f32[12,40,128]{2,1,0:T(8,128)S(1)} %collective-permute-done.before), channel_id=1, source_target_pairs={{0,64},{64,0},{1,65},{65,1},{2,66},{66,2},{3,67},{67,3},{4,68},{68... | collective-permute-start | bytes 737288 | tf_op jit(solution)/shard_map/ppermute | solution.py:891
  25.9 0.8 copy-start.9
  74.7 22.7 %slice-start = ((s8[4874240]{0:T(1024)(128)(4,1)}), s8[4194304]{0:T(1024)(128)(4,1)S(1)}, s32[]{:S(2)}) async-start(s8[4874240]{0:T(1024)(128)(4,1)} %bitcast.2), calls=%async_computation.4 | async-start | bytes 8388608
  74.7 22.7 %slice-start.1 = ((s8[4874240]{0:T(1024)(128)(4,1)}), s8[679936]{0:T(1024)(128)(4,1)S(1)}, s32[]{:S(2)}) async-start(s8[4874240]{0:T(1024)(128)(4,1)} %bitcast.2), calls=%async_computation.5 | async-start | bytes 1359872
  74.7 22.7 %copy-start = (f32[8,16,24,128]{3,2,1,0:T(8,128)S(1)}, f32[8,16,24,128]{3,2,1,0:T(8,128)}, u32[]{:S(2)}) copy-start(f32[8,16,24,128]{3,2,1,0:T(8,128)} %get-tuple-element.56.c1_hbm.c1) | copy-start | bytes 4718596
  80.6 16.8 %collective-permute-start.9 = (f32[2,8,40,128]{3,2,1,0:T(8,128)S(1)}, f32[2,8,40,128]{3,2,1,0:T(8,128)S(1)}, u32[]{:S(2)}, u32[]{:S(2)}) collective-permute-start(f32[2,8,40,128]{3,2,1,0:T(8,128)S(1)} %get-tuple-element.57.own), channel_id=1, source_target_pairs={{1,0},{2,1},{3,2},{4,3},{5,4},{6,5},{7,6},{8,7},{9,8},{10,9},{11,1... | collective-permute-start | bytes 983048 | tf_op jit(solution)/shard_map/ppermute | solution.py:853
  81.9 15.5 %collective-permute-start.8 = (f32[2,8,40,128]{3,2,1,0:T(8,128)S(1)}, f32[2,8,40,128]{3,2,1,0:T(8,128)S(1)}, u32[]{:S(2)}, u32[]{:S(2)}) collective-permute-start(f32[2,8,40,128]{3,2,1,0:T(8,128)S(1)} %get-tuple-element.57.own), channel_id=1, source_target_pairs={{0,1},{1,2},{2,3},{3,4},{4,5},{5,6},{6,7},{7,8},{8,9},{9,10},{10,1... | collective-permute-start | bytes 983048 | tf_op jit(solution)/shard_map/ppermute | solution.py:852
  85.9 11.4 %collective-permute-start.10 = (f32[2,5,40,128]{3,2,1,0:T(8,128)S(1)}, f32[2,5,40,128]{3,2,1,0:T(8,128)S(1)}, u32[]{:S(2)}, u32[]{:S(2)}) collective-permute-start(f32[2,5,40,128]{3,2,1,0:T(8,128)S(1)} %get-tuple-element.58), channel_id=1, source_target_pairs={{0,2},{1,3},{2,4},{3,5},{4,6},{5,7},{6,8},{7,9},{8,10},{9,11},{10,... | collective-permute-start | bytes 614408 | tf_op jit(solution)/shard_map/ppermute | solution.py:854
  88.8 8.6 %collective-permute-start.11 = (f32[2,5,40,128]{3,2,1,0:T(8,128)S(1)}, f32[2,5,40,128]{3,2,1,0:T(8,128)S(1)}, u32[]{:S(2)}, u32[]{:S(2)}) collective-permute-start(f32[2,5,40,128]{3,2,1,0:T(8,128)S(1)} %get-tuple-element.59), channel_id=1, source_target_pairs={{2,0},{3,1},{4,2},{5,3},{6,4},{7,5},{8,6},{9,7},{10,8},{11,9},{12,... | collective-permute-start | bytes 614408 | tf_op jit(solution)/shard_map/ppermute | solution.py:855
  127.7 21.8 %slice-start.2 = ((s8[4874240]{0:T(1024)(128)(4,1)}), s8[4194304]{0:T(1024)(128)(4,1)S(1)}, s32[]{:S(2)}) async-start(s8[4874240]{0:T(1024)(128)(4,1)} %bitcast.4), calls=%async_computation.6 | async-start | bytes 8388608
  127.7 21.8 %slice-start.3 = ((s8[4874240]{0:T(1024)(128)(4,1)}), s8[679936]{0:T(1024)(128)(4,1)S(1)}, s32[]{:S(2)}) async-start(s8[4874240]{0:T(1024)(128)(4,1)} %bitcast.4), calls=%async_computation.7 | async-start | bytes 1359872
  127.7 21.8 %copy-start.1 = (f32[8,16,24,128]{3,2,1,0:T(8,128)S(1)}, f32[8,16,24,128]{3,2,1,0:T(8,128)}, u32[]{:S(2)}) copy-start(f32[8,16,24,128]{3,2,1,0:T(8,128)} %get-tuple-element.56.c1_hbm.c1) | copy-start | bytes 4718596
  133.3 16.3 %collective-permute-start.13 = (f32[2,8,40,128]{3,2,1,0:T(8,128)S(1)}, f32[2,8,40,128]{3,2,1,0:T(8,128)S(1)}, u32[]{:S(2)}, u32[]{:S(2)}) collective-permute-start(f32[2,8,40,128]{3,2,1,0:T(8,128)S(1)} %get-tuple-element.67.own), channel_id=1, source_target_pairs={{1,0},{2,1},{3,2},{4,3},{5,4},{6,5},{7,6},{8,7},{9,8},{10,9},{11,1... | collective-permute-start | bytes 983048 | tf_op jit(solution)/shard_map/ppermute | solution.py:853
  134.6 15.0 %collective-permute-start.12 = (f32[2,8,40,128]{3,2,1,0:T(8,128)S(1)}, f32[2,8,40,128]{3,2,1,0:T(8,128)S(1)}, u32[]{:S(2)}, u32[]{:S(2)}) collective-permute-start(f32[2,8,40,128]{3,2,1,0:T(8,128)S(1)} %get-tuple-element.67.own), channel_id=1, source_target_pairs={{0,1},{1,2},{2,3},{3,4},{4,5},{5,6},{6,7},{7,8},{8,9},{9,10},{10,1... | collective-permute-start | bytes 983048 | tf_op jit(solution)/shard_map/ppermute | solution.py:852
  138.6 8.2 %collective-permute-start.14 = (f32[2,5,40,128]{3,2,1,0:T(8,128)S(1)}, f32[2,5,40,128]{3,2,1,0:T(8,128)S(1)}, u32[]{:S(2)}, u32[]{:S(2)}) collective-permute-start(f32[2,5,40,128]{3,2,1,0:T(8,128)S(1)} %get-tuple-element.68), channel_id=1, source_target_pairs={{0,2},{1,3},{2,4},{3,5},{4,6},{5,7},{6,8},{7,9},{8,10},{9,11},{10,... | collective-permute-start | bytes 614408 | tf_op jit(solution)/shard_map/ppermute | solution.py:854
  141.3 8.2 %collective-permute-start.15 = (f32[2,5,40,128]{3,2,1,0:T(8,128)S(1)}, f32[2,5,40,128]{3,2,1,0:T(8,128)S(1)}, u32[]{:S(2)}, u32[]{:S(2)}) collective-permute-start(f32[2,5,40,128]{3,2,1,0:T(8,128)S(1)} %get-tuple-element.69), channel_id=1, source_target_pairs={{2,0},{3,1},{4,2},{5,3},{6,4},{7,5},{8,6},{9,7},{10,8},{11,9},{12,... | collective-permute-start | bytes 614408 | tf_op jit(solution)/shard_map/ppermute | solution.py:855
  182.5 21.0 %copy-start.4 = (f32[12,40,128]{2,1,0:T(8,128)S(1)}, f32[12,40,128]{2,1,0:T(8,128)}, u32[]{:S(2)}) copy-start(f32[12,40,128]{2,1,0:T(8,128)} %get-tuple-element.85.mod) | copy-start | bytes 737284
  182.5 21.0 %copy-start.5 = (f32[12,40,128]{2,1,0:T(8,128)S(1)}, f32[12,40,128]{2,1,0:T(8,128)}, u32[]{:S(2)}) copy-start(f32[12,40,128]{2,1,0:T(8,128)} %get-tuple-element.86.free) | copy-start | bytes 737284
  189.7 20.8 %copy-start.3 = (s32[8,40,128]{2,1,0:T(8,128)S(1)}, s32[8,40,128]{2,1,0:T(8,128)}, u32[]{:S(2)}) copy-start(s32[8,40,128]{2,1,0:T(8,128)} %passive.3) | copy-start | bytes 491524
  189.7 20.8 %copy-start.6 = (f32[10,40,128]{2,1,0:T(8,128)S(1)}, f32[10,40,128]{2,1,0:T(8,128)}, u32[]{:S(2)}) copy-start(f32[10,40,128]{2,1,0:T(8,128)} %get-tuple-element.89.scale) | copy-start | bytes 614404
  205.1 5.4 %collective-permute-start.16 = (f32[10,40,128]{2,1,0:T(8,128)S(1)}, f32[10,40,128]{2,1,0:T(8,128)S(1)}, u32[]{:S(2)}, u32[]{:S(2)}) collective-permute-start(f32[10,40,128]{2,1,0:T(8,128)S(1)} %get-tuple-element.88.mine), channel_id=1, source_target_pairs={{0,64},{64,0},{1,65},{65,1},{2,66},{66,2},{3,67},{67,3},{4,68},{68... | collective-permute-start | bytes 614408 | tf_op jit(solution)/shard_map/ppermute | solution.py:961

commit v3 on v2

--- a/solution.py
+++ b/solution.py
@@ -313,7 +313,13 @@
 NEAR, AWAY = 3 * BLOCK, 3 * NEXT + 1
 
 
-def collect_kernel(case_ref, design, passive, fixed, own, near, head, tail, all_head, all_tail):
+def collect_kernel(
+    case_ref, design_hbm, passive_hbm, fixed_hbm, own, near, head, tail, all_head, all_tail, design, passive, fixed, sems
+):
+    pairs = ((design_hbm, design), (passive_hbm, passive), (fixed_hbm, fixed))
+    copies = [copy_in(a, b, sems.at[i]) for i, (a, b) in enumerate(pairs)]
+    for copy in copies:
+        copy.wait()
     at = 0
     for k, source in enumerate((design, passive, fixed)):
         value = source[...].astype(F32)
@@ -822,7 +828,7 @@
 
 def call(body, outs, scratch, args, name, sems=0, cost=None):
     pairs = [a if isinstance(a, tuple) else (a, pltpu.VMEM) for a in args]
-    scratches = [pltpu.VMEM(s, F32) for s in scratch]
+    scratches = [pltpu.VMEM(s, F32) if isinstance(s, tuple) else s for s in scratch]
     if sems:
         scratches.append(pltpu.SemaphoreType.DMA((sems,)))
     given = [pltpu.with_memory_space_constraint(a, m) if m is pltpu.HBM else a for a, m in pairs]
@@ -848,12 +854,8 @@
     def two_either_side(own, head, tail):
         skip = [(i, i + 2) for i in range(members - 2)]
         skip_back = [(i + 2, i) for i in range(members - 2)]
-        return (
-            lax.ppermute(own, "space", ahead),
-            lax.ppermute(own, "space", back),
-            lax.ppermute(tail, "space", skip),
-            lax.ppermute(head, "space", skip_back),
-        )
+        away = lax.ppermute(tail, "space", skip), lax.ppermute(head, "space", skip_back)
+        return (lax.ppermute(own, "space", ahead), lax.ppermute(own, "space", back)) + away
 
     def gather(tiles):
         return lax.all_to_all(tiles, "space", 0, 0)
@@ -883,12 +885,12 @@
     own, near, head, tail = call(
         collect_kernel,
         [vmem(NEAR, *plane), vmem(NEAR // 2, *plane), vmem(AWAY // 2, *plane), vmem(AWAY // 2, *plane)],
-        [(AWAY,) + plane] * 2,
-        (case_ref, design, passive, fixed_mask),
+        [(AWAY,) + plane] * 2 + [pltpu.VMEM((BLOCK,) + plane, x.dtype) for x in (design, passive, fixed_mask)],
+        (case_ref, far(design), far(passive), far(fixed_mask)),
         "collect",
+        3,
     )
     listened = two_either_side(near, head, tail)
-    listened += tuple(lax.ppermute(x, "case", [(0, 1), (1, 0)]) for x in listened)
     counts = call(
         count_kernel,
         [vmem(*window)],
@@ -897,6 +899,8 @@
         "counts",
         cost=pl.CostEstimate(flops=3 * 10**10, bytes_accessed=10**7, transcendentals=0),
     )[0]
+    listened, counts = lax.optimization_barrier((listened, counts))
+    listened += tuple(lax.ppermute(x, "case", [(0, 1), (1, 0)]) for x in listened)
     c0, c1, force, s2, s21, r1, talk, mod, free, scale = call(
         functools.partial(setup_kernel, members),
         [hbm(COUNT0, WINDOW, *plane), hbm(COUNT, Q1, R1, 128), hbm(*window)]

time: 212 us -> 205 us (0.967)
  starting transfers between devices: 41.5 us -> 38.3 us
  waiting for transfers between devices: 19.2 us -> 16.2 us
  local copies, waits for them, and re-layouts: 3.54 us -> 0.79 us
    ppermute x4, starting transfers between devices: 5.32 us -> 2.2 us  [on_device(): lax.ppermute(x, 'case', [(0, 1), (1, 0)])]
    ppermute x3, waiting for transfers between devices: 5.82 us -> 2.75 us  [two_either_side(): lax.ppermute(head, 'space', skip_back)]
    unnamed x28 -> x22, local copies, waits for them, and re-layouts: 3.54 us -> 0.79 us
where the time goes in v3:
time: 205 us; the launch traced here: 204 us
  blocking collectives  95 us (46%)
  Pallas kernels  53.1 us (26%)
  starting transfers between devices  38.3 us (19%)
  waiting for transfers between devices  16.2 us (8%)
    all_to_all x4, blocking collectives, gather(): return lax.all_to_all(tiles, 'space', 0, 0)  95 us
    pallas_call x10, Pallas kernels, call(): pl.pallas_call(body, out_shape=[o for o, _ in outs], in_specs=[pl.BlockSp...  53.1 us
    ppermute x3, starting transfers between devices, two_either_side(): lax.ppermute(own, 'space', ahead)  13 us
    ppermute x3, waiting for transfers between devices, two_either_side(): lax.ppermute(tail, 'space', skip)  11 us
    ppermute x3, starting transfers between devices, two_either_side(): lax.ppermute(tail, 'space', skip)  10.8 us
    ppermute x1, starting transfers between devices, on_device(): other = lax.ppermute(energy, 'case', [(0, 1), (1, 0)])  4.34 us
  transfers between devices with their start and end apart: 17, of which 6 were waited for; matrix products, arithmetic and copies ran while one was open for 0% of the time, Pallas kernels for 4%

profile of v3, /device:TPU:1, one launch (start us, length us, event | category | flops | bytes accessed | tf_op | source)
XLA Modules:
  0.0 204.3 jit_solution(6821850746334241535)
XLA Ops:
  0.6 1.2 collect.1
  1.9 1.3 collective-permute-start.1
  3.2 5.0 %collective-permute-start = (f32[12,40,128]{2,1,0:T(8,128)S(1)}, f32[12,40,128]{2,1,0:T(8,128)S(1)}, u32[]{:S(2)}, u32[]{:S(2)}) collective-permute-start(f32[12,40,128]{2,1,0:T(8,128)S(1)} %get-tuple-element.52), channel_id=1, source_target_pairs={{0,1},{1,2},{2,3},{3,4},{4,5},{5,6},{6,7},{7,8},{8,9},{9,10},{10,1... | collective-permute-start | bytes 737288 | tf_op jit(solution)/shard_map/ppermute | solution.py:858
  8.2 5.3 %collective-permute-start.2 = (f32[8,40,128]{2,1,0:T(8,128)S(1)}, f32[8,40,128]{2,1,0:T(8,128)S(1)}, u32[]{:S(2)}, u32[]{:S(2)}) collective-permute-start(f32[8,40,128]{2,1,0:T(8,128)S(1)} %get-tuple-element.53), channel_id=1, source_target_pairs={{0,2},{1,3},{2,4},{3,5},{4,6},{5,7},{6,8},{7,9},{8,10},{9,11},{10,... | collective-permute-start | bytes 491528 | tf_op jit(solution)/shard_map/ppermute | solution.py:857
  13.5 1.3 collective-permute-start.3
  15.6 8.7 %counts.1 = f32[2,34,40,128]{3,2,1,0:T(8,128)S(1)} custom-call(s32[1]{0:T(128)} %bitcast.me.me_ref, s32[2,4096]{1,0:T(2,128)S(1)} %copy-done.6), custom_call_target="tpu_custom_call" | custom-call | flops 30000001024 | bytes 10000000 | tf_op jit(solution)/shard_map/counts/pallas_call | solution.py:835
  24.4 1.6 collective-permute-start.4
  26.6 1.1 collective-permute-done.6.o_before2
  27.9 9.6 %setup.1 = (f32[7,34,40,128]{3,2,1,0:T(8,128)}, f32[8,16,24,128]{3,2,1,0:T(8,128)}, f32[2,34,40,128]{3,2,1,0:T(8,128)}, f32[2,12,40,128]{3,2,1,0:T(8,128)}, f32[...) custom-call(s32[1]{0:T(128)} %bitcast.me.me_ref, ...), custom_call_target="tpu_custom_call" | custom-call | tf_op jit(solution)/shard_map/setup/pallas_call | solution.py:835
  37.6 30.1 %all_to_all.20.gathered = f32[64,24,128]{2,1,0:T(8,128)S(1)} all-to-all(f32[64,24,128]{2,1,0:T(8,128)S(1)} %get-tuple-element.60), channel_id=1, replica_groups=mesh['case'=2,'space'=64] {'space'}, dimensions={0} | all-to-all | bytes 1572864 | tf_op jit(solution)/shard_map/all_to_all | solution.py:861
  67.6 5.9 %up.2 = (f32[2,8,40,128]{3,2,1,0:T(8,128)S(1)}, f32[2,5,40,128]{3,2,1,0:T(8,128)S(1)}, f32[2,5,40,128]{3,2,1,0:T(8,128)S(1)}, f32[8,23,16,128]{3,2,1,0:T(8,128)S(1)}, f32[8,23,8,128]{3,2,1,0:T(8,128)S(1)}) custom-call(s32[1]{0:T(128)} %bitcast.me.me_ref, f32[64,24,128]{2,1,0:T(8,128)S(1)} %all_to_all.20.gathered, ...), custom_call_target="tpu_custom_call" | custom-call | tf_op jit(solution)/shard_map/up/pallas_call | solution.py:835
  73.5 1.3 collective-permute-start.9
  74.8 4.0 %collective-permute-start.8 = (f32[2,8,40,128]{3,2,1,0:T(8,128)S(1)}, f32[2,8,40,128]{3,2,1,0:T(8,128)S(1)}, u32[]{:S(2)}, u32[]{:S(2)}) collective-permute-start(f32[2,8,40,128]{3,2,1,0:T(8,128)S(1)} %get-tuple-element.67.own), channel_id=1, source_target_pairs={{0,1},{1,2},{2,3},{3,4},{4,5},{5,6},{6,7},{7,8},{8,9},{9,10},{10,1... | collective-permute-start | bytes 983048 | tf_op jit(solution)/shard_map/ppermute | solution.py:858
  78.8 2.8 %collective-permute-start.10 = (f32[2,5,40,128]{3,2,1,0:T(8,128)S(1)}, f32[2,5,40,128]{3,2,1,0:T(8,128)S(1)}, u32[]{:S(2)}, u32[]{:S(2)}) collective-permute-start(f32[2,5,40,128]{3,2,1,0:T(8,128)S(1)} %get-tuple-element.68), channel_id=1, source_target_pairs={{0,2},{1,3},{2,4},{3,5},{4,6},{5,7},{6,8},{7,9},{8,10},{9,11},{10,... | collective-permute-start | bytes 614408 | tf_op jit(solution)/shard_map/ppermute | solution.py:857
  81.6 1.5 collective-permute-start.11
  83.1 6.8 %collective-permute-done.10.before2 = f32[2,5,40,128]{3,2,1,0:T(8,128)S(1)} collective-permute-done((f32[2,5,40,128]{3,2,1,0:T(8,128)S(1)}, f32[2,5,40,128]{3,2,1,0:T(8,128)S(1)}, u32[]{:S(2)}, u32[]{:S(2)}) %collective-permute-start.10) | collective-permute-done | bytes 204832 | tf_op jit(solution)/shard_map/ppermute | solution.py:857
  90.0 5.0 %first.1 = (f32[2,12,40,128]{3,2,1,0:T(8,128)}, f32[2,34,40,128]{3,2,1,0:T(8,128)}, f32[2,12,40,128]{3,2,1,0:T(8,128)}, f32[10,24,128]{2,1,0:T(8,128)S(1)}, f32[...) custom-call(f32[2,8,40,128]{3,2,1,0:T(8,128)S(1)} %get-tuple-element.67.own, ...), custom_call_target="tpu_custom_call" | custom-call | tf_op jit(solution)/shard_map/first/pallas_call | solution.py:835
  95.0 25.5 %all_to_all.21.gathered = f32[64,16,128]{2,1,0:T(8,128)S(1)} all-to-all(f32[64,16,128]{2,1,0:T(8,128)S(1)} %get-tuple-element.70), channel_id=1, replica_groups=mesh['case'=2,'space'=64] {'space'}, dimensions={0} | all-to-all | bytes 1048576 | tf_op jit(solution)/shard_map/all_to_all | solution.py:861
  120.5 5.6 %up.3 = (f32[2,8,40,128]{3,2,1,0:T(8,128)S(1)}, f32[2,5,40,128]{3,2,1,0:T(8,128)S(1)}, f32[2,5,40,128]{3,2,1,0:T(8,128)S(1)}, f32[8,128]{1,0:T(8,128)S(1)}) custom-call(s32[1]{0:T(128)} %bitcast.me.me_ref, f32[64,16,128]{2,1,0:T(8,128)S(1)} %all_to_all.21.gathered, f32[2,34,40,128]{3,2,1,0:T(8,128)} %get-tuple-element.71.r_hbm.w0_hbm, ...), custom_call_target="tpu_custom_call" | custom-call | tf_op jit(solution)/shard_map/up/pallas_call | solution.py:835
  126.1 1.3 collective-permute-start.13
  127.4 4.0 %collective-permute-start.12 = (f32[2,8,40,128]{3,2,1,0:T(8,128)S(1)}, f32[2,8,40,128]{3,2,1,0:T(8,128)S(1)}, u32[]{:S(2)}, u32[]{:S(2)}) collective-permute-start(f32[2,8,40,128]{3,2,1,0:T(8,128)S(1)} %get-tuple-element.77.own), channel_id=1, source_target_pairs={{0,1},{1,2},{2,3},{3,4},{4,5},{5,6},{6,7},{7,8},{8,9},{9,10},{10,1... | collective-permute-start | bytes 983048 | tf_op jit(solution)/shard_map/ppermute | solution.py:858
  131.4 2.7 %collective-permute-start.14 = (f32[2,5,40,128]{3,2,1,0:T(8,128)S(1)}, f32[2,5,40,128]{3,2,1,0:T(8,128)S(1)}, u32[]{:S(2)}, u32[]{:S(2)}) collective-permute-start(f32[2,5,40,128]{3,2,1,0:T(8,128)S(1)} %get-tuple-element.78), channel_id=1, source_target_pairs={{0,2},{1,3},{2,4},{3,5},{4,6},{5,7},{6,8},{7,9},{8,10},{9,11},{10,... | collective-permute-start | bytes 614408 | tf_op jit(solution)/shard_map/ppermute | solution.py:857
  134.1 1.3 collective-permute-start.15
  135.4 4.2 %collective-permute-done.14.before2 = f32[2,5,40,128]{3,2,1,0:T(8,128)S(1)} collective-permute-done((f32[2,5,40,128]{3,2,1,0:T(8,128)S(1)}, f32[2,5,40,128]{3,2,1,0:T(8,128)S(1)}, u32[]{:S(2)}, u32[]{:S(2)}) %collective-permute-start.14) | collective-permute-done | bytes 204832 | tf_op jit(solution)/shard_map/ppermute | solution.py:857
  139.6 2.7 %collective-permute-done.15.after2 = f32[2,5,40,128]{3,2,1,0:T(8,128)S(1)} collective-permute-done((f32[2,5,40,128]{3,2,1,0:T(8,128)S(1)}, f32[2,5,40,128]{3,2,1,0:T(8,128)S(1)}, u32[]{:S(2)}, u32[]{:S(2)}) %collective-permute-start.15) | collective-permute-done | bytes 204832 | tf_op jit(solution)/shard_map/ppermute | solution.py:857
  142.4 7.3 %second.1 = (f32[2,12,40,128]{3,2,1,0:T(8,128)}, f32[2,12,40,128]{3,2,1,0:T(8,128)}, f32[2,34,40,128]{3,2,1,0:T(8,128)}, f32[2,8,40,128]{3,2,1,0:T(8,128)}, f32[...) custom-call(f32[2,8,40,128]{3,2,1,0:T(8,128)S(1)} %get-tuple-element, ...), custom_call_target="tpu_custom_call" | custom-call | tf_op jit(solution)/shard_map/second/pallas_call | solution.py:835
  149.7 25.6 %all_to_all.22.gathered = f32[64,16,128]{2,1,0:T(8,128)S(1)} all-to-all(f32[64,16,128]{2,1,0:T(8,128)S(1)} %get-tuple-element.82), channel_id=1, replica_groups=mesh['case'=2,'space'=64] {'space'}, dimensions={0} | all-to-all | bytes 1048576 | tf_op jit(solution)/shard_map/all_to_all | solution.py:861
  175.3 7.1 %third.1 = (f32[2,12,40,128]{3,2,1,0:T(8,128)S(1)}, f32[2,12,40,128]{3,2,1,0:T(8,128)S(1)}, f32[2,12,40,128]{3,2,1,0:T(8,128)S(1)}, f32[64,8,128]{2,1,0:T(8,128)S(1)}, f32[8,128]{1,0:T(8,128)S(1)}) custom-call(s32[1]{0:T(128)} %bitcast.me.me_ref, f32[64,16,128]{2,1,0:T(8,128)S(1)} %all_to_all.22.gathered, f32[8,128]{1,0:T(8,128)S(1)} %get-tuple-element.80.dots0, ...), custom_call_target="tpu_custom_call" | custom-call | tf_op jit(solution)/shard_map/third/pallas_call | solution.py:835
  182.5 13.8 %all_to_all.23.gathered = f32[64,8,128]{2,1,0:T(8,128)S(1)} all-to-all(f32[64,8,128]{2,1,0:T(8,128)S(1)} %get-tuple-element.90), channel_id=1, replica_groups=mesh['case'=2,'space'=64] {'space'}, dimensions={0} | all-to-all | bytes 524288 | tf_op jit(solution)/shard_map/all_to_all | solution.py:861
  196.3 1.5 last.1
  197.8 4.3 %collective-permute-start.16 = (f32[10,40,128]{2,1,0:T(8,128)S(1)}, f32[10,40,128]{2,1,0:T(8,128)S(1)}, u32[]{:S(2)}, u32[]{:S(2)}) collective-permute-start(f32[10,40,128]{2,1,0:T(8,128)S(1)} %get-tuple-element.98.mine), channel_id=1, source_target_pairs={{0,64},{64,0},{1,65},{65,1},{2,66},{66,2},{3,67},{67,3},{4,68},{68... | collective-permute-start | bytes 614408 | tf_op jit(solution)/shard_map/ppermute | solution.py:965
  202.1 1.1 collective-permute-done.16.other
  (40 shorter events, 2.7 us)
Async XLA Ops:
  1.9 22.5 %collective-permute-start.1 = (f32[12,40,128]{2,1,0:T(8,128)S(1)}, f32[12,40,128]{2,1,0:T(8,128)S(1)}, u32[]{:S(2)}, u32[]{:S(2)}) collective-permute-start(f32[12,40,128]{2,1,0:T(8,128)S(1)} %get-tuple-element.52), channel_id=1, source_target_pairs={{1,0},{2,1},{3,2},{4,3},{5,4},{6,5},{7,6},{8,7},{9,8},{10,9},{11,1... | collective-permute-start | bytes 737288 | tf_op jit(solution)/shard_map/ppermute | solution.py:858
  3.2 21.2 %collective-permute-start = (f32[12,40,128]{2,1,0:T(8,128)S(1)}, f32[12,40,128]{2,1,0:T(8,128)S(1)}, u32[]{:S(2)}, u32[]{:S(2)}) collective-permute-start(f32[12,40,128]{2,1,0:T(8,128)S(1)} %get-tuple-element.52), channel_id=1, source_target_pairs={{0,1},{1,2},{2,3},{3,4},{4,5},{5,6},{6,7},{7,8},{8,9},{9,10},{10,1... | collective-permute-start | bytes 737288 | tf_op jit(solution)/shard_map/ppermute | solution.py:858
  8.2 16.1 %collective-permute-start.2 = (f32[8,40,128]{2,1,0:T(8,128)S(1)}, f32[8,40,128]{2,1,0:T(8,128)S(1)}, u32[]{:S(2)}, u32[]{:S(2)}) collective-permute-start(f32[8,40,128]{2,1,0:T(8,128)S(1)} %get-tuple-element.53), channel_id=1, source_target_pairs={{0,2},{1,3},{2,4},{3,5},{4,6},{5,7},{6,8},{7,9},{8,10},{9,11},{10,... | collective-permute-start | bytes 491528 | tf_op jit(solution)/shard_map/ppermute | solution.py:857
  13.5 10.8 %collective-permute-start.3 = (f32[8,40,128]{2,1,0:T(8,128)S(1)}, f32[8,40,128]{2,1,0:T(8,128)S(1)}, u32[]{:S(2)}, u32[]{:S(2)}) collective-permute-start(f32[8,40,128]{2,1,0:T(8,128)S(1)} %get-tuple-element.54), channel_id=1, source_target_pairs={{2,0},{3,1},{4,2},{5,3},{6,4},{7,5},{8,6},{9,7},{10,8},{11,9},{12,... | collective-permute-start | bytes 491528 | tf_op jit(solution)/shard_map/ppermute | solution.py:857
  14.8 0.8 copy-start.6
  24.4 3.6 %collective-permute-start.4 = (f32[12,40,128]{2,1,0:T(8,128)S(1)}, f32[12,40,128]{2,1,0:T(8,128)S(1)}, u32[]{:S(2)}, u32[]{:S(2)}) collective-permute-start(f32[12,40,128]{2,1,0:T(8,128)S(1)} %collective-permute-done.before), channel_id=1, source_target_pairs={{0,64},{64,0},{1,65},{65,1},{2,66},{66,2},{3,67},{67,3},{4,68},{68... | collective-permute-start | bytes 737288 | tf_op jit(solution)/shard_map/ppermute | solution.py:903
  26.0 2.0 collective-permute-start.5
  26.0 1.7 collective-permute-start.6
  26.5 1.5 collective-permute-start.7
  67.6 22.3 %slice-start = ((s8[4874240]{0:T(1024)(128)(4,1)}), s8[4194304]{0:T(1024)(128)(4,1)S(1)}, s32[]{:S(2)}) async-start(s8[4874240]{0:T(1024)(128)(4,1)} %bitcast.2), calls=%async_computation.4 | async-start | bytes 8388608
  67.6 22.3 %slice-start.1 = ((s8[4874240]{0:T(1024)(128)(4,1)}), s8[679936]{0:T(1024)(128)(4,1)S(1)}, s32[]{:S(2)}) async-start(s8[4874240]{0:T(1024)(128)(4,1)} %bitcast.2), calls=%async_computation.5 | async-start | bytes 1359872
  67.6 22.3 %copy-start = (f32[8,16,24,128]{3,2,1,0:T(8,128)S(1)}, f32[8,16,24,128]{3,2,1,0:T(8,128)}, u32[]{:S(2)}) copy-start(f32[8,16,24,128]{3,2,1,0:T(8,128)} %get-tuple-element.66.c1_hbm.c1) | copy-start | bytes 4718596
  73.5 16.4 %collective-permute-start.9 = (f32[2,8,40,128]{3,2,1,0:T(8,128)S(1)}, f32[2,8,40,128]{3,2,1,0:T(8,128)S(1)}, u32[]{:S(2)}, u32[]{:S(2)}) collective-permute-start(f32[2,8,40,128]{3,2,1,0:T(8,128)S(1)} %get-tuple-element.67.own), channel_id=1, source_target_pairs={{1,0},{2,1},{3,2},{4,3},{5,4},{6,5},{7,6},{8,7},{9,8},{10,9},{11,1... | collective-permute-start | bytes 983048 | tf_op jit(solution)/shard_map/ppermute | solution.py:858
  74.8 15.1 %collective-permute-start.8 = (f32[2,8,40,128]{3,2,1,0:T(8,128)S(1)}, f32[2,8,40,128]{3,2,1,0:T(8,128)S(1)}, u32[]{:S(2)}, u32[]{:S(2)}) collective-permute-start(f32[2,8,40,128]{3,2,1,0:T(8,128)S(1)} %get-tuple-element.67.own), channel_id=1, source_target_pairs={{0,1},{1,2},{2,3},{3,4},{4,5},{5,6},{6,7},{7,8},{8,9},{9,10},{10,1... | collective-permute-start | bytes 983048 | tf_op jit(solution)/shard_map/ppermute | solution.py:858
  78.8 11.1 %collective-permute-start.10 = (f32[2,5,40,128]{3,2,1,0:T(8,128)S(1)}, f32[2,5,40,128]{3,2,1,0:T(8,128)S(1)}, u32[]{:S(2)}, u32[]{:S(2)}) collective-permute-start(f32[2,5,40,128]{3,2,1,0:T(8,128)S(1)} %get-tuple-element.68), channel_id=1, source_target_pairs={{0,2},{1,3},{2,4},{3,5},{4,6},{5,7},{6,8},{7,9},{8,10},{9,11},{10,... | collective-permute-start | bytes 614408 | tf_op jit(solution)/shard_map/ppermute | solution.py:857
  81.6 8.3 %collective-permute-start.11 = (f32[2,5,40,128]{3,2,1,0:T(8,128)S(1)}, f32[2,5,40,128]{3,2,1,0:T(8,128)S(1)}, u32[]{:S(2)}, u32[]{:S(2)}) collective-permute-start(f32[2,5,40,128]{3,2,1,0:T(8,128)S(1)} %get-tuple-element.69), channel_id=1, source_target_pairs={{2,0},{3,1},{4,2},{5,3},{6,4},{7,5},{8,6},{9,7},{10,8},{11,9},{12,... | collective-permute-start | bytes 614408 | tf_op jit(solution)/shard_map/ppermute | solution.py:857
  120.5 21.8 %slice-start.2 = ((s8[4874240]{0:T(1024)(128)(4,1)}), s8[4194304]{0:T(1024)(128)(4,1)S(1)}, s32[]{:S(2)}) async-start(s8[4874240]{0:T(1024)(128)(4,1)} %bitcast.4), calls=%async_computation.6 | async-start | bytes 8388608
  120.5 21.8 %slice-start.3 = ((s8[4874240]{0:T(1024)(128)(4,1)}), s8[679936]{0:T(1024)(128)(4,1)S(1)}, s32[]{:S(2)}) async-start(s8[4874240]{0:T(1024)(128)(4,1)} %bitcast.4), calls=%async_computation.7 | async-start | bytes 1359872
  120.5 21.8 %copy-start.1 = (f32[8,16,24,128]{3,2,1,0:T(8,128)S(1)}, f32[8,16,24,128]{3,2,1,0:T(8,128)}, u32[]{:S(2)}) copy-start(f32[8,16,24,128]{3,2,1,0:T(8,128)} %get-tuple-element.66.c1_hbm.c1) | copy-start | bytes 4718596
  126.1 16.2 %collective-permute-start.13 = (f32[2,8,40,128]{3,2,1,0:T(8,128)S(1)}, f32[2,8,40,128]{3,2,1,0:T(8,128)S(1)}, u32[]{:S(2)}, u32[]{:S(2)}) collective-permute-start(f32[2,8,40,128]{3,2,1,0:T(8,128)S(1)} %get-tuple-element.77.own), channel_id=1, source_target_pairs={{1,0},{2,1},{3,2},{4,3},{5,4},{6,5},{7,6},{8,7},{9,8},{10,9},{11,1... | collective-permute-start | bytes 983048 | tf_op jit(solution)/shard_map/ppermute | solution.py:858
  127.4 14.9 %collective-permute-start.12 = (f32[2,8,40,128]{3,2,1,0:T(8,128)S(1)}, f32[2,8,40,128]{3,2,1,0:T(8,128)S(1)}, u32[]{:S(2)}, u32[]{:S(2)}) collective-permute-start(f32[2,8,40,128]{3,2,1,0:T(8,128)S(1)} %get-tuple-element.77.own), channel_id=1, source_target_pairs={{0,1},{1,2},{2,3},{3,4},{4,5},{5,6},{6,7},{7,8},{8,9},{9,10},{10,1... | collective-permute-start | bytes 983048 | tf_op jit(solution)/shard_map/ppermute | solution.py:858
  131.4 8.2 %collective-permute-start.14 = (f32[2,5,40,128]{3,2,1,0:T(8,128)S(1)}, f32[2,5,40,128]{3,2,1,0:T(8,128)S(1)}, u32[]{:S(2)}, u32[]{:S(2)}) collective-permute-start(f32[2,5,40,128]{3,2,1,0:T(8,128)S(1)} %get-tuple-element.78), channel_id=1, source_target_pairs={{0,2},{1,3},{2,4},{3,5},{4,6},{5,7},{6,8},{7,9},{8,10},{9,11},{10,... | collective-permute-start | bytes 614408 | tf_op jit(solution)/shard_map/ppermute | solution.py:857
  134.1 8.2 %collective-permute-start.15 = (f32[2,5,40,128]{3,2,1,0:T(8,128)S(1)}, f32[2,5,40,128]{3,2,1,0:T(8,128)S(1)}, u32[]{:S(2)}, u32[]{:S(2)}) collective-permute-start(f32[2,5,40,128]{3,2,1,0:T(8,128)S(1)} %get-tuple-element.79), channel_id=1, source_target_pairs={{2,0},{3,1},{4,2},{5,3},{6,4},{7,5},{8,6},{9,7},{10,8},{11,9},{12,... | collective-permute-start | bytes 614408 | tf_op jit(solution)/shard_map/ppermute | solution.py:857
  175.3 21.0 %copy-start.3 = (f32[12,40,128]{2,1,0:T(8,128)S(1)}, f32[12,40,128]{2,1,0:T(8,128)}, u32[]{:S(2)}) copy-start(f32[12,40,128]{2,1,0:T(8,128)} %get-tuple-element.95.mod) | copy-start | bytes 737284
  175.3 21.0 %copy-start.4 = (f32[12,40,128]{2,1,0:T(8,128)S(1)}, f32[12,40,128]{2,1,0:T(8,128)}, u32[]{:S(2)}) copy-start(f32[12,40,128]{2,1,0:T(8,128)} %get-tuple-element.96.free) | copy-start | bytes 737284
  182.4 20.8 %copy-start.2 = (s32[8,40,128]{2,1,0:T(8,128)S(1)}, s32[8,40,128]{2,1,0:T(8,128)}, u32[]{:S(2)}) copy-start(s32[8,40,128]{2,1,0:T(8,128)} %passive.1) | copy-start | bytes 491524
  182.5 20.8 %copy-start.5 = (f32[10,40,128]{2,1,0:T(8,128)S(1)}, f32[10,40,128]{2,1,0:T(8,128)}, u32[]{:S(2)}) copy-start(f32[10,40,128]{2,1,0:T(8,128)} %get-tuple-element.99.scale) | copy-start | bytes 614404
  197.8 5.4 %collective-permute-start.16 = (f32[10,40,128]{2,1,0:T(8,128)S(1)}, f32[10,40,128]{2,1,0:T(8,128)S(1)}, u32[]{:S(2)}, u32[]{:S(2)}) collective-permute-start(f32[10,40,128]{2,1,0:T(8,128)S(1)} %get-tuple-element.98.mine), channel_id=1, source_target_pairs={{0,64},{64,0},{1,65},{65,1},{2,66},{66,2},{3,67},{67,3},{4,68},{68... | collective-permute-start | bytes 614408 | tf_op jit(solution)/shard_map/ppermute | solution.py:965

commit v4 on v3

--- a/solution.py
+++ b/solution.py
@@ -38,9 +38,14 @@
 
 
 def dot(a, b):
-    return lax.dot_general(
-        a, b, (((1,), (0,)), ((), ())), precision=lax.Precision.HIGHEST, preferred_element_type=F32
-    )
+    b = b.astype(jnp.bfloat16)
+    out = None
+    for _ in range(3):
+        part = a.astype(jnp.bfloat16)
+        a = a - part.astype(F32)
+        product = lax.dot_general(part, b, (((1,), (0,)), ((), ())), preferred_element_type=F32)
+        out = product if out is None else out + product
+    return out
 
 
 def planes(lo, hi, body, group=8):
@@ -262,9 +267,11 @@
     return copy
 
 
-def count_kernel(me, index, out, acc):
+COUNT_ROWS = 8 * -(-WINDOW * NY // 32)
+
+
+def count_kernel(me, index, out, acc, flat):
     base = (me[0] * BLOCK - HALO) * NY
-    rows = WINDOW * NY
     chunk = 512
     total = index.shape[1]
     for case in range(2):
@@ -273,16 +280,18 @@
         def step(i, carry):
             ids = index[pl.ds(case, 1), pl.ds(pl.multiple_of(i * chunk, chunk), chunk)]
             row = (ids >> 7) - base
-            col = ids & 127
-            hit_row = jnp.where(iota((rows, chunk), 0) == row, 1.0, 0.0).astype(jnp.bfloat16)
-            hit_col = jnp.where(iota((128, chunk), 0) == col, 1.0, 0.0).astype(jnp.bfloat16)
+            col = (ids & 127) + 128 * (row & 3)
+            hit_row = jnp.where(iota((COUNT_ROWS, chunk), 0) == (row >> 2), 1.0, 0.0).astype(jnp.bfloat16)
+            hit_col = jnp.where(iota((512, chunk), 0) == col, 1.0, 0.0).astype(jnp.bfloat16)
             acc[...] += lax.dot_general(
                 hit_row, hit_col, (((1,), (1,)), ((), ())), preferred_element_type=F32
             )
             return carry
 
         lax.fori_loop(0, total // chunk, step, 0)
-        out[case] = acc[...].reshape(WINDOW, NY, 128)
+        for low in range(4):
+            flat[pl.ds(low, COUNT_ROWS, stride=4), :] = acc[:, 128 * low : 128 * (low + 1)]
+        out[case] = flat[0 : WINDOW * NY, :].reshape(WINDOW, NY, 128)
 
 
 def neighbours_x(p):
@@ -894,7 +903,7 @@
     counts = call(
         count_kernel,
         [vmem(*window)],
-        [(WINDOW * NY, 128)],
+        [(COUNT_ROWS, 512), (4 * COUNT_ROWS, 128)],
         (position_ref, load_index),
         "counts",
         cost=pl.CostEstimate(flops=3 * 10**10, bytes_accessed=10**7, transcendentals=0),

time: 205 us -> 201 us (0.980)
  Pallas kernels: 53.1 us -> 49.2 us
    pallas_call x10, Pallas kernels: 53.1 us -> 49.2 us  [call(): pl.pallas_call(body, out_shape=[o for o, _ in outs], in_specs=[pl.BlockSp...]
  transfers between devices with their start and end apart: 17 -> 17, of which waited for: 6 -> 6; matrix products, arithmetic and copies ran while one was open for 0% -> 0% of each run, Pallas kernels for 4% -> 3%
where the time goes in v4:
time: 201 us; the launch traced here: 200 us
  blocking collectives  95 us (47%)
  Pallas kernels  49.2 us (24%)
  starting transfers between devices  38.3 us (19%)
  waiting for transfers between devices  16.2 us (8%)
    all_to_all x4, blocking collectives, gather(): return lax.all_to_all(tiles, 'space', 0, 0)  95 us
    pallas_call x10, Pallas kernels, call(): pl.pallas_call(body, out_shape=[o for o, _ in outs], in_specs=[pl.BlockSp...  49.2 us
    ppermute x3, starting transfers between devices, two_either_side(): lax.ppermute(own, 'space', ahead)  13 us
    ppermute x3, waiting for transfers between devices, two_either_side(): lax.ppermute(tail, 'space', skip)  11 us
    ppermute x3, starting transfers between devices, two_either_side(): lax.ppermute(tail, 'space', skip)  10.8 us
    ppermute x1, starting transfers between devices, on_device(): other = lax.ppermute(energy, 'case', [(0, 1), (1, 0)])  4.35 us
    ppermute x3, starting transfers between devices, two_either_side(): lax.ppermute(head, 'space', skip_back)  4.06 us
  transfers between devices with their start and end apart: 17, of which 6 were waited for; matrix products, arithmetic and copies ran while one was open for 0% of the time, Pallas kernels for 3%

profile of v4, /device:TPU:1, one launch (start us, length us, event | category | flops | bytes accessed | tf_op | source)
XLA Modules:
  0.0 200.4 jit_solution(11449432245984304197)
XLA Ops:
  0.6 1.2 collect.1
  1.9 1.3 collective-permute-start.1
  3.2 5.0 %collective-permute-start = (f32[12,40,128]{2,1,0:T(8,128)S(1)}, f32[12,40,128]{2,1,0:T(8,128)S(1)}, u32[]{:S(2)}, u32[]{:S(2)}) collective-permute-start(f32[12,40,128]{2,1,0:T(8,128)S(1)} %get-tuple-element.52), channel_id=1, source_target_pairs={{0,1},{1,2},{2,3},{3,4},{4,5},{5,6},{6,7},{7,8},{8,9},{9,10},{10,1... | collective-permute-start | bytes 737288 | tf_op jit(solution)/shard_map/ppermute | solution.py:867
  8.2 5.3 %collective-permute-start.2 = (f32[8,40,128]{2,1,0:T(8,128)S(1)}, f32[8,40,128]{2,1,0:T(8,128)S(1)}, u32[]{:S(2)}, u32[]{:S(2)}) collective-permute-start(f32[8,40,128]{2,1,0:T(8,128)S(1)} %get-tuple-element.53), channel_id=1, source_target_pairs={{0,2},{1,3},{2,4},{3,5},{4,6},{5,7},{6,8},{7,9},{8,10},{9,11},{10,... | collective-permute-start | bytes 491528 | tf_op jit(solution)/shard_map/ppermute | solution.py:866
  13.5 1.3 collective-permute-start.3
  15.6 6.9 %counts.1 = f32[2,34,40,128]{3,2,1,0:T(8,128)S(1)} custom-call(s32[1]{0:T(128)} %bitcast.me.me_ref, s32[2,4096]{1,0:T(2,128)S(1)} %copy-done.6), custom_call_target="tpu_custom_call" | custom-call | flops 30000001024 | bytes 10000000 | tf_op jit(solution)/shard_map/counts/pallas_call | solution.py:844
  22.5 1.6 collective-permute-start.4
  24.7 1.1 collective-permute-done.6.o_before2
  26.1 8.7 %setup.1 = (f32[7,34,40,128]{3,2,1,0:T(8,128)}, f32[8,16,24,128]{3,2,1,0:T(8,128)}, f32[2,34,40,128]{3,2,1,0:T(8,128)}, f32[2,12,40,128]{3,2,1,0:T(8,128)}, f32[...) custom-call(s32[1]{0:T(128)} %bitcast.me.me_ref, ...), custom_call_target="tpu_custom_call" | custom-call | tf_op jit(solution)/shard_map/setup/pallas_call | solution.py:844
  34.8 30.0 %all_to_all.20.gathered = f32[64,24,128]{2,1,0:T(8,128)S(1)} all-to-all(f32[64,24,128]{2,1,0:T(8,128)S(1)} %get-tuple-element.60), channel_id=1, replica_groups=mesh['case'=2,'space'=64] {'space'}, dimensions={0} | all-to-all | bytes 1572864 | tf_op jit(solution)/shard_map/all_to_all | solution.py:870
  64.8 5.7 %up.2 = (f32[2,8,40,128]{3,2,1,0:T(8,128)S(1)}, f32[2,5,40,128]{3,2,1,0:T(8,128)S(1)}, f32[2,5,40,128]{3,2,1,0:T(8,128)S(1)}, f32[8,23,16,128]{3,2,1,0:T(8,128)S(1)}, f32[8,23,8,128]{3,2,1,0:T(8,128)S(1)}) custom-call(s32[1]{0:T(128)} %bitcast.me.me_ref, f32[64,24,128]{2,1,0:T(8,128)S(1)} %all_to_all.20.gathered, ...), custom_call_target="tpu_custom_call" | custom-call | tf_op jit(solution)/shard_map/up/pallas_call | solution.py:844
  70.5 1.3 collective-permute-start.9
  71.8 4.0 %collective-permute-start.8 = (f32[2,8,40,128]{3,2,1,0:T(8,128)S(1)}, f32[2,8,40,128]{3,2,1,0:T(8,128)S(1)}, u32[]{:S(2)}, u32[]{:S(2)}) collective-permute-start(f32[2,8,40,128]{3,2,1,0:T(8,128)S(1)} %get-tuple-element.67.own), channel_id=1, source_target_pairs={{0,1},{1,2},{2,3},{3,4},{4,5},{5,6},{6,7},{7,8},{8,9},{9,10},{10,1... | collective-permute-start | bytes 983048 | tf_op jit(solution)/shard_map/ppermute | solution.py:867
  75.8 2.8 %collective-permute-start.10 = (f32[2,5,40,128]{3,2,1,0:T(8,128)S(1)}, f32[2,5,40,128]{3,2,1,0:T(8,128)S(1)}, u32[]{:S(2)}, u32[]{:S(2)}) collective-permute-start(f32[2,5,40,128]{3,2,1,0:T(8,128)S(1)} %get-tuple-element.68), channel_id=1, source_target_pairs={{0,2},{1,3},{2,4},{3,5},{4,6},{5,7},{6,8},{7,9},{8,10},{9,11},{10,... | collective-permute-start | bytes 614408 | tf_op jit(solution)/shard_map/ppermute | solution.py:866
  78.6 1.5 collective-permute-start.11
  80.1 6.8 %collective-permute-done.10.before2 = f32[2,5,40,128]{3,2,1,0:T(8,128)S(1)} collective-permute-done((f32[2,5,40,128]{3,2,1,0:T(8,128)S(1)}, f32[2,5,40,128]{3,2,1,0:T(8,128)S(1)}, u32[]{:S(2)}, u32[]{:S(2)}) %collective-permute-start.10) | collective-permute-done | bytes 204832 | tf_op jit(solution)/shard_map/ppermute | solution.py:866
  86.9 4.7 %first.1 = (f32[2,12,40,128]{3,2,1,0:T(8,128)}, f32[2,34,40,128]{3,2,1,0:T(8,128)}, f32[2,12,40,128]{3,2,1,0:T(8,128)}, f32[10,24,128]{2,1,0:T(8,128)S(1)}, f32[...) custom-call(f32[2,8,40,128]{3,2,1,0:T(8,128)S(1)} %get-tuple-element.67.own, ...), custom_call_target="tpu_custom_call" | custom-call | tf_op jit(solution)/shard_map/first/pallas_call | solution.py:844
  91.6 25.5 %all_to_all.21.gathered = f32[64,16,128]{2,1,0:T(8,128)S(1)} all-to-all(f32[64,16,128]{2,1,0:T(8,128)S(1)} %get-tuple-element.70), channel_id=1, replica_groups=mesh['case'=2,'space'=64] {'space'}, dimensions={0} | all-to-all | bytes 1048576 | tf_op jit(solution)/shard_map/all_to_all | solution.py:870
  117.1 5.4 %up.3 = (f32[2,8,40,128]{3,2,1,0:T(8,128)S(1)}, f32[2,5,40,128]{3,2,1,0:T(8,128)S(1)}, f32[2,5,40,128]{3,2,1,0:T(8,128)S(1)}, f32[8,128]{1,0:T(8,128)S(1)}) custom-call(s32[1]{0:T(128)} %bitcast.me.me_ref, f32[64,16,128]{2,1,0:T(8,128)S(1)} %all_to_all.21.gathered, f32[2,34,40,128]{3,2,1,0:T(8,128)} %get-tuple-element.71.r_hbm.w0_hbm, ...), custom_call_target="tpu_custom_call" | custom-call | tf_op jit(solution)/shard_map/up/pallas_call | solution.py:844
  122.5 1.3 collective-permute-start.13
  123.8 4.0 %collective-permute-start.12 = (f32[2,8,40,128]{3,2,1,0:T(8,128)S(1)}, f32[2,8,40,128]{3,2,1,0:T(8,128)S(1)}, u32[]{:S(2)}, u32[]{:S(2)}) collective-permute-start(f32[2,8,40,128]{3,2,1,0:T(8,128)S(1)} %get-tuple-element.77.own), channel_id=1, source_target_pairs={{0,1},{1,2},{2,3},{3,4},{4,5},{5,6},{6,7},{7,8},{8,9},{9,10},{10,1... | collective-permute-start | bytes 983048 | tf_op jit(solution)/shard_map/ppermute | solution.py:867
  127.9 2.7 %collective-permute-start.14 = (f32[2,5,40,128]{3,2,1,0:T(8,128)S(1)}, f32[2,5,40,128]{3,2,1,0:T(8,128)S(1)}, u32[]{:S(2)}, u32[]{:S(2)}) collective-permute-start(f32[2,5,40,128]{3,2,1,0:T(8,128)S(1)} %get-tuple-element.78), channel_id=1, source_target_pairs={{0,2},{1,3},{2,4},{3,5},{4,6},{5,7},{6,8},{7,9},{8,10},{9,11},{10,... | collective-permute-start | bytes 614408 | tf_op jit(solution)/shard_map/ppermute | solution.py:866
  130.6 1.3 collective-permute-start.15
  131.9 4.2 %collective-permute-done.14.before2 = f32[2,5,40,128]{3,2,1,0:T(8,128)S(1)} collective-permute-done((f32[2,5,40,128]{3,2,1,0:T(8,128)S(1)}, f32[2,5,40,128]{3,2,1,0:T(8,128)S(1)}, u32[]{:S(2)}, u32[]{:S(2)}) %collective-permute-start.14) | collective-permute-done | bytes 204832 | tf_op jit(solution)/shard_map/ppermute | solution.py:866
  136.0 2.7 %collective-permute-done.15.after2 = f32[2,5,40,128]{3,2,1,0:T(8,128)S(1)} collective-permute-done((f32[2,5,40,128]{3,2,1,0:T(8,128)S(1)}, f32[2,5,40,128]{3,2,1,0:T(8,128)S(1)}, u32[]{:S(2)}, u32[]{:S(2)}) %collective-permute-start.15) | collective-permute-done | bytes 204832 | tf_op jit(solution)/shard_map/ppermute | solution.py:866
  138.8 7.1 %second.1 = (f32[2,12,40,128]{3,2,1,0:T(8,128)}, f32[2,12,40,128]{3,2,1,0:T(8,128)}, f32[2,34,40,128]{3,2,1,0:T(8,128)}, f32[2,8,40,128]{3,2,1,0:T(8,128)}, f32[...) custom-call(f32[2,8,40,128]{3,2,1,0:T(8,128)S(1)} %get-tuple-element, ...), custom_call_target="tpu_custom_call" | custom-call | tf_op jit(solution)/shard_map/second/pallas_call | solution.py:844
  146.0 25.6 %all_to_all.22.gathered = f32[64,16,128]{2,1,0:T(8,128)S(1)} all-to-all(f32[64,16,128]{2,1,0:T(8,128)S(1)} %get-tuple-element.82), channel_id=1, replica_groups=mesh['case'=2,'space'=64] {'space'}, dimensions={0} | all-to-all | bytes 1048576 | tf_op jit(solution)/shard_map/all_to_all | solution.py:870
  171.6 6.9 %third.1 = (f32[2,12,40,128]{3,2,1,0:T(8,128)S(1)}, f32[2,12,40,128]{3,2,1,0:T(8,128)S(1)}, f32[2,12,40,128]{3,2,1,0:T(8,128)S(1)}, f32[64,8,128]{2,1,0:T(8,128)S(1)}, f32[8,128]{1,0:T(8,128)S(1)}) custom-call(s32[1]{0:T(128)} %bitcast.me.me_ref, f32[64,16,128]{2,1,0:T(8,128)S(1)} %all_to_all.22.gathered, f32[8,128]{1,0:T(8,128)S(1)} %get-tuple-element.80.dots0, ...), custom_call_target="tpu_custom_call" | custom-call | tf_op jit(solution)/shard_map/third/pallas_call | solution.py:844
  178.5 13.8 %all_to_all.23.gathered = f32[64,8,128]{2,1,0:T(8,128)S(1)} all-to-all(f32[64,8,128]{2,1,0:T(8,128)S(1)} %get-tuple-element.90), channel_id=1, replica_groups=mesh['case'=2,'space'=64] {'space'}, dimensions={0} | all-to-all | bytes 524288 | tf_op jit(solution)/shard_map/all_to_all | solution.py:870
  192.3 1.5 last.1
  193.9 4.3 %collective-permute-start.16 = (f32[10,40,128]{2,1,0:T(8,128)S(1)}, f32[10,40,128]{2,1,0:T(8,128)S(1)}, u32[]{:S(2)}, u32[]{:S(2)}) collective-permute-start(f32[10,40,128]{2,1,0:T(8,128)S(1)} %get-tuple-element.98.mine), channel_id=1, source_target_pairs={{0,64},{64,0},{1,65},{65,1},{2,66},{66,2},{3,67},{67,3},{4,68},{68... | collective-permute-start | bytes 614408 | tf_op jit(solution)/shard_map/ppermute | solution.py:974
  198.2 1.1 collective-permute-done.16.other
  (40 shorter events, 2.7 us)
Async XLA Ops:
  1.9 20.6 %collective-permute-start.1 = (f32[12,40,128]{2,1,0:T(8,128)S(1)}, f32[12,40,128]{2,1,0:T(8,128)S(1)}, u32[]{:S(2)}, u32[]{:S(2)}) collective-permute-start(f32[12,40,128]{2,1,0:T(8,128)S(1)} %get-tuple-element.52), channel_id=1, source_target_pairs={{1,0},{2,1},{3,2},{4,3},{5,4},{6,5},{7,6},{8,7},{9,8},{10,9},{11,1... | collective-permute-start | bytes 737288 | tf_op jit(solution)/shard_map/ppermute | solution.py:867
  3.2 19.3 %collective-permute-start = (f32[12,40,128]{2,1,0:T(8,128)S(1)}, f32[12,40,128]{2,1,0:T(8,128)S(1)}, u32[]{:S(2)}, u32[]{:S(2)}) collective-permute-start(f32[12,40,128]{2,1,0:T(8,128)S(1)} %get-tuple-element.52), channel_id=1, source_target_pairs={{0,1},{1,2},{2,3},{3,4},{4,5},{5,6},{6,7},{7,8},{8,9},{9,10},{10,1... | collective-permute-start | bytes 737288 | tf_op jit(solution)/shard_map/ppermute | solution.py:867
  8.2 14.3 %collective-permute-start.2 = (f32[8,40,128]{2,1,0:T(8,128)S(1)}, f32[8,40,128]{2,1,0:T(8,128)S(1)}, u32[]{:S(2)}, u32[]{:S(2)}) collective-permute-start(f32[8,40,128]{2,1,0:T(8,128)S(1)} %get-tuple-element.53), channel_id=1, source_target_pairs={{0,2},{1,3},{2,4},{3,5},{4,6},{5,7},{6,8},{7,9},{8,10},{9,11},{10,... | collective-permute-start | bytes 491528 | tf_op jit(solution)/shard_map/ppermute | solution.py:866
  13.5 8.9 %collective-permute-start.3 = (f32[8,40,128]{2,1,0:T(8,128)S(1)}, f32[8,40,128]{2,1,0:T(8,128)S(1)}, u32[]{:S(2)}, u32[]{:S(2)}) collective-permute-start(f32[8,40,128]{2,1,0:T(8,128)S(1)} %get-tuple-element.54), channel_id=1, source_target_pairs={{2,0},{3,1},{4,2},{5,3},{6,4},{7,5},{8,6},{9,7},{10,8},{11,9},{12,... | collective-permute-start | bytes 491528 | tf_op jit(solution)/shard_map/ppermute | solution.py:866
  14.8 0.8 copy-start.6
  22.5 3.6 %collective-permute-start.4 = (f32[12,40,128]{2,1,0:T(8,128)S(1)}, f32[12,40,128]{2,1,0:T(8,128)S(1)}, u32[]{:S(2)}, u32[]{:S(2)}) collective-permute-start(f32[12,40,128]{2,1,0:T(8,128)S(1)} %collective-permute-done.before), channel_id=1, source_target_pairs={{0,64},{64,0},{1,65},{65,1},{2,66},{66,2},{3,67},{67,3},{4,68},{68... | collective-permute-start | bytes 737288 | tf_op jit(solution)/shard_map/ppermute | solution.py:912
  24.1 2.0 collective-permute-start.5
  24.2 1.7 collective-permute-start.6
  24.6 1.5 collective-permute-start.7
  64.8 22.1 %slice-start = ((s8[4874240]{0:T(1024)(128)(4,1)}), s8[4194304]{0:T(1024)(128)(4,1)S(1)}, s32[]{:S(2)}) async-start(s8[4874240]{0:T(1024)(128)(4,1)} %bitcast.2), calls=%async_computation.4 | async-start | bytes 8388608
  64.8 22.1 %slice-start.1 = ((s8[4874240]{0:T(1024)(128)(4,1)}), s8[679936]{0:T(1024)(128)(4,1)S(1)}, s32[]{:S(2)}) async-start(s8[4874240]{0:T(1024)(128)(4,1)} %bitcast.2), calls=%async_computation.5 | async-start | bytes 1359872
  64.8 22.1 %copy-start = (f32[8,16,24,128]{3,2,1,0:T(8,128)S(1)}, f32[8,16,24,128]{3,2,1,0:T(8,128)}, u32[]{:S(2)}) copy-start(f32[8,16,24,128]{3,2,1,0:T(8,128)} %get-tuple-element.66.c1_hbm.c1) | copy-start | bytes 4718596
  70.5 16.4 %collective-permute-start.9 = (f32[2,8,40,128]{3,2,1,0:T(8,128)S(1)}, f32[2,8,40,128]{3,2,1,0:T(8,128)S(1)}, u32[]{:S(2)}, u32[]{:S(2)}) collective-permute-start(f32[2,8,40,128]{3,2,1,0:T(8,128)S(1)} %get-tuple-element.67.own), channel_id=1, source_target_pairs={{1,0},{2,1},{3,2},{4,3},{5,4},{6,5},{7,6},{8,7},{9,8},{10,9},{11,1... | collective-permute-start | bytes 983048 | tf_op jit(solution)/shard_map/ppermute | solution.py:867
  71.8 15.1 %collective-permute-start.8 = (f32[2,8,40,128]{3,2,1,0:T(8,128)S(1)}, f32[2,8,40,128]{3,2,1,0:T(8,128)S(1)}, u32[]{:S(2)}, u32[]{:S(2)}) collective-permute-start(f32[2,8,40,128]{3,2,1,0:T(8,128)S(1)} %get-tuple-element.67.own), channel_id=1, source_target_pairs={{0,1},{1,2},{2,3},{3,4},{4,5},{5,6},{6,7},{7,8},{8,9},{9,10},{10,1... | collective-permute-start | bytes 983048 | tf_op jit(solution)/shard_map/ppermute | solution.py:867
  75.8 11.1 %collective-permute-start.10 = (f32[2,5,40,128]{3,2,1,0:T(8,128)S(1)}, f32[2,5,40,128]{3,2,1,0:T(8,128)S(1)}, u32[]{:S(2)}, u32[]{:S(2)}) collective-permute-start(f32[2,5,40,128]{3,2,1,0:T(8,128)S(1)} %get-tuple-element.68), channel_id=1, source_target_pairs={{0,2},{1,3},{2,4},{3,5},{4,6},{5,7},{6,8},{7,9},{8,10},{9,11},{10,... | collective-permute-start | bytes 614408 | tf_op jit(solution)/shard_map/ppermute | solution.py:866
  78.6 8.3 %collective-permute-start.11 = (f32[2,5,40,128]{3,2,1,0:T(8,128)S(1)}, f32[2,5,40,128]{3,2,1,0:T(8,128)S(1)}, u32[]{:S(2)}, u32[]{:S(2)}) collective-permute-start(f32[2,5,40,128]{3,2,1,0:T(8,128)S(1)} %get-tuple-element.69), channel_id=1, source_target_pairs={{2,0},{3,1},{4,2},{5,3},{6,4},{7,5},{8,6},{9,7},{10,8},{11,9},{12,... | collective-permute-start | bytes 614408 | tf_op jit(solution)/shard_map/ppermute | solution.py:866
  117.1 21.7 %slice-start.2 = ((s8[4874240]{0:T(1024)(128)(4,1)}), s8[4194304]{0:T(1024)(128)(4,1)S(1)}, s32[]{:S(2)}) async-start(s8[4874240]{0:T(1024)(128)(4,1)} %bitcast.4), calls=%async_computation.6 | async-start | bytes 8388608
  117.1 21.7 %slice-start.3 = ((s8[4874240]{0:T(1024)(128)(4,1)}), s8[679936]{0:T(1024)(128)(4,1)S(1)}, s32[]{:S(2)}) async-start(s8[4874240]{0:T(1024)(128)(4,1)} %bitcast.4), calls=%async_computation.7 | async-start | bytes 1359872
  117.1 21.7 %copy-start.1 = (f32[8,16,24,128]{3,2,1,0:T(8,128)S(1)}, f32[8,16,24,128]{3,2,1,0:T(8,128)}, u32[]{:S(2)}) copy-start(f32[8,16,24,128]{3,2,1,0:T(8,128)} %get-tuple-element.66.c1_hbm.c1) | copy-start | bytes 4718596
  122.5 16.2 %collective-permute-start.13 = (f32[2,8,40,128]{3,2,1,0:T(8,128)S(1)}, f32[2,8,40,128]{3,2,1,0:T(8,128)S(1)}, u32[]{:S(2)}, u32[]{:S(2)}) collective-permute-start(f32[2,8,40,128]{3,2,1,0:T(8,128)S(1)} %get-tuple-element.77.own), channel_id=1, source_target_pairs={{1,0},{2,1},{3,2},{4,3},{5,4},{6,5},{7,6},{8,7},{9,8},{10,9},{11,1... | collective-permute-start | bytes 983048 | tf_op jit(solution)/shard_map/ppermute | solution.py:867
  123.8 14.9 %collective-permute-start.12 = (f32[2,8,40,128]{3,2,1,0:T(8,128)S(1)}, f32[2,8,40,128]{3,2,1,0:T(8,128)S(1)}, u32[]{:S(2)}, u32[]{:S(2)}) collective-permute-start(f32[2,8,40,128]{3,2,1,0:T(8,128)S(1)} %get-tuple-element.77.own), channel_id=1, source_target_pairs={{0,1},{1,2},{2,3},{3,4},{4,5},{5,6},{6,7},{7,8},{8,9},{9,10},{10,1... | collective-permute-start | bytes 983048 | tf_op jit(solution)/shard_map/ppermute | solution.py:867
  127.9 8.2 %collective-permute-start.14 = (f32[2,5,40,128]{3,2,1,0:T(8,128)S(1)}, f32[2,5,40,128]{3,2,1,0:T(8,128)S(1)}, u32[]{:S(2)}, u32[]{:S(2)}) collective-permute-start(f32[2,5,40,128]{3,2,1,0:T(8,128)S(1)} %get-tuple-element.78), channel_id=1, source_target_pairs={{0,2},{1,3},{2,4},{3,5},{4,6},{5,7},{6,8},{7,9},{8,10},{9,11},{10,... | collective-permute-start | bytes 614408 | tf_op jit(solution)/shard_map/ppermute | solution.py:866
  130.6 8.2 %collective-permute-start.15 = (f32[2,5,40,128]{3,2,1,0:T(8,128)S(1)}, f32[2,5,40,128]{3,2,1,0:T(8,128)S(1)}, u32[]{:S(2)}, u32[]{:S(2)}) collective-permute-start(f32[2,5,40,128]{3,2,1,0:T(8,128)S(1)} %get-tuple-element.79), channel_id=1, source_target_pairs={{2,0},{3,1},{4,2},{5,3},{6,4},{7,5},{8,6},{9,7},{10,8},{11,9},{12,... | collective-permute-start | bytes 614408 | tf_op jit(solution)/shard_map/ppermute | solution.py:866
  171.6 20.8 %copy-start.3 = (f32[12,40,128]{2,1,0:T(8,128)S(1)}, f32[12,40,128]{2,1,0:T(8,128)}, u32[]{:S(2)}) copy-start(f32[12,40,128]{2,1,0:T(8,128)} %get-tuple-element.95.mod) | copy-start | bytes 737284
  171.6 20.8 %copy-start.4 = (f32[12,40,128]{2,1,0:T(8,128)S(1)}, f32[12,40,128]{2,1,0:T(8,128)}, u32[]{:S(2)}) copy-start(f32[12,40,128]{2,1,0:T(8,128)} %get-tuple-element.96.free) | copy-start | bytes 737284
  178.5 20.8 %copy-start.2 = (s32[8,40,128]{2,1,0:T(8,128)S(1)}, s32[8,40,128]{2,1,0:T(8,128)}, u32[]{:S(2)}) copy-start(s32[8,40,128]{2,1,0:T(8,128)} %passive.1) | copy-start | bytes 491524
  178.5 20.8 %copy-start.5 = (f32[10,40,128]{2,1,0:T(8,128)S(1)}, f32[10,40,128]{2,1,0:T(8,128)}, u32[]{:S(2)}) copy-start(f32[10,40,128]{2,1,0:T(8,128)} %get-tuple-element.99.scale) | copy-start | bytes 614404
  193.9 5.4 %collective-permute-start.16 = (f32[10,40,128]{2,1,0:T(8,128)S(1)}, f32[10,40,128]{2,1,0:T(8,128)S(1)}, u32[]{:S(2)}, u32[]{:S(2)}) collective-permute-start(f32[10,40,128]{2,1,0:T(8,128)S(1)} %get-tuple-element.98.mine), channel_id=1, source_target_pairs={{0,64},{64,0},{1,65},{65,1},{2,66},{66,2},{3,67},{67,3},{4,68},{68... | collective-permute-start | bytes 614408 | tf_op jit(solution)/shard_map/ppermute | solution.py:974

commit v5 on v4

--- a/solution.py
+++ b/solution.py
@@ -26,6 +26,7 @@
 R2 = 16
 R3 = 8
 TALK = 24
+LONG = pl.CostEstimate(flops=4 * 10**10, bytes_accessed=10**8, transcendentals=0)
 CPARAMS = pltpu.CompilerParams(vmem_limit_bytes=32 * 1024 * 1024)
 
 
@@ -571,6 +572,10 @@
     return slice(HALO - reach, HALO + BLOCK + reach)
 
 
+def pass_kernel(source, target):
+    target[...] = source[...]
+
+
 def up_kernel(first, me_ref, gathered, r_hbm, s2_hbm, s21, r1_ref, c0_hbm, c1_hbm, *rest):
     if first:
         out, head, tail, c2, c3, s2, r, c0, c1, vb, work, wide, sems = rest
@@ -864,6 +869,8 @@
         skip = [(i, i + 2) for i in range(members - 2)]
         skip_back = [(i + 2, i) for i in range(members - 2)]
         away = lax.ppermute(tail, "space", skip), lax.ppermute(head, "space", skip_back)
+        if own.ndim == 4:
+            own = call(pass_kernel, [vmem(*own.shape)], [], (own,), "pass", cost=LONG)[0]
         return (lax.ppermute(own, "space", ahead), lax.ppermute(own, "space", back)) + away
 
     def gather(tiles):

time: 201 us -> 201 us (level)
    pallas_call x10 -> x12, Pallas kernels: 49.2 us -> 48.6 us  [call(): pl.pallas_call(body, out_shape=[o for o, _ in outs], in_specs=[pl.BlockSp...]
where the time goes in v5:
time: 201 us
  blocking collectives  95.1 us (47%)
  Pallas kernels  48.6 us (24%)
  starting transfers between devices  38.9 us (19%)
  waiting for transfers between devices  16.2 us (8%)
    all_to_all x4, blocking collectives, gather(): return lax.all_to_all(tiles, 'space', 0, 0)  95.1 us
    pallas_call x12, Pallas kernels, call(): pl.pallas_call(body, out_shape=[o for o, _ in outs], in_specs=[pl.BlockSp...  48.6 us
    ppermute x3, starting transfers between devices, two_either_side(): lax.ppermute(own, 'space', ahead)  13 us
    ppermute x3, starting transfers between devices, two_either_side(): lax.ppermute(tail, 'space', skip)  10.9 us
    ppermute x3, waiting for transfers between devices, two_either_side(): lax.ppermute(tail, 'space', skip)  10.9 us
    ppermute x3, starting transfers between devices, two_either_side(): lax.ppermute(own, 'space', back)  4.4 us
    ppermute x1, starting transfers between devices, on_device(): other = lax.ppermute(energy, 'case', [(0, 1), (1, 0)])  4.33 us
    ppermute x3, starting transfers between devices, two_either_side(): lax.ppermute(head, 'space', skip_back)  4.06 us
  transfers between devices with their start and end apart: 17, of which 6 were waited for; matrix products, arithmetic and copies ran while one was open for 0% of the time, Pallas kernels for 3%

profile of v5, /device:TPU:1, one launch (start us, length us, event | category | flops | bytes accessed | tf_op | source)
XLA Modules:
  0.0 200.6 jit_solution(8851389015275471723)
XLA Ops:
  0.6 1.2 collect.1
  1.9 1.3 collective-permute-start.1
  3.2 5.0 %collective-permute-start = (f32[12,40,128]{2,1,0:T(8,128)S(1)}, f32[12,40,128]{2,1,0:T(8,128)S(1)}, u32[]{:S(2)}, u32[]{:S(2)}) collective-permute-start(f32[12,40,128]{2,1,0:T(8,128)S(1)} %get-tuple-element.52), channel_id=1, source_target_pairs={{0,1},{1,2},{2,3},{3,4},{4,5},{5,6},{6,7},{7,8},{8,9},{9,10},{10,1... | collective-permute-start | bytes 737288 | tf_op jit(solution)/shard_map/ppermute | solution.py:874
  8.2 5.3 %collective-permute-start.2 = (f32[8,40,128]{2,1,0:T(8,128)S(1)}, f32[8,40,128]{2,1,0:T(8,128)S(1)}, u32[]{:S(2)}, u32[]{:S(2)}) collective-permute-start(f32[8,40,128]{2,1,0:T(8,128)S(1)} %get-tuple-element.53), channel_id=1, source_target_pairs={{0,2},{1,3},{2,4},{3,5},{4,6},{5,7},{6,8},{7,9},{8,10},{9,11},{10,... | collective-permute-start | bytes 491528 | tf_op jit(solution)/shard_map/ppermute | solution.py:871
  13.5 1.3 collective-permute-start.3
  15.6 6.9 %counts.1 = f32[2,34,40,128]{3,2,1,0:T(8,128)S(1)} custom-call(s32[1]{0:T(128)} %bitcast.me.me_ref, s32[2,4096]{1,0:T(2,128)S(1)} %copy-done.6), custom_call_target="tpu_custom_call" | custom-call | flops 30000001024 | bytes 10000000 | tf_op jit(solution)/shard_map/counts/pallas_call | solution.py:849
  22.5 1.6 collective-permute-start.4
  24.7 1.1 collective-permute-done.6.o_before2
  26.1 8.7 %setup.1 = (f32[7,34,40,128]{3,2,1,0:T(8,128)}, f32[8,16,24,128]{3,2,1,0:T(8,128)}, f32[2,34,40,128]{3,2,1,0:T(8,128)}, f32[2,12,40,128]{3,2,1,0:T(8,128)}, f32[...) custom-call(s32[1]{0:T(128)} %bitcast.me.me_ref, ...), custom_call_target="tpu_custom_call" | custom-call | tf_op jit(solution)/shard_map/setup/pallas_call | solution.py:849
  34.8 30.0 %all_to_all.20.gathered = f32[64,24,128]{2,1,0:T(8,128)S(1)} all-to-all(f32[64,24,128]{2,1,0:T(8,128)S(1)} %get-tuple-element.60), channel_id=1, replica_groups=mesh['case'=2,'space'=64] {'space'}, dimensions={0} | all-to-all | bytes 1572864 | tf_op jit(solution)/shard_map/all_to_all | solution.py:877
  64.8 5.7 %up.2 = (f32[2,8,40,128]{3,2,1,0:T(8,128)S(1)}, f32[2,5,40,128]{3,2,1,0:T(8,128)S(1)}, f32[2,5,40,128]{3,2,1,0:T(8,128)S(1)}, f32[8,23,16,128]{3,2,1,0:T(8,128)S(1)}, f32[8,23,8,128]{3,2,1,0:T(8,128)S(1)}) custom-call(s32[1]{0:T(128)} %bitcast.me.me_ref, f32[64,24,128]{2,1,0:T(8,128)S(1)} %all_to_all.20.gathered, ...), custom_call_target="tpu_custom_call" | custom-call | tf_op jit(solution)/shard_map/up/pallas_call | solution.py:849
  70.5 1.6 collective-permute-start.9
  72.1 4.0 %collective-permute-start.8 = (f32[2,8,40,128]{3,2,1,0:T(8,128)S(1)}, f32[2,8,40,128]{3,2,1,0:T(8,128)S(1)}, u32[]{:S(2)}, u32[]{:S(2)}) collective-permute-start(f32[2,8,40,128]{3,2,1,0:T(8,128)S(1)} %pass.2), channel_id=1, source_target_pairs={{0,1},{1,2},{2,3},{3,4},{4,5},{5,6},{6,7},{7,8},{8,9},{9,10},{10,1... | collective-permute-start | bytes 983048 | tf_op jit(solution)/shard_map/ppermute | solution.py:874
  76.1 2.8 %collective-permute-start.10 = (f32[2,5,40,128]{3,2,1,0:T(8,128)S(1)}, f32[2,5,40,128]{3,2,1,0:T(8,128)S(1)}, u32[]{:S(2)}, u32[]{:S(2)}) collective-permute-start(f32[2,5,40,128]{3,2,1,0:T(8,128)S(1)} %get-tuple-element.68), channel_id=1, source_target_pairs={{0,2},{1,3},{2,4},{3,5},{4,6},{5,7},{6,8},{7,9},{8,10},{9,11},{10,... | collective-permute-start | bytes 614408 | tf_op jit(solution)/shard_map/ppermute | solution.py:871
  78.9 1.5 collective-permute-start.11
  80.4 6.8 %collective-permute-done.10.before2 = f32[2,5,40,128]{3,2,1,0:T(8,128)S(1)} collective-permute-done((f32[2,5,40,128]{3,2,1,0:T(8,128)S(1)}, f32[2,5,40,128]{3,2,1,0:T(8,128)S(1)}, u32[]{:S(2)}, u32[]{:S(2)}) %collective-permute-start.10) | collective-permute-done | bytes 204832 | tf_op jit(solution)/shard_map/ppermute | solution.py:871
  87.2 4.7 %first.1 = (f32[2,12,40,128]{3,2,1,0:T(8,128)}, f32[2,34,40,128]{3,2,1,0:T(8,128)}, f32[2,12,40,128]{3,2,1,0:T(8,128)}, f32[10,24,128]{2,1,0:T(8,128)S(1)}, f32[...) custom-call(f32[2,8,40,128]{3,2,1,0:T(8,128)S(1)} %get-tuple-element.67.source.own, ...), custom_call_target="tpu_custom_call" | custom-call | tf_op jit(solution)/shard_map/first/pallas_call | solution.py:849
  91.9 25.6 %all_to_all.21.gathered = f32[64,16,128]{2,1,0:T(8,128)S(1)} all-to-all(f32[64,16,128]{2,1,0:T(8,128)S(1)} %get-tuple-element.70), channel_id=1, replica_groups=mesh['case'=2,'space'=64] {'space'}, dimensions={0} | all-to-all | bytes 1048576 | tf_op jit(solution)/shard_map/all_to_all | solution.py:877
  117.6 4.8 %up.3 = (f32[2,8,40,128]{3,2,1,0:T(8,128)S(1)}, f32[2,5,40,128]{3,2,1,0:T(8,128)S(1)}, f32[2,5,40,128]{3,2,1,0:T(8,128)S(1)}, f32[8,128]{1,0:T(8,128)S(1)}) custom-call(s32[1]{0:T(128)} %bitcast.me.me_ref, f32[64,16,128]{2,1,0:T(8,128)S(1)} %all_to_all.21.gathered, f32[2,34,40,128]{3,2,1,0:T(8,128)} %get-tuple-element.71.r_hbm.w0_hbm, ...), custom_call_target="tpu_custom_call" | custom-call | tf_op jit(solution)/shard_map/up/pallas_call | solution.py:849
  122.5 1.6 collective-permute-start.13
  124.0 4.0 %collective-permute-start.12 = (f32[2,8,40,128]{3,2,1,0:T(8,128)S(1)}, f32[2,8,40,128]{3,2,1,0:T(8,128)S(1)}, u32[]{:S(2)}, u32[]{:S(2)}) collective-permute-start(f32[2,8,40,128]{3,2,1,0:T(8,128)S(1)} %pass.3), channel_id=1, source_target_pairs={{0,1},{1,2},{2,3},{3,4},{4,5},{5,6},{6,7},{7,8},{8,9},{9,10},{10,1... | collective-permute-start | bytes 983048 | tf_op jit(solution)/shard_map/ppermute | solution.py:874
  128.0 2.8 %collective-permute-start.14 = (f32[2,5,40,128]{3,2,1,0:T(8,128)S(1)}, f32[2,5,40,128]{3,2,1,0:T(8,128)S(1)}, u32[]{:S(2)}, u32[]{:S(2)}) collective-permute-start(f32[2,5,40,128]{3,2,1,0:T(8,128)S(1)} %get-tuple-element.78), channel_id=1, source_target_pairs={{0,2},{1,3},{2,4},{3,5},{4,6},{5,7},{6,8},{7,9},{8,10},{9,11},{10,... | collective-permute-start | bytes 614408 | tf_op jit(solution)/shard_map/ppermute | solution.py:871
  130.9 1.3 collective-permute-start.15
  132.2 4.1 %collective-permute-done.14.before2 = f32[2,5,40,128]{3,2,1,0:T(8,128)S(1)} collective-permute-done((f32[2,5,40,128]{3,2,1,0:T(8,128)S(1)}, f32[2,5,40,128]{3,2,1,0:T(8,128)S(1)}, u32[]{:S(2)}, u32[]{:S(2)}) %collective-permute-start.14) | collective-permute-done | bytes 204832 | tf_op jit(solution)/shard_map/ppermute | solution.py:871
  136.2 2.8 %collective-permute-done.15.after2 = f32[2,5,40,128]{3,2,1,0:T(8,128)S(1)} collective-permute-done((f32[2,5,40,128]{3,2,1,0:T(8,128)S(1)}, f32[2,5,40,128]{3,2,1,0:T(8,128)S(1)}, u32[]{:S(2)}, u32[]{:S(2)}) %collective-permute-start.15) | collective-permute-done | bytes 204832 | tf_op jit(solution)/shard_map/ppermute | solution.py:871
  139.1 7.1 %second.1 = (f32[2,12,40,128]{3,2,1,0:T(8,128)}, f32[2,12,40,128]{3,2,1,0:T(8,128)}, f32[2,34,40,128]{3,2,1,0:T(8,128)}, f32[2,8,40,128]{3,2,1,0:T(8,128)}, f32[...) custom-call(f32[2,8,40,128]{3,2,1,0:T(8,128)S(1)} %get-tuple-element, ...), custom_call_target="tpu_custom_call" | custom-call | tf_op jit(solution)/shard_map/second/pallas_call | solution.py:849
  146.3 25.6 %all_to_all.22.gathered = f32[64,16,128]{2,1,0:T(8,128)S(1)} all-to-all(f32[64,16,128]{2,1,0:T(8,128)S(1)} %get-tuple-element.82), channel_id=1, replica_groups=mesh['case'=2,'space'=64] {'space'}, dimensions={0} | all-to-all | bytes 1048576 | tf_op jit(solution)/shard_map/all_to_all | solution.py:877
  171.8 6.9 %third.1 = (f32[2,12,40,128]{3,2,1,0:T(8,128)S(1)}, f32[2,12,40,128]{3,2,1,0:T(8,128)S(1)}, f32[2,12,40,128]{3,2,1,0:T(8,128)S(1)}, f32[64,8,128]{2,1,0:T(8,128)S(1)}, f32[8,128]{1,0:T(8,128)S(1)}) custom-call(s32[1]{0:T(128)} %bitcast.me.me_ref, f32[64,16,128]{2,1,0:T(8,128)S(1)} %all_to_all.22.gathered, f32[8,128]{1,0:T(8,128)S(1)} %get-tuple-element.80.dots0, ...), custom_call_target="tpu_custom_call" | custom-call | tf_op jit(solution)/shard_map/third/pallas_call | solution.py:849
  178.8 13.8 %all_to_all.23.gathered = f32[64,8,128]{2,1,0:T(8,128)S(1)} all-to-all(f32[64,8,128]{2,1,0:T(8,128)S(1)} %get-tuple-element.90), channel_id=1, replica_groups=mesh['case'=2,'space'=64] {'space'}, dimensions={0} | all-to-all | bytes 524288 | tf_op jit(solution)/shard_map/all_to_all | solution.py:877
  192.6 1.5 last.1
  194.1 4.3 %collective-permute-start.16 = (f32[10,40,128]{2,1,0:T(8,128)S(1)}, f32[10,40,128]{2,1,0:T(8,128)S(1)}, u32[]{:S(2)}, u32[]{:S(2)}) collective-permute-start(f32[10,40,128]{2,1,0:T(8,128)S(1)} %get-tuple-element.98.mine), channel_id=1, source_target_pairs={{0,64},{64,0},{1,65},{65,1},{2,66},{66,2},{3,67},{67,3},{4,68},{68... | collective-permute-start | bytes 614408 | tf_op jit(solution)/shard_map/ppermute | solution.py:981
  198.5 1.1 collective-permute-done.16.other
  (42 shorter events, 2.8 us)
Async XLA Ops:
  1.9 20.6 %collective-permute-start.1 = (f32[12,40,128]{2,1,0:T(8,128)S(1)}, f32[12,40,128]{2,1,0:T(8,128)S(1)}, u32[]{:S(2)}, u32[]{:S(2)}) collective-permute-start(f32[12,40,128]{2,1,0:T(8,128)S(1)} %get-tuple-element.52), channel_id=1, source_target_pairs={{1,0},{2,1},{3,2},{4,3},{5,4},{6,5},{7,6},{8,7},{9,8},{10,9},{11,1... | collective-permute-start | bytes 737288 | tf_op jit(solution)/shard_map/ppermute | solution.py:874
  3.2 19.3 %collective-permute-start = (f32[12,40,128]{2,1,0:T(8,128)S(1)}, f32[12,40,128]{2,1,0:T(8,128)S(1)}, u32[]{:S(2)}, u32[]{:S(2)}) collective-permute-start(f32[12,40,128]{2,1,0:T(8,128)S(1)} %get-tuple-element.52), channel_id=1, source_target_pairs={{0,1},{1,2},{2,3},{3,4},{4,5},{5,6},{6,7},{7,8},{8,9},{9,10},{10,1... | collective-permute-start | bytes 737288 | tf_op jit(solution)/shard_map/ppermute | solution.py:874
  8.2 14.3 %collective-permute-start.2 = (f32[8,40,128]{2,1,0:T(8,128)S(1)}, f32[8,40,128]{2,1,0:T(8,128)S(1)}, u32[]{:S(2)}, u32[]{:S(2)}) collective-permute-start(f32[8,40,128]{2,1,0:T(8,128)S(1)} %get-tuple-element.53), channel_id=1, source_target_pairs={{0,2},{1,3},{2,4},{3,5},{4,6},{5,7},{6,8},{7,9},{8,10},{9,11},{10,... | collective-permute-start | bytes 491528 | tf_op jit(solution)/shard_map/ppermute | solution.py:871
  13.5 8.9 %collective-permute-start.3 = (f32[8,40,128]{2,1,0:T(8,128)S(1)}, f32[8,40,128]{2,1,0:T(8,128)S(1)}, u32[]{:S(2)}, u32[]{:S(2)}) collective-permute-start(f32[8,40,128]{2,1,0:T(8,128)S(1)} %get-tuple-element.54), channel_id=1, source_target_pairs={{2,0},{3,1},{4,2},{5,3},{6,4},{7,5},{8,6},{9,7},{10,8},{11,9},{12,... | collective-permute-start | bytes 491528 | tf_op jit(solution)/shard_map/ppermute | solution.py:871
  14.8 0.8 copy-start.6
  22.5 3.6 %collective-permute-start.4 = (f32[12,40,128]{2,1,0:T(8,128)S(1)}, f32[12,40,128]{2,1,0:T(8,128)S(1)}, u32[]{:S(2)}, u32[]{:S(2)}) collective-permute-start(f32[12,40,128]{2,1,0:T(8,128)S(1)} %collective-permute-done.before), channel_id=1, source_target_pairs={{0,64},{64,0},{1,65},{65,1},{2,66},{66,2},{3,67},{67,3},{4,68},{68... | collective-permute-start | bytes 737288 | tf_op jit(solution)/shard_map/ppermute | solution.py:919
  24.1 2.0 collective-permute-start.5
  24.2 1.7 collective-permute-start.6
  24.6 1.5 collective-permute-start.7
  70.5 16.7 %slice-start = ((s8[4874240]{0:T(1024)(128)(4,1)}), s8[4194304]{0:T(1024)(128)(4,1)S(1)}, s32[]{:S(2)}) async-start(s8[4874240]{0:T(1024)(128)(4,1)} %bitcast.2), calls=%async_computation.4 | async-start | bytes 8388608
  70.5 16.7 %slice-start.1 = ((s8[4874240]{0:T(1024)(128)(4,1)}), s8[679936]{0:T(1024)(128)(4,1)S(1)}, s32[]{:S(2)}) async-start(s8[4874240]{0:T(1024)(128)(4,1)} %bitcast.2), calls=%async_computation.5 | async-start | bytes 1359872
  70.5 16.7 %copy-start = (f32[8,16,24,128]{3,2,1,0:T(8,128)S(1)}, f32[8,16,24,128]{3,2,1,0:T(8,128)}, u32[]{:S(2)}) copy-start(f32[8,16,24,128]{3,2,1,0:T(8,128)} %get-tuple-element.66.c1_hbm.c1) | copy-start | bytes 4718596
  70.5 16.7 %collective-permute-start.9 = (f32[2,8,40,128]{3,2,1,0:T(8,128)S(1)}, f32[2,8,40,128]{3,2,1,0:T(8,128)S(1)}, u32[]{:S(2)}, u32[]{:S(2)}) collective-permute-start(f32[2,8,40,128]{3,2,1,0:T(8,128)S(1)} %pass.2), channel_id=1, source_target_pairs={{1,0},{2,1},{3,2},{4,3},{5,4},{6,5},{7,6},{8,7},{9,8},{10,9},{11,1... | collective-permute-start | bytes 983048 | tf_op jit(solution)/shard_map/ppermute | solution.py:874
  72.1 15.1 %collective-permute-start.8 = (f32[2,8,40,128]{3,2,1,0:T(8,128)S(1)}, f32[2,8,40,128]{3,2,1,0:T(8,128)S(1)}, u32[]{:S(2)}, u32[]{:S(2)}) collective-permute-start(f32[2,8,40,128]{3,2,1,0:T(8,128)S(1)} %pass.2), channel_id=1, source_target_pairs={{0,1},{1,2},{2,3},{3,4},{4,5},{5,6},{6,7},{7,8},{8,9},{9,10},{10,1... | collective-permute-start | bytes 983048 | tf_op jit(solution)/shard_map/ppermute | solution.py:874
  76.1 11.1 %collective-permute-start.10 = (f32[2,5,40,128]{3,2,1,0:T(8,128)S(1)}, f32[2,5,40,128]{3,2,1,0:T(8,128)S(1)}, u32[]{:S(2)}, u32[]{:S(2)}) collective-permute-start(f32[2,5,40,128]{3,2,1,0:T(8,128)S(1)} %get-tuple-element.68), channel_id=1, source_target_pairs={{0,2},{1,3},{2,4},{3,5},{4,6},{5,7},{6,8},{7,9},{8,10},{9,11},{10,... | collective-permute-start | bytes 614408 | tf_op jit(solution)/shard_map/ppermute | solution.py:871
  78.9 8.3 %collective-permute-start.11 = (f32[2,5,40,128]{3,2,1,0:T(8,128)S(1)}, f32[2,5,40,128]{3,2,1,0:T(8,128)S(1)}, u32[]{:S(2)}, u32[]{:S(2)}) collective-permute-start(f32[2,5,40,128]{3,2,1,0:T(8,128)S(1)} %get-tuple-element.69), channel_id=1, source_target_pairs={{2,0},{3,1},{4,2},{5,3},{6,4},{7,5},{8,6},{9,7},{10,8},{11,9},{12,... | collective-permute-start | bytes 614408 | tf_op jit(solution)/shard_map/ppermute | solution.py:871
  122.4 16.7 %slice-start.2 = ((s8[4874240]{0:T(1024)(128)(4,1)}), s8[4194304]{0:T(1024)(128)(4,1)S(1)}, s32[]{:S(2)}) async-start(s8[4874240]{0:T(1024)(128)(4,1)} %bitcast.4), calls=%async_computation.6 | async-start | bytes 8388608
  122.4 16.7 %slice-start.3 = ((s8[4874240]{0:T(1024)(128)(4,1)}), s8[679936]{0:T(1024)(128)(4,1)S(1)}, s32[]{:S(2)}) async-start(s8[4874240]{0:T(1024)(128)(4,1)} %bitcast.4), calls=%async_computation.7 | async-start | bytes 1359872
  122.4 16.7 %copy-start.1 = (f32[8,16,24,128]{3,2,1,0:T(8,128)S(1)}, f32[8,16,24,128]{3,2,1,0:T(8,128)}, u32[]{:S(2)}) copy-start(f32[8,16,24,128]{3,2,1,0:T(8,128)} %get-tuple-element.66.c1_hbm.c1) | copy-start | bytes 4718596
  122.5 16.6 %collective-permute-start.13 = (f32[2,8,40,128]{3,2,1,0:T(8,128)S(1)}, f32[2,8,40,128]{3,2,1,0:T(8,128)S(1)}, u32[]{:S(2)}, u32[]{:S(2)}) collective-permute-start(f32[2,8,40,128]{3,2,1,0:T(8,128)S(1)} %pass.3), channel_id=1, source_target_pairs={{1,0},{2,1},{3,2},{4,3},{5,4},{6,5},{7,6},{8,7},{9,8},{10,9},{11,1... | collective-permute-start | bytes 983048 | tf_op jit(solution)/shard_map/ppermute | solution.py:874
  124.0 15.1 %collective-permute-start.12 = (f32[2,8,40,128]{3,2,1,0:T(8,128)S(1)}, f32[2,8,40,128]{3,2,1,0:T(8,128)S(1)}, u32[]{:S(2)}, u32[]{:S(2)}) collective-permute-start(f32[2,8,40,128]{3,2,1,0:T(8,128)S(1)} %pass.3), channel_id=1, source_target_pairs={{0,1},{1,2},{2,3},{3,4},{4,5},{5,6},{6,7},{7,8},{8,9},{9,10},{10,1... | collective-permute-start | bytes 983048 | tf_op jit(solution)/shard_map/ppermute | solution.py:874
  128.0 8.2 %collective-permute-start.14 = (f32[2,5,40,128]{3,2,1,0:T(8,128)S(1)}, f32[2,5,40,128]{3,2,1,0:T(8,128)S(1)}, u32[]{:S(2)}, u32[]{:S(2)}) collective-permute-start(f32[2,5,40,128]{3,2,1,0:T(8,128)S(1)} %get-tuple-element.78), channel_id=1, source_target_pairs={{0,2},{1,3},{2,4},{3,5},{4,6},{5,7},{6,8},{7,9},{8,10},{9,11},{10,... | collective-permute-start | bytes 614408 | tf_op jit(solution)/shard_map/ppermute | solution.py:871
  130.9 8.2 %collective-permute-start.15 = (f32[2,5,40,128]{3,2,1,0:T(8,128)S(1)}, f32[2,5,40,128]{3,2,1,0:T(8,128)S(1)}, u32[]{:S(2)}, u32[]{:S(2)}) collective-permute-start(f32[2,5,40,128]{3,2,1,0:T(8,128)S(1)} %get-tuple-element.79), channel_id=1, source_target_pairs={{2,0},{3,1},{4,2},{5,3},{6,4},{7,5},{8,6},{9,7},{10,8},{11,9},{12,... | collective-permute-start | bytes 614408 | tf_op jit(solution)/shard_map/ppermute | solution.py:871
  171.8 20.8 %copy-start.3 = (f32[12,40,128]{2,1,0:T(8,128)S(1)}, f32[12,40,128]{2,1,0:T(8,128)}, u32[]{:S(2)}) copy-start(f32[12,40,128]{2,1,0:T(8,128)} %get-tuple-element.95.mod) | copy-start | bytes 737284
  171.8 20.8 %copy-start.4 = (f32[12,40,128]{2,1,0:T(8,128)S(1)}, f32[12,40,128]{2,1,0:T(8,128)}, u32[]{:S(2)}) copy-start(f32[12,40,128]{2,1,0:T(8,128)} %get-tuple-element.96.free) | copy-start | bytes 737284
  178.8 20.8 %copy-start.2 = (s32[8,40,128]{2,1,0:T(8,128)S(1)}, s32[8,40,128]{2,1,0:T(8,128)}, u32[]{:S(2)}) copy-start(s32[8,40,128]{2,1,0:T(8,128)} %passive.1) | copy-start | bytes 491524
  178.8 20.8 %copy-start.5 = (f32[10,40,128]{2,1,0:T(8,128)S(1)}, f32[10,40,128]{2,1,0:T(8,128)}, u32[]{:S(2)}) copy-start(f32[10,40,128]{2,1,0:T(8,128)} %get-tuple-element.99.scale) | copy-start | bytes 614404
  194.1 5.4 %collective-permute-start.16 = (f32[10,40,128]{2,1,0:T(8,128)S(1)}, f32[10,40,128]{2,1,0:T(8,128)S(1)}, u32[]{:S(2)}, u32[]{:S(2)}) collective-permute-start(f32[10,40,128]{2,1,0:T(8,128)S(1)} %get-tuple-element.98.mine), channel_id=1, source_target_pairs={{0,64},{64,0},{1,65},{65,1},{2,66},{66,2},{3,67},{67,3},{4,68},{68... | collective-permute-start | bytes 614408 | tf_op jit(solution)/shard_map/ppermute | solution.py:981
